TPU v7x, 32 devices: a whole 2x2x4 slice. The times are simulated.
32 devices in a mesh: gx: 8 (over z, y), gy: 4 (over x, core).
Axes of the slice: x: 2, y: 2, z: 4, core: 2. Of those that a mesh axis runs over, the one named last changes fastest.
Arguments:
- cell_state: float32 [17, 64, 64, 256], P(None, 'gx', 'gy')
- evap_rate: float32 [8], replicated, may hold values from 0.05 to 0.5
- parcels: float32 [8, 524288], P(None, ('gx', 'gy'))
- crossing: int32 [2, 32768], P(None, ('gx', 'gy')), may hold values from 0 to 16383, as said below
- conv_mass: float32 [8, 65536], P(None, ('gx', 'gy')), may hold values from 0.5 to 2
- conv_owner: int32 [65536, 1], P(('gx', 'gy')), may hold values from 0 to 31; in each aligned block of 2048 rows (0 to 2047, 2048 to 4095, ...) at most 128 rows name the same one
- conv_cell: int32 [65536], P(('gx', 'gy')), may hold values from 0 to 32767
Outputs:
- new_cells: float32 [14, 64, 64, 256], P(None, 'gx', 'gy')
- new_parcels: float32 [8, 524288], P(None, ('gx', 'gy'))
Inputs may be any that keep to these rules, and one draw needn't show every extreme that they name: On each device the 2048 entries of crossing are distinct local parcel slots. `conv_owner`: the rows of one device name one owner at most 128 times.
All inputs are finite; a program needn't handle non-finite values.
Results may differ from a plain program's by a relative error of at most 0.0003.
Values sent between devices are 32-bit elements; how exact they have to be, the bound alone decides.
No kernel may reach another device: no remote copies, remote signals or barrier semaphores. Data moves between devices by JAX's collectives and lax.ppermute only.
A program may use at most 64 MiB of HBM per device.

v0:
```python
import math

import jax
import jax.numpy as jnp
from jax import lax
from jax.sharding import PartitionSpec as P

SECTIONS = 8
SPECIES = 6


def padded_2(value, sides, width):
    for axis, dim in sides:
        size, length = (lax.axis_size(axis), value.shape[dim])
        up = [(i, (i + 1) % size) for i in range(size)]
        down = [(j, i) for i, j in up]
        last = lax.slice_in_dim(value, length - width, length, axis=dim)
        initial = lax.slice_in_dim(value, 0, width, axis=dim)
        before = lax.ppermute(last, axis, up)
        after = lax.ppermute(initial, axis, down)
        value = jnp.concatenate([before, value, after], axis=dim)
    return value


def advect_split(first_padded, second_padded, wall_normal):
    count = SECTIONS + SPECIES
    amount_first = first_padded[:count]
    courant_first = first_padded[count]
    face_x = 0.5 * (courant_first[:-1] + courant_first[1:])
    flux_x = (
        jnp.maximum(face_x, 0.0) * amount_first[:, :-1]
        + jnp.minimum(face_x, 0.0) * amount_first[:, 1:]
    )
    change_x = flux_x[:, 1:] - flux_x[:, :-1]
    amount_second = second_padded[:count]
    courant_second = second_padded[count]
    face_y = 0.5 * (courant_second[:, :-1] + courant_second[:, 1:])
    flux_y = (
        jnp.maximum(face_y, 0.0) * amount_second[:, :, :-1]
        + jnp.minimum(face_y, 0.0) * amount_second[:, :, 1:]
    )
    change_y = flux_y[:, :, 1:] - flux_y[:, :, :-1]
    center = amount_first[:, 1:-1]
    face_z = 0.5 * (wall_normal[:, :, :-1] + wall_normal[:, :, 1:])
    flux_z = (
        jnp.maximum(face_z, 0.0) * center[:, :, :, :-1]
        + jnp.minimum(face_z, 0.0) * center[:, :, :, 1:]
    )
    flux_z = jnp.pad(flux_z, ((0, 0), (0, 0), (0, 0), (1, 1)))
    change_z = flux_z[:, :, :, 1:] - flux_z[:, :, :, :-1]
    return center - change_x - change_y - change_z


def evaporate(moved, evap_rate):
    sections = moved[:SECTIONS]
    species = moved[SECTIONS:]
    vapour = species[0]
    loss = evap_rate[:, None, None, None] * sections / (1.0 + vapour)
    passed = jnp.concatenate([loss[1:], jnp.zeros_like(loss[:1])], axis=0)
    new_sections = sections - loss + 0.5 * passed
    new_fuel = vapour + loss[0] + 0.5 * jnp.sum(loss[1:], axis=0)
    new_species = jnp.concatenate([new_fuel[None], species[1:]], axis=0)
    return (new_sections, new_species)


def advance(parcels):
    position = parcels[0:3]
    velocity = parcels[3:6]
    diameter = parcels[6]
    warmth = parcels[7]
    factor = 0.8 / (1.0 + diameter * diameter)
    velocity_new = velocity * (1.0 - factor)
    position_new = position + 0.5 * (velocity + velocity_new)
    diameter_new = diameter * (1.0 - 0.05 * warmth)
    warmth_new = warmth + factor * (1.0 - warmth)
    return jnp.concatenate(
        [position_new, velocity_new, diameter_new[None], warmth_new[None]], axis=0
    )


def bucket_rows(values, owner, owner_total, capacity):
    width = values.shape[0]
    row_total = owner.shape[0]
    block = math.gcd(row_total, 512)
    blocks = row_total // block
    positions = jnp.arange(block, dtype=jnp.int32)
    lower = (positions[:, None] > positions[None, :]).astype(jnp.bfloat16)
    owner_ids = jnp.arange(owner_total, dtype=jnp.int32)
    slot_ids = jnp.arange(capacity, dtype=jnp.float32)
    value_blocks = values.reshape(width, blocks, block).transpose(1, 0, 2)
    owner_blocks = owner.reshape(blocks, block)

    def bucket_step(carry, item):
        counts, filled = carry
        value_block, owner_block = item
        onehot = (owner_block[:, None] == owner_ids[None, :]).astype(jnp.float32)
        before = jnp.dot(lower, onehot.astype(jnp.bfloat16), preferred_element_type=jnp.float32)
        rank = jnp.sum((before + counts[None, :]) * onehot, axis=1)
        slot_hot = (rank[:, None] == slot_ids[None, :]).astype(jnp.float32)
        spread = value_block[:, :, None] * onehot[None]
        placed = jnp.einsum("sro,rw->sow", spread, slot_hot, precision=lax.Precision.HIGHEST)
        return ((counts + jnp.sum(onehot, axis=0), filled + placed), None)

    start = (
        jnp.zeros((owner_total,), jnp.float32),
        jnp.zeros((width, owner_total, capacity), jnp.float32),
    )
    (counts, filled), unused = lax.scan(bucket_step, start, (value_blocks, owner_blocks))
    return filled


def deposit_rows(mass_flat, cell_flat, plane_cells, size_z):
    row_total = cell_flat.shape[0]
    block = math.gcd(row_total, 1024)
    blocks = row_total // block
    plane_ids = jnp.arange(plane_cells, dtype=jnp.int32)
    depth_ids = jnp.arange(size_z, dtype=jnp.int32)
    mass_blocks = mass_flat.reshape(SECTIONS, blocks, block).transpose(1, 0, 2)
    cell_blocks = cell_flat.reshape(blocks, block)

    def deposit_step(total, item):
        mass_block, cell_block = item
        plane_hot = (cell_block[:, None] // size_z == plane_ids[None, :]).astype(jnp.float32)
        depth_hot = (cell_block[:, None] % size_z == depth_ids[None, :]).astype(jnp.float32)
        spread = mass_block[:, :, None] * plane_hot[None]
        added = jnp.einsum("srh,rl->shl", spread, depth_hot, precision=lax.Precision.HIGHEST)
        return (total + added, None)

    total, unused = lax.scan(
        deposit_step,
        jnp.zeros((SECTIONS, plane_cells, size_z), jnp.float32),
        (mass_blocks, cell_blocks),
    )
    return total


def on_device(cell_state, evap_rate, parcels, crossing, conv_mass, conv_owner, conv_cell):
    count = SECTIONS + SPECIES
    wall_normal = cell_state[count + 2]
    padded = padded_2(cell_state, (("gx", 1), ("gy", 2)), 1)
    first_padded = padded[: count + 1, :, 1:-1]
    second_padded = jnp.concatenate(
        [padded[:count, 1:-1], padded[count + 1 : count + 2, 1:-1]], axis=0
    )
    moved = advect_split(first_padded, second_padded, wall_normal)
    new_sections, new_species = evaporate(moved, evap_rate)
    size_x = cell_state.shape[1]
    size_y = cell_state.shape[2]
    size_z = cell_state.shape[3]
    owner_total = lax.axis_size("gx") * lax.axis_size("gy")
    row_total = conv_owner.shape[0]
    capacity = 2 * row_total // owner_total
    carried = jnp.concatenate([conv_mass, conv_cell.astype(jnp.float32)[None]], axis=0)
    filled = bucket_rows(carried, conv_owner[:, 0], owner_total, capacity)
    mass_buffer = filled[:SECTIONS]
    cell_buffer = filled[SECTIONS:].astype(jnp.int32)
    mass_in, cell_in = (
        lax.all_to_all(mass_buffer, ("gx", "gy"), split_axis=1, concat_axis=1, tiled=True),
        lax.all_to_all(cell_buffer, ("gx", "gy"), split_axis=1, concat_axis=1, tiled=True),
    )
    mass_flat = mass_in.reshape(SECTIONS, -1)
    cell_flat = cell_in.reshape(-1)
    deposit = deposit_rows(mass_flat, cell_flat, size_x * size_y, size_z)
    deposit = deposit.reshape(SECTIONS, size_x, size_y, size_z)
    new_cells = jnp.concatenate([new_sections + deposit, new_species], axis=0)
    advanced = advance(parcels)
    attr_count = advanced.shape[0]
    slot_total = advanced.shape[1]
    upper_count = slot_total // 128
    cross_count = crossing.shape[1]
    slots = jnp.concatenate([crossing[1], crossing[0]], axis=0)
    upper_hot = (slots[:, None] // 128 == jnp.arange(upper_count, dtype=jnp.int32)[None, :]).astype(
        jnp.float32
    )
    lower_hot = (slots[:, None] % 128 == jnp.arange(128, dtype=jnp.int32)[None, :]).astype(
        jnp.float32
    )
    folded = advanced.reshape(attr_count, upper_count, 128)
    picked = jnp.einsum("ahl,kh->akl", folded, upper_hot, precision=lax.Precision.HIGHEST)
    gathered = jnp.sum(picked * lower_hot[None], axis=2)
    leaving = jnp.stack([gathered[:, :cross_count], gathered[:, cross_count:]], axis=1)
    arrived = padded_2(leaving, (("gx", 1),), 1)
    incoming = jnp.concatenate([arrived[:, 3], arrived[:, 0]], axis=1)
    spread = incoming[:, :, None] * lower_hot[None]
    placed = jnp.einsum("akl,kh->ahl", spread, upper_hot, precision=lax.Precision.HIGHEST)
    hit = jnp.einsum("kh,kl->hl", upper_hot, lower_hot, precision=lax.Precision.HIGHEST)
    new_parcels = (folded * (1.0 - hit)[None] + placed).reshape(attr_count, slot_total)
    return (new_cells, new_parcels)


def solution(mesh):
    in_specs = (
        P(None, "gx", "gy", None),
        P(),
        P(None, ("gx", "gy")),
        P(None, ("gx", "gy")),
        P(None, ("gx", "gy")),
        P(("gx", "gy"), None),
        P(("gx", "gy")),
    )
    out_specs = (P(None, "gx", "gy", None), P(None, ("gx", "gy")))
    return jax.shard_map(
        on_device, mesh=mesh, in_specs=in_specs, out_specs=out_specs, check_vma=False
    )
```

profile of v0, /device:TPU:0, one launch (start us, length us, event | category | flops | bytes accessed | tf_op | source)
XLA Modules:
  0.0 94.3 jit_solution(13302226179811873498)
XLA Ops:
  0.6 1.9 %fusion.75 = (f32[17,1,16,256]{3,2,1,0:T(8,128)}, f32[17,1,16,256]{3,2,1,0:T(8,128)}) fusion(f32[17,8,16,256]{3,2,1,0:T(8,128)} %param.11), kind=kLoop, calls=%fused_computation.140 | loop fusion | bytes 1114112 | tf_op jit(solution)/shard_map/slice | solution.py:18
  2.5 3.0 %collective-permute-start = (f32[17,1,16,256]{3,2,1,0:T(8,128)}, f32[17,1,16,256]{3,2,1,0:T(8,128)}, u32[]{:S(2)}, u32[]{:S(2)}) collective-permute-start(f32[17,1,16,256]{3,2,1,0:T(8,128)} %get-tuple-element.215), channel_id=1, source_target_pairs={{0,4},{4,8},{8,12},{12,16},{16,20},{20,24},{24,28},{28,0},{1,5},{5... | collective-permute-start | bytes 835592 | tf_op jit(solution)/shard_map/ppermute | solution.py:19
  5.5 3.0 %collective-permute-start.1 = (f32[17,1,16,256]{3,2,1,0:T(8,128)}, f32[17,1,16,256]{3,2,1,0:T(8,128)}, u32[]{:S(2)}, u32[]{:S(2)}) collective-permute-start(f32[17,1,16,256]{3,2,1,0:T(8,128)} %get-tuple-element.214), channel_id=1, source_target_pairs={{4,0},{8,4},{12,8},{16,12},{20,16},{24,20},{28,24},{0,28},{5,1},{9... | collective-permute-start | bytes 835592 | tf_op jit(solution)/shard_map/ppermute | solution.py:20
  9.1 1.3 %reduce.7 = s32[2048]{0:T(1024)S(1)} reduce(s32[2048,1]{0,1:T(1,128)} %param.16, s32[]{:T(128)} %broadcast.329), dimensions={1}, to_apply=%param.16.reduce_sub_computation.3 | reduce | bytes 16388 | tf_op args[5]
  12.0 4.2 %while.26 = (s32[]{:T(128)}, f32[32]{0:T(128)S(1)}, f32[9,32,128]{2,1,0:T(8,128)S(1)}, s32[4,512]{1,0:T(4,128)S(1)}, f32[4,9,512]{2,1,0:T(8,128)S(1)}, /*index=5*/s32[]{:T(128)}, s32[]{:T(128)}) while((s32[]{:T(128)}, f32[32]{0:T(128)S(1)}, f32[9,32,128]{2,1,0:T(8,128)S(1)}, s32[4,512]{1,0:T(4,128)S(1)}, ...), condition=%wide.region_3.4_spmd.clone, body=%wide.region_0.3_spmd.clone.sunk | while | flops 244276768 | bytes 496480 | solution.py:108
  16.8 3.3 %all-to-all-start.1 = ((s32[1,32,128]{2,0,1:T(1,128)}), s32[1,32,128]{2,0,1:T(1,128)S(1)}, u32[]{:S(2)}, u32[]{:S(2)}) async-start(s32[1,32,128]{2,0,1:T(1,128)} %bitcast.9), calls=%async_computation.1 | async-start | bytes 32768 | tf_op jit(solution)/shard_map/all_to_all | solution.py:159
  23.6 3.9 %multiply_reduce_fusion = f32[2048,8]{0,1:T(8,128)S(1)} fusion(f32[2048,128]{0,1:T(8,128)S(1)} %fusion.57, f32[128,1024]{0,1:T(8,128)S(1)} %bitcast.98, s32[2048]{0:T(1024)S(1)} %get-tuple-element.232), kind=kOutput, calls=%fused_computation.49 | convolution fusion | flops 3225665536 | bytes 1646592
  28.1 4.6 %collective-permute-start.4 = (f32[8,1,1024]{2,0,1:T(8,128)}, f32[8,1,1024]{2,0,1:T(8,128)}, u32[]{:S(2)}, u32[]{:S(2)}) collective-permute-start(f32[8,1,1024]{2,0,1:T(8,128)} %get-tuple-element.230), channel_id=1, source_target_pairs={{4,0},{8,4},{12,8},{16,12},{20,16},{24,20},{28,24},{0,28},{5,1},{9... | collective-permute-start | bytes 98312 | tf_op jit(solution)/shard_map/ppermute | solution.py:20
  32.8 1.8 %multiply_add_fusion = f32[14,8,16,255]{3,2,1,0:T(8,128)} fusion(f32[17,8,16,256]{3,2,1,0:T(8,128)S(1)} %copy-done, f32[8,16,255]{2,1,0:T(8,128)S(1)} %get-tuple-element.229, f32[8,16,255]{2,1,0:T(8,128)S(1)} %get-tuple-element.228), kind=kLoop, calls=%fused_computation.69 | loop fusion | flops 1370880 | bytes 5744640 | tf_op jit(solution)/shard_map/add | solution.py:46
  34.6 1.0 %convolution_subtract_fusion = f32[128,128]{1,0:T(8,128)} fusion(s32[2048]{0:T(1024)S(1)} %get-tuple-element.233, s32[2048]{0:T(1024)S(1)} %get-tuple-element.232), kind=kOutput, calls=%fused_computation.72 | convolution fusion | flops 67649536 | bytes 81920 | tf_op jit(solution)/shard_map/kh,kl->hl/dot_general | solution.py:186
  36.4 1.3 %copy.65 = f32[2048,128]{1,0:T(8,128)} copy(f32[2048,128]{0,1:T(8,128)S(1)} %fusion.57) | data formatting | bytes 2097152 | tf_op jit(solution)/shard_map/convert_element_type | solution.py:175
  37.7 1.6 %slice.205 = f32[8,32,128]{2,0,1:T(8,128)} slice(f32[9,32,128]{2,0,1:T(8,128)} %copy.55), slice={[0:8], [0:32], [0:128]} | slice | bytes 262144 | tf_op jit(solution)/shard_map/slice | solution.py:155
  40.2 6.2 %all-to-all-start = ((f32[8,32,128]{2,0,1:T(8,128)}), f32[8,32,128]{2,0,1:T(8,128)S(1)}, u32[]{:S(2)}, u32[]{:S(2)}) async-start(f32[8,32,128]{2,0,1:T(8,128)} %slice.205), calls=%async_computation | async-start | bytes 262144 | tf_op jit(solution)/shard_map/all_to_all | solution.py:158
  47.9 10.3 %fusion.54 = f32[8,128,128]{1,2,0:T(8,128)S(1)} fusion(f32[2048,128]{1,0:T(8,128)} %copy.65, f32[8,2048]{1,0:T(8,128)S(1)} %pad_maximum_fusion.6, s32[2048]{0:T(1024)} %copy-done.6, f32[128,128]{0,1:T(8,128)S(1)} %copy.63, f32[1,128,128]{1,2,0:T(8,128)} %copy.62, f32[1,128,128]{1,2,0:T(8,128)S(1)} %copy.61, f32[3,128,128]{1,2,0:T(8,128)} %copy.60, ...), kind=kOutput, calls=%fused_computation.71 | convolution fusion | flops 3224240128 | bytes 2236416 | tf_op jit(solution)/shard_map/akl,kh->ahl/dot_general | solution.py:185
  58.4 1.1 %copy.80 = f32[1,8,128,128]{3,1,2,0:T(8,128)} copy(f32[1,8,128,128]{3,2,1,0:T(8,128)S(1)} %bitcast.92) | data formatting | bytes 1048576
  59.6 17.7 %while.27 = (s32[]{:T(128)}, f32[8,128,256]{2,1,0:T(8,128)}, f32[4,8,1024]{2,0,1:T(4,128)S(1)}, s32[4,1024]{1,0:T(4,128)S(1)}, s32[]{:T(128)}, /*index=5*/s32[]{:T(128)}) while((s32[]{:T(128)}, f32[8,128,256]{2,1,0:T(8,128)}, f32[4,8,1024]{2,0,1:T(4,128)S(1)}, s32[4,1024]{1,0:T(4,128)S(1)}, s32[]{:T(128)}, ...), condition=%wide.region_5.6_spmd.clone, body=%wide.region_4.5_spmd.clone.sunk | while | flops 3223342080 | bytes 3338327 | solution.py:129
  60.0 3.3 %fusion.102 = f32[8,128,256]{2,1,0:T(8,128)} fusion(f32[1024,128]{0,1:T(8,128)S(1)} %fusion.101, f32[8,1024]{1,0:T(8,128)S(1)} %bitcast.95, f32[8,128,256]{2,1,0:T(8,128)} %get-tuple-element.330, s32[1024]{0:T(1024)S(1)} %get-tuple-element.301, pred[]{:T(512)S(6)} %compare.36), kind=kOutput, calls=%fused_computation.30.clone.1 | convolution fusion | flops 3223060480 | bytes 2658305 | tf_op jit(solution)/shard_map/while/body/eval_jaxpr/srh,rl->shl/dot_general | solution.py:126
  63.4 4.5 %fusion.102 = f32[8,128,256]{2,1,0:T(8,128)} fusion(f32[1024,128]{0,1:T(8,128)S(1)} %fusion.101, f32[8,1024]{1,0:T(8,128)S(1)} %bitcast.95, f32[8,128,256]{2,1,0:T(8,128)} %get-tuple-element.330, s32[1024]{0:T(1024)S(1)} %get-tuple-element.301, pred[]{:T(512)S(6)} %compare.36), kind=kOutput, calls=%fused_computation.30.clone.1 | convolution fusion | flops 3223060480 | bytes 2658305 | tf_op jit(solution)/shard_map/while/body/eval_jaxpr/srh,rl->shl/dot_general | solution.py:126
  68.1 4.5 %fusion.102 = f32[8,128,256]{2,1,0:T(8,128)} fusion(f32[1024,128]{0,1:T(8,128)S(1)} %fusion.101, f32[8,1024]{1,0:T(8,128)S(1)} %bitcast.95, f32[8,128,256]{2,1,0:T(8,128)} %get-tuple-element.330, s32[1024]{0:T(1024)S(1)} %get-tuple-element.301, pred[]{:T(512)S(6)} %compare.36), kind=kOutput, calls=%fused_computation.30.clone.1 | convolution fusion | flops 3223060480 | bytes 2658305 | tf_op jit(solution)/shard_map/while/body/eval_jaxpr/srh,rl->shl/dot_general | solution.py:126
  72.8 4.5 %fusion.102 = f32[8,128,256]{2,1,0:T(8,128)} fusion(f32[1024,128]{0,1:T(8,128)S(1)} %fusion.101, f32[8,1024]{1,0:T(8,128)S(1)} %bitcast.95, f32[8,128,256]{2,1,0:T(8,128)} %get-tuple-element.330, s32[1024]{0:T(1024)S(1)} %get-tuple-element.301, pred[]{:T(512)S(6)} %compare.36), kind=kOutput, calls=%fused_computation.30.clone.1 | convolution fusion | flops 3223060480 | bytes 2658305 | tf_op jit(solution)/shard_map/while/body/eval_jaxpr/srh,rl->shl/dot_general | solution.py:126
  80.7 1.7 %collective-permute-start.3 = (f32[17,10,1,256]{3,0,2,1:T(8,128)S(1)}, f32[17,10,1,256]{3,0,2,1:T(8,128)S(1)}, u32[]{:S(2)}, u32[]{:S(2)}) collective-permute-start(f32[17,10,1,256]{3,0,2,1:T(8,128)S(1)} %copy.47), channel_id=1, source_target_pairs={{1,0},{2,1},{3,2},{0,3},{5,4},{6,5},{7,6},{4,7},{9,8},{10,9},{11,1... | collective-permute-start | bytes 522248 | tf_op jit(solution)/shard_map/ppermute | solution.py:20
  83.0 3.8 %collective-permute-done.2 = f32[17,10,1,256]{3,0,2,1:T(8,128)S(1)} collective-permute-done((f32[17,10,1,256]{3,0,2,1:T(8,128)S(1)}, f32[17,10,1,256]{3,0,2,1:T(8,128)S(1)}, u32[]{:S(2)}, u32[]{:S(2)}) %collective-permute-start.2) | collective-permute-done | bytes 174112 | tf_op jit(solution)/shard_map/ppermute | solution.py:19
  89.9 1.3 %fusion.48 = f32[14,8,16,256]{3,2,1,0:T(8,128)S(1)} fusion(f32[14,8,16,255]{3,2,1,0:T(8,128)S(1)} %copy-done.1, f32[14,8,17,256]{3,2,1,0:T(8,128)S(1)} %fusion.44, f32[14,9,16,256]{3,2,1,0:T(8,128)S(1)} %fusion.46, f32[17,8,16,256]{3,2,1,0:T(8,128)S(1)} %copy-done), kind=kLoop, calls=%fused_computation.63 | loop fusion | flops 2752512 | bytes 12837888 | tf_op jit(solution)/shard_map/sub | solution.py:51
  92.9 1.4 %pad_maximum_fusion.2 = f32[14,8,16,256]{3,2,1,0:T(8,128)} fusion(f32[5,8,16,256]{3,2,1,0:T(8,128)S(1)} %slice.207, f32[1,8,16,256]{3,2,1,0:T(8,128)S(1)} %fusion.70, f32[8,8,16,256]{3,2,1,0:T(8,128)S(1)} %add_add_fusion), kind=kLoop, calls=%fused_computation.68 | loop fusion | flops 917504 | bytes 3670016 | tf_op jit(solution)/shard_map/concatenate | solution.py:165
  (128 shorter events, 23.3 us)
Async XLA Ops:
  2.5 74.8 %collective-permute-start = (f32[17,1,16,256]{3,2,1,0:T(8,128)}, f32[17,1,16,256]{3,2,1,0:T(8,128)}, u32[]{:S(2)}, u32[]{:S(2)}) collective-permute-start(f32[17,1,16,256]{3,2,1,0:T(8,128)} %get-tuple-element.215), channel_id=1, source_target_pairs={{0,4},{4,8},{8,12},{12,16},{16,20},{20,24},{24,28},{28,0},{1,5},{5... | collective-permute-start | bytes 835592 | tf_op jit(solution)/shard_map/ppermute | solution.py:19
  5.5 73.8 %collective-permute-start.1 = (f32[17,1,16,256]{3,2,1,0:T(8,128)}, f32[17,1,16,256]{3,2,1,0:T(8,128)}, u32[]{:S(2)}, u32[]{:S(2)}) collective-permute-start(f32[17,1,16,256]{3,2,1,0:T(8,128)} %get-tuple-element.214), channel_id=1, source_target_pairs={{4,0},{8,4},{12,8},{16,12},{20,16},{24,20},{28,24},{0,28},{5,1},{9... | collective-permute-start | bytes 835592 | tf_op jit(solution)/shard_map/ppermute | solution.py:20
  12.0 8.2 %copy-start.3 = (f32[8,16384]{1,0:T(8,128)S(1)}, f32[8,16384]{1,0:T(8,128)}, u32[]{:S(2)}) copy-start(f32[8,16384]{1,0:T(8,128)} %param.13) | copy-start | bytes 1572868
  16.1 0.7 copy-start.4
  16.1 6.3 %copy-start.7 = (s32[2,1024]{1,0:T(2,128)S(1)}, s32[2,1024]{1,0:T(2,128)}, u32[]{:S(2)}) copy-start(s32[2,1024]{1,0:T(2,128)} %param.14) | copy-start | bytes 24580
  16.8 23.4 %all-to-all-start.1 = ((s32[1,32,128]{2,0,1:T(1,128)}), s32[1,32,128]{2,0,1:T(1,128)S(1)}, u32[]{:S(2)}, u32[]{:S(2)}) async-start(s32[1,32,128]{2,0,1:T(1,128)} %bitcast.9), calls=%async_computation.1 | async-start | bytes 32768 | tf_op jit(solution)/shard_map/all_to_all | solution.py:159
  21.4 11.3 %copy-start = (f32[17,8,16,256]{3,2,1,0:T(8,128)S(1)}, f32[17,8,16,256]{3,2,1,0:T(8,128)}, u32[]{:S(2)}) copy-start(f32[17,8,16,256]{3,2,1,0:T(8,128)} %param.11) | copy-start | bytes 6684676
  22.4 12.1 %copy-start.6 = (s32[2048]{0:T(1024)}, s32[2048]{0:T(1024)S(1)}, u32[]{:S(2)}) copy-start(s32[2048]{0:T(1024)S(1)} %get-tuple-element.232) | copy-start | bytes 24580
  28.1 19.0 %collective-permute-start.4 = (f32[8,1,1024]{2,0,1:T(8,128)}, f32[8,1,1024]{2,0,1:T(8,128)}, u32[]{:S(2)}, u32[]{:S(2)}) collective-permute-start(f32[8,1,1024]{2,0,1:T(8,128)} %get-tuple-element.230), channel_id=1, source_target_pairs={{4,0},{8,4},{12,8},{16,12},{20,16},{24,20},{28,24},{0,28},{5,1},{9... | collective-permute-start | bytes 98312 | tf_op jit(solution)/shard_map/ppermute | solution.py:20
  32.6 14.4 %collective-permute-start.5 = (f32[8,1,1024]{2,0,1:T(8,128)}, f32[8,1,1024]{2,0,1:T(8,128)}, u32[]{:S(2)}, u32[]{:S(2)}) collective-permute-start(f32[8,1,1024]{2,0,1:T(8,128)} %get-tuple-element.231), channel_id=1, source_target_pairs={{0,4},{4,8},{8,12},{12,16},{16,20},{20,24},{24,28},{28,0},{1,5},{5... | collective-permute-start | bytes 98312 | tf_op jit(solution)/shard_map/ppermute | solution.py:19
  32.8 2.8 %copy-start.5 = (f32[9,32,128]{2,1,0:T(8,128)S(1)}, f32[9,32,128]{2,1,0:T(8,128)}, u32[]{:S(2)}) copy-start(f32[9,32,128]{2,1,0:T(8,128)} %copy-done.4) | copy-start | bytes 442372
  40.2 19.3 %all-to-all-start = ((f32[8,32,128]{2,0,1:T(8,128)}), f32[8,32,128]{2,0,1:T(8,128)S(1)}, u32[]{:S(2)}, u32[]{:S(2)}) async-start(f32[8,32,128]{2,0,1:T(8,128)} %slice.205), calls=%async_computation | async-start | bytes 262144 | tf_op jit(solution)/shard_map/all_to_all | solution.py:158
  80.5 6.3 %collective-permute-start.2 = (f32[17,10,1,256]{3,0,2,1:T(8,128)S(1)}, f32[17,10,1,256]{3,0,2,1:T(8,128)S(1)}, u32[]{:S(2)}, u32[]{:S(2)}) collective-permute-start(f32[17,10,1,256]{3,0,2,1:T(8,128)S(1)} %copy.46), channel_id=1, source_target_pairs={{0,1},{1,2},{2,3},{3,0},{4,5},{5,6},{6,7},{7,4},{8,9},{9,10},{10,1... | collective-permute-start | bytes 522248 | tf_op jit(solution)/shard_map/ppermute | solution.py:19
  80.7 7.3 %collective-permute-start.3 = (f32[17,10,1,256]{3,0,2,1:T(8,128)S(1)}, f32[17,10,1,256]{3,0,2,1:T(8,128)S(1)}, u32[]{:S(2)}, u32[]{:S(2)}) collective-permute-start(f32[17,10,1,256]{3,0,2,1:T(8,128)S(1)} %copy.47), channel_id=1, source_target_pairs={{1,0},{2,1},{3,2},{0,3},{5,4},{6,5},{7,6},{4,7},{9,8},{10,9},{11,1... | collective-permute-start | bytes 522248 | tf_op jit(solution)/shard_map/ppermute | solution.py:20
  88.4 1.5 %copy-start.1 = (f32[14,8,16,255]{3,2,1,0:T(8,128)S(1)}, f32[14,8,16,255]{3,2,1,0:T(8,128)}, u32[]{:S(2)}) copy-start(f32[14,8,16,255]{3,2,1,0:T(8,128)} %multiply_add_fusion) | copy-start | bytes 5483524
  89.9 1.3 %copy-start.8 = (f32[8]{0:T(128)S(1)}, f32[8]{0:T(128)}, u32[]{:S(2)}) copy-start(f32[8]{0:T(128)} %param.12) | copy-start | bytes 100
  91.2 1.2 %copy-start.2 = (f32[8,128,256]{2,1,0:T(8,128)S(1)}, f32[8,128,256]{2,1,0:T(8,128)}, u32[]{:S(2)}) copy-start(f32[8,128,256]{2,1,0:T(8,128)} %get-tuple-element.125) | copy-start | bytes 3145732
where the time goes:
time: 95.4 us; the launch traced here: 94.3 us
  matrix products  35.4 us (37%)
  starting transfers between devices  21.9 us (23%)
  local copies, waits for them, and re-layouts  16.8 us (18%)
  other arithmetic  13.8 us (14%)
  waiting for transfers between devices  4.81 us (5%)
  between operations  1.06 us (1%)
    dot_general x4, matrix products, deposit_step(): jnp.einsum('srh,rl->shl', spread, depth_hot, precision=lax.Precision.HIGH...  16.8 us
    dot_general x1, matrix products, on_device(): jnp.einsum('akl,kh->ahl', spread, upper_hot, precision=lax.Precision.HIGH...  10.3 us
    ppermute x3, starting transfers between devices, padded_2(): after = lax.ppermute(initial, axis, down)  9.32 us
    all_to_all x1, starting transfers between devices, on_device(): lax.all_to_all(mass_buffer, ('gx', 'gy'), split_axis=1, concat_axis=1, ti...  6.18 us
    unnamed x21, local copies, waits for them, and re-layouts  4.53 us
    unnamed x1, matrix products  3.89 us
    ppermute x3, waiting for transfers between devices, padded_2(): before = lax.ppermute(last, axis, up)  3.84 us
    all_to_all x1, starting transfers between devices, on_device(): lax.all_to_all(cell_buffer, ('gx', 'gy'), split_axis=1, concat_axis=1, ti...  3.31 us
  transfers between devices with their start and end apart: 8, of which 2 were waited for; matrix products, arithmetic and copies ran while one was open for 60% of the time, Pallas kernels for 0%

commit v1 on v0

v1 whole, which is shorter than its diff:
```python
import functools

import jax
import jax.numpy as jnp
from jax import lax
from jax.experimental import pallas as pl
from jax.experimental.pallas import tpu as pltpu
from jax.sharding import PartitionSpec as P

SECTIONS = 8
SPECIES = 6
COUNT = SECTIONS + SPECIES
LANES = 128
F32 = jnp.float32
BF16 = jnp.bfloat16
VMEM = pl.BlockSpec(memory_space=pltpu.VMEM)


def call(kernel, out_shape, operands, scratch=(), flops=0, moved_bytes=0, limit=24):
    return pl.pallas_call(
        kernel,
        out_shape=out_shape,
        in_specs=[VMEM] * len(operands),
        out_specs=jax.tree.map(lambda unused: VMEM, out_shape),
        scratch_shapes=list(scratch),
        compiler_params=pltpu.CompilerParams(vmem_limit_bytes=limit << 20),
        cost_estimate=pl.CostEstimate(flops=flops, bytes_accessed=moved_bytes, transcendentals=0),
    )(*operands)


def iota(shape, axis):
    return lax.broadcasted_iota(jnp.int32, shape, axis)


def lane_pick(values, index):
    return jnp.take_along_axis(values, index, axis=1, mode="promise_in_bounds")


def advance_block(block):
    diameter = block[6:7]
    warmth = block[7:8]
    velocity = block[3:6]
    factor = 0.8 / (1.0 + diameter * diameter)
    velocity_new = velocity * (1.0 - factor)
    position_new = block[0:3] + 0.5 * (velocity + velocity_new)
    diameter_new = diameter * (1.0 - 0.05 * warmth)
    warmth_new = warmth + factor * (1.0 - warmth)
    return jnp.concatenate([position_new, velocity_new, diameter_new, warmth_new], axis=0)


def advance_all(parcels_ref, advanced_ref):
    diameter = parcels_ref[6:7, :]
    warmth = parcels_ref[7:8, :]
    velocity = parcels_ref[3:6, :]
    factor = 0.8 / (1.0 + diameter * diameter)
    velocity_new = velocity * (1.0 - factor)
    advanced_ref[0:3, :] = parcels_ref[0:3, :] + 0.5 * (velocity + velocity_new)
    advanced_ref[3:6, :] = velocity_new
    advanced_ref[6:7, :] = diameter * (1.0 - 0.05 * warmth)
    advanced_ref[7:8, :] = warmth + factor * (1.0 - warmth)


def prepare_kernel(cells_ref, parcels_ref, crossing_ref, up_ref, down_ref, yup_ref, ydown_ref, advanced_ref):
    size_x, size_y, size_z = cells_ref.shape[1:]
    up_ref[: COUNT + 1] = cells_ref[: COUNT + 1, size_x - 1]
    down_ref[: COUNT + 1] = cells_ref[: COUNT + 1, 0]
    for c in range(COUNT + 1):
        source = c if c < COUNT else COUNT + 1
        yup_ref[c] = cells_ref[source, :, size_y - 1, :]
        ydown_ref[c] = cells_ref[source, :, 0, :]
    advance_all(parcels_ref, advanced_ref)
    slot_total = parcels_ref.shape[1]
    cross = crossing_ref.shape[1]
    halves_y, halves_z = size_y // 8, size_z // LANES
    for side, out_ref in ((0, up_ref), (1, down_ref)):
        for start in range(0, cross, 4 * LANES):
            blocks = range(start, min(start + 4 * LANES, cross), LANES)
            picks = []
            for first in blocks:
                slots = jnp.broadcast_to(crossing_ref[side : side + 1, first : first + LANES], (8, LANES))
                picks.append((slots // LANES, slots % LANES))

            def step(h, totals, picks=picks):
                block = advanced_ref[:, pl.ds(pl.multiple_of(h * LANES, LANES), LANES)]
                return tuple(
                    jnp.where(high == h, lane_pick(block, low), total)
                    for (high, low), total in zip(picks, totals)
                )

            totals = lax.fori_loop(
                0, slot_total // LANES, step, tuple(jnp.zeros((8, LANES), F32) for unused in picks), unroll=8
            )
            for first, total in zip(blocks, totals):
                at = first // LANES
                layer, rest = divmod(at, halves_y * halves_z)
                half_y, half_z = divmod(rest, halves_z)
                out_ref[
                    COUNT + 1 + layer, 8 * half_y : 8 * half_y + 8, LANES * half_z : LANES * (half_z + 1)
                ] = total


def prepare(cells, parcels, crossing):
    size_x, size_y, size_z = cells.shape[1:]
    layers = COUNT + 1 + 8 * crossing.shape[1] // (size_y * size_z)
    face = jax.ShapeDtypeStruct((layers, size_y, size_z), F32)
    side = jax.ShapeDtypeStruct((COUNT + 1, size_x, size_z), F32)
    advanced = jax.ShapeDtypeStruct(parcels.shape, F32)
    return call(
        prepare_kernel, (face, face, side, side, advanced), (cells, parcels, crossing),
        moved_bytes=6 << 20,
    )


def inverse_kernel(crossing_ref, high_ref, low_ref, hot_ref, value_ref):
    sides, cross = crossing_ref.shape
    uppers = high_ref.shape[0]
    for side in range(sides):
        for first in range(0, cross, LANES):
            row = side * cross + first
            slots = crossing_ref[side : side + 1, first : first + LANES]
            upper = jnp.broadcast_to(slots // LANES, (uppers, LANES))
            lower = jnp.broadcast_to(slots % LANES, (LANES, LANES))
            at = pl.ds(row, LANES)
            block = row // LANES + 1
            hit = upper == iota((uppers, LANES), 0)
            value_ref[:uppers, at] = jnp.where(hit, float(block), 0.0).astype(BF16)
            value_ref[uppers:, at] = jnp.where(hit, iota((uppers, LANES), 1).astype(F32), 0.0).astype(BF16)
            hot_ref[:, at] = jnp.where(lower == iota((LANES, LANES), 0), 1.0, 0.0).astype(BF16)
    found = lax.dot_general(
        value_ref[...], hot_ref[...], (((1,), (1,)), ((), ())), preferred_element_type=F32
    ).astype(jnp.int32)
    high_ref[...] = found[:uppers]
    low_ref[...] = found[uppers:]


def inverse_map(crossing, slot_total):
    uppers = slot_total // LANES
    rows = crossing.size
    table = jax.ShapeDtypeStruct((uppers, LANES), jnp.int32)
    return call(
        inverse_kernel, (table, table), (crossing,),
        scratch=(pltpu.VMEM((LANES, rows), BF16), pltpu.VMEM((2 * uppers, rows), BF16)),
        flops=4 * uppers * LANES * rows, moved_bytes=1 << 20,
    )


def arrive_kernel(advanced_ref, high_ref, low_ref, before_ref, after_ref, out_ref):
    slot_total = advanced_ref.shape[1]
    size_y, size_z = before_ref.shape[1:]
    halves_y, halves_z = size_y // 8, size_z // LANES
    blocks = []
    for ref in (before_ref, after_ref):
        for layer in range(COUNT + 1, ref.shape[0]):
            for half_y in range(halves_y):
                for half_z in range(halves_z):
                    blocks.append(
                        (ref, layer, slice(8 * half_y, 8 * half_y + 8), slice(LANES * half_z, LANES * (half_z + 1)))
                    )

    def step(h, unused):
        at = pl.ds(pl.multiple_of(h * LANES, LANES), LANES)
        high = jnp.broadcast_to(high_ref[pl.ds(h, 1), :], (8, LANES))
        low = jnp.broadcast_to(low_ref[pl.ds(h, 1), :], (8, LANES))
        total = advanced_ref[:, at]
        for number, (ref, layer, rows, lanes) in enumerate(blocks):
            total = jnp.where(high == number + 1, lane_pick(ref[layer, rows, lanes], low), total)
        out_ref[:, at] = total
        return unused

    lax.fori_loop(0, slot_total // LANES, step, 0, unroll=4)


def arrive(advanced, high, low, before, after):
    return call(
        arrive_kernel, jax.ShapeDtypeStruct(advanced.shape, F32), (advanced, high, low, before, after),
        moved_bytes=4 << 20,
    )


def bucket_kernel(owner_total, capacity, mass_ref, owner_ref, cell_ref, out_ref, hot_ref, value_ref):
    blocks = owner_ref.shape[0]
    rows_out = out_ref.shape[0] // 9
    strict = iota((LANES, 2 * LANES), 0) < iota((LANES, 2 * LANES), 1)
    strict = jnp.where(strict, 1.0, 0.0).astype(BF16)
    owners = owner_ref[...]
    hots = [
        jnp.where(jnp.broadcast_to(owners[b : b + 1], (owner_total, LANES)) == iota((owner_total, LANES), 0), 1.0, 0.0)
        for b in range(blocks)
    ]
    ranks = lax.dot_general(
        jnp.concatenate(hots, axis=0).astype(BF16), strict, (((1,), (0,)), ((), ())), preferred_element_type=F32
    )
    carry = jnp.zeros((owner_total, LANES), F32)
    for b in range(blocks):
        part = ranks[b * owner_total : (b + 1) * owner_total]
        rank = jnp.sum(hots[b] * (part[:, :LANES] + carry), axis=0, keepdims=True).astype(jnp.int32)
        carry = carry + part[:, LANES:]
        spot = owners[b : b + 1] * capacity + rank
        upper = jnp.broadcast_to(spot // LANES, (rows_out, LANES))
        lower = jnp.broadcast_to(spot % LANES, (LANES, LANES))
        at = slice(b * LANES, (b + 1) * LANES)
        hit = upper == iota((rows_out, LANES), 0)
        value_ref[:rows_out, at] = jnp.where(hit, float(b + 1), 0.0).astype(BF16)
        value_ref[rows_out:, at] = jnp.where(hit, iota((rows_out, LANES), 1).astype(F32), 0.0).astype(BF16)
        hot_ref[:, at] = jnp.where(lower == iota((LANES, LANES), 0), 1.0, 0.0).astype(BF16)
    found = lax.dot_general(
        value_ref[...], hot_ref[...], (((1,), (1,)), ((), ())), preferred_element_type=F32
    ).astype(jnp.int32)
    cells = cell_ref[...].astype(F32)
    for group in range(0, rows_out, 8):
        high = found[group : group + 8]
        low = found[rows_out + group : rows_out + group + 8]
        total = jnp.zeros((8, LANES), F32)
        for b in range(blocks):
            total = jnp.where(high == b + 1, lane_pick(jnp.broadcast_to(cells[b : b + 1], (8, LANES)), low), total)
        for i in range(8):
            row = group + i
            row_high = jnp.broadcast_to(high[i : i + 1], (8, LANES))
            row_low = jnp.broadcast_to(low[i : i + 1], (8, LANES))
            mass = jnp.zeros((8, LANES), F32)
            for b in range(blocks):
                mass = jnp.where(row_high == b + 1, lane_pick(mass_ref[:, b * LANES : (b + 1) * LANES], row_low), mass)
            out_ref[9 * row : 9 * row + 8, :] = mass
            out_ref[9 * row + 8 : 9 * row + 9, :] = total[i : i + 1]


def bucket(mass, owner, cell, owner_total, capacity):
    rows = mass.shape[1]
    rows_out = owner_total * capacity // LANES
    return call(
        functools.partial(bucket_kernel, owner_total, capacity),
        jax.ShapeDtypeStruct((9 * rows_out, LANES), F32),
        (mass, owner.reshape(-1, LANES), cell.reshape(-1, LANES)),
        scratch=(pltpu.VMEM((LANES, rows), BF16), pltpu.VMEM((2 * rows_out, rows), BF16)),
        moved_bytes=1 << 20,
    )


def shift_up(value, axis):
    return pltpu.roll(value, value.shape[axis] - 1, axis)


def shift_down(value, axis):
    return pltpu.roll(value, 1, axis)


def slab_update(left, center, right, side_low, side_high, rate_ref, write):
    course = center(COUNT)
    size_y, size_z = course.shape
    first_row = iota((size_y, size_z), 0) == 0
    last_row = iota((size_y, size_z), 0) == size_y - 1

    def row_up(value, edge):
        return jnp.where(last_row, edge, shift_up(value, 0))

    def row_down(value, edge):
        return jnp.where(first_row, edge, shift_down(value, 0))

    face_x = 0.5 * (course + right(COUNT))
    face_x_low = 0.5 * (left(COUNT) + course)
    course_y = center(COUNT + 1)
    face_y = 0.5 * (course_y + row_up(course_y, side_high(COUNT)))
    face_y_low = 0.5 * (row_down(course_y, side_low(COUNT)) + course_y)
    course_z = center(COUNT + 2)
    lane = iota((size_y, size_z), 1)
    face_z = jnp.where(lane == size_z - 1, 0.0, 0.5 * (course_z + shift_up(course_z, 1)))
    face_z_low = jnp.where(lane == 0, 0.0, 0.5 * (shift_down(course_z, 1) + course_z))
    from_x_up, from_x_low = jnp.minimum(face_x, 0.0), jnp.maximum(face_x_low, 0.0)
    from_y_up, from_y_low = jnp.minimum(face_y, 0.0), jnp.maximum(face_y_low, 0.0)
    from_z_up, from_z_low = jnp.minimum(face_z, 0.0), jnp.maximum(face_z_low, 0.0)
    own = 1.0 - (
        (jnp.maximum(face_x, 0.0) - jnp.minimum(face_x_low, 0.0))
        + (jnp.maximum(face_y, 0.0) - jnp.minimum(face_y_low, 0.0))
        + (jnp.maximum(face_z, 0.0) - jnp.minimum(face_z_low, 0.0))
    )

    def moved(c):
        amount = center(c)
        total = own * amount
        total = total - from_x_up * right(c) + from_x_low * left(c)
        total = total - from_y_up * row_up(amount, side_high(c)) + from_y_low * row_down(amount, side_low(c))
        return total - from_z_up * shift_up(amount, 1) + from_z_low * shift_down(amount, 1)

    vapour = moved(SECTIONS)
    beside = 1.0 + vapour
    later = None
    gained = None
    for s in reversed(range(SECTIONS)):
        section = moved(s)
        loss = rate_ref[s] * section / beside
        value = section - loss
        if later is not None:
            value = value + 0.5 * later
            gained = later if gained is None else gained + later
        write(s, value)
        later = loss
    write(SECTIONS, vapour + later + 0.5 * gained)
    for c in range(SECTIONS + 1, COUNT):
        write(c, moved(c))


def inner_kernel(cells_ref, low_ref, high_ref, rate_ref, out_ref):
    size_x = cells_ref.shape[1]

    def layer(x, unused):
        def write(c, value):
            out_ref[c, x] = value

        slab_update(
            lambda c: cells_ref[c, x - 1],
            lambda c: cells_ref[c, x],
            lambda c: cells_ref[c, x + 1],
            lambda c: low_ref[c, pl.ds(x, 1), :],
            lambda c: high_ref[c, pl.ds(x, 1), :],
            rate_ref,
            write,
        )
        return unused

    lax.fori_loop(1, size_x - 1, layer, 0)


SMEM = pl.BlockSpec(memory_space=pltpu.SMEM)


def inner(cells, low, high, rate):
    return pl.pallas_call(
        inner_kernel,
        out_shape=jax.ShapeDtypeStruct((COUNT,) + cells.shape[1:], F32),
        in_specs=[VMEM, VMEM, VMEM, SMEM],
        out_specs=VMEM,
        compiler_params=pltpu.CompilerParams(vmem_limit_bytes=24 << 20),
        cost_estimate=pl.CostEstimate(flops=20 << 20, bytes_accessed=4 << 20, transcendentals=0),
    )(cells, low, high, rate)


def final_kernel(cells_ref, inner_ref, before_ref, after_ref, low_ref, high_ref, routed_ref, rate_ref, out_ref, depth_ref, spread_ref):
    size_x, size_y, size_z = cells_ref.shape[1:]
    groups = routed_ref.shape[0] // 9
    cell_rows = jnp.concatenate([routed_ref[9 * g + 8 : 9 * g + 9, :] for g in range(groups)], axis=0).astype(jnp.int32)
    depth = (cell_rows % size_z).T
    for g in range(groups):
        column = jnp.broadcast_to(depth[:, g : g + 1], (LANES, size_z))
        depth_ref[g * LANES : (g + 1) * LANES, :] = jnp.where(
            column == iota((LANES, size_z), 1), 1.0, 0.0
        ).astype(BF16)

    edge = {
        0: lambda: slab_update(
            lambda c: before_ref[c],
            lambda c: cells_ref[c, 0],
            lambda c: cells_ref[c, 1],
            lambda c: low_ref[c, 0:1, :],
            lambda c: high_ref[c, 0:1, :],
            rate_ref,
            functools.partial(put, out_ref, 0),
        ),
        size_x - 1: lambda: slab_update(
            lambda c: cells_ref[c, size_x - 2],
            lambda c: cells_ref[c, size_x - 1],
            lambda c: after_ref[c],
            lambda c: low_ref[c, size_x - 1 : size_x, :],
            lambda c: high_ref[c, size_x - 1 : size_x, :],
            rate_ref,
            functools.partial(put, out_ref, size_x - 1),
        ),
    }
    half = SECTIONS * size_y
    for x in range(size_x):
        for g in range(groups):
            at = slice(g * LANES, (g + 1) * LANES)
            plane = jnp.broadcast_to(cell_rows[g : g + 1] // size_z, (size_y, LANES))
            hit = plane == x * size_y + iota((size_y, LANES), 0)
            for s in range(SECTIONS):
                mass = routed_ref[9 * g + s : 9 * g + s + 1, :]
                coarse = mass.astype(BF16)
                fine = (mass - coarse.astype(F32)).astype(BF16)
                spread_ref[s * size_y : (s + 1) * size_y, at] = jnp.where(
                    hit, jnp.broadcast_to(coarse.astype(F32), hit.shape), 0.0
                ).astype(BF16)
                spread_ref[half + s * size_y : half + (s + 1) * size_y, at] = jnp.where(
                    hit, jnp.broadcast_to(fine.astype(F32), hit.shape), 0.0
                ).astype(BF16)
        added = jnp.dot(spread_ref[...], depth_ref[...], preferred_element_type=F32)
        if x in edge:
            edge[x]()
            base = out_ref
        else:
            base = inner_ref
            out_ref[SECTIONS:, x] = inner_ref[SECTIONS:, x]
        for s in range(SECTIONS):
            low, high = s * size_y, (s + 1) * size_y
            out_ref[s, x] = base[s, x] + (added[low:high] + added[half + low : half + high])


def put(ref, x, c, value):
    ref[c, x] = value


def final(cells, inner_cells, before, after, low, high, routed, rate):
    size_x, size_y, size_z = cells.shape[1:]
    rows = routed.shape[0] // 9 * LANES
    return pl.pallas_call(
        final_kernel,
        out_shape=jax.ShapeDtypeStruct(inner_cells.shape, F32),
        in_specs=[VMEM] * 7 + [SMEM],
        out_specs=VMEM,
        scratch_shapes=[pltpu.VMEM((rows, size_z), BF16), pltpu.VMEM((2 * SECTIONS * size_y, rows), BF16)],
        compiler_params=pltpu.CompilerParams(vmem_limit_bytes=32 << 20),
        cost_estimate=pl.CostEstimate(flops=4 << 30, bytes_accessed=6 << 20, transcendentals=0),
    )(cells, inner_cells, before, after, low, high, routed, rate)


def ring(size):
    up = [(i, (i + 1) % size) for i in range(size)]
    return up, [(j, i) for i, j in up]


def on_device(cell_state, evap_rate, parcels, crossing, conv_mass, conv_owner, conv_cell):
    owner_total = lax.axis_size("gx") * lax.axis_size("gy")
    row_total = conv_owner.shape[0]
    capacity = 2 * row_total // owner_total
    up_x, down_x = ring(lax.axis_size("gx"))
    up_y, down_y = ring(lax.axis_size("gy"))

    send_up, send_down, side_up, side_down, advanced = prepare(cell_state, parcels, crossing)
    before = lax.ppermute(send_up, "gx", up_x)
    after = lax.ppermute(send_down, "gx", down_x)
    low = lax.ppermute(side_up, "gy", up_y)
    high = lax.ppermute(side_down, "gy", down_y)

    filled = bucket(conv_mass, conv_owner, conv_cell, owner_total, capacity)
    fold = LANES // capacity
    filled = filled.reshape(-1, 9, fold, capacity).transpose(0, 2, 1, 3).reshape(owner_total, 1, 9 * capacity)
    routed = lax.all_to_all(filled, ("gx", "gy"), split_axis=0, concat_axis=0, tiled=True)
    routed = routed.reshape(-1, fold, 9, capacity).transpose(0, 2, 1, 3).reshape(-1, LANES)

    high_map, low_map = inverse_map(crossing, parcels.shape[1])
    inner_cells = inner(cell_state, low, high, evap_rate)
    new_parcels = arrive(advanced, high_map, low_map, before, after)
    new_cells = final(cell_state, inner_cells, before, after, low, high, routed, evap_rate)
    return (new_cells, new_parcels)


def solution(mesh):
    in_specs = (
        P(None, "gx", "gy", None),
        P(),
        P(None, ("gx", "gy")),
        P(None, ("gx", "gy")),
        P(None, ("gx", "gy")),
        P(("gx", "gy"), None),
        P(("gx", "gy")),
    )
    out_specs = (P(None, "gx", "gy", None), P(None, ("gx", "gy")))
    return jax.shard_map(
        on_device, mesh=mesh, in_specs=in_specs, out_specs=out_specs, check_vma=False
    )
```

time: 95.4 us -> 58.8 us (0.62)
  matrix products: 35.4 us -> 0 us
  Pallas kernels: 0 us -> 29.7 us
  other arithmetic: 13.8 us -> 0 us
  local copies, waits for them, and re-layouts: 16.8 us -> 8.32 us
  starting transfers between devices: 21.9 us -> 13.8 us
    dot_general x14 -> x0, matrix products: 31.5 us -> none  [the longest x4 16.8 us: deposit_step(): jnp.einsum('srh,rl->shl', spread, depth_hot, precision=lax.Precision.HIGH...]
    pallas_call x0 -> x6, Pallas kernels: none -> 29.7 us  [the longest x4 18.8 us: call(): pl.pallas_call(kernel, out_shape=out_shape, in_specs=[VMEM] * len(operand...]
    ppermute x6 -> x4, starting transfers between devices: 12.4 us -> 6.52 us  [the longest x1 2.95 us: on_device(): after = lax.ppermute(send_down, 'gx', down_x)]
    unnamed x1 -> x0, matrix products: 3.89 us -> none
    slice x8 -> x0, local copies, waits for them, and re-layouts: 3.83 us -> none  [the longest x2 1.9 us: padded_2(): initial = lax.slice_in_dim(value, 0, width, axis=dim)]
    unnamed x21 -> x20, local copies, waits for them, and re-layouts: 4.53 us -> 8.32 us
    concatenate x7 -> x0, local copies, waits for them, and re-layouts: 3.7 us -> none  [the longest x2 1.91 us: padded_2(): value = jnp.concatenate([before, value, after], axis=dim)]
    add x9 -> x0, other arithmetic: 3.37 us -> none  [the longest x1 1.78 us: advect_split(): jnp.maximum(face_z, 0.0) * center[:, :, :, :-1]]
  transfers between devices with their start and end apart: 8 -> 5, of which waited for: 2 -> 4; matrix products, arithmetic and copies ran while one was open for 60% -> 0% of each run, Pallas kernels for 0% -> 32%
where the time goes in v1:
time: 58.8 us; the launch traced here: 58.3 us
  Pallas kernels  29.7 us (51%)
  starting transfers between devices  13.8 us (23%)
  local copies, waits for them, and re-layouts  8.32 us (14%)
  waiting for transfers between devices  5.73 us (10%)
  between operations  0.69 us (1%)
    pallas_call x4, Pallas kernels, call(): pl.pallas_call(kernel, out_shape=out_shape, in_specs=[VMEM] * len(operand...  18.8 us
    pallas_call x1, Pallas kernels, final(): pl.pallas_call(final_kernel, out_shape=jax.ShapeDtypeStruct(inner_cells.s...  8.99 us
    unnamed x20, local copies, waits for them, and re-layouts  8.32 us
    all_to_all x1, starting transfers between devices, on_device(): lax.all_to_all(filled, ('gx', 'gy'), split_axis=0, concat_axis=0, tiled=T...  7.3 us
    ppermute x1, starting transfers between devices, on_device(): after = lax.ppermute(send_down, 'gx', down_x)  2.95 us
    ppermute x1, waiting for transfers between devices, on_device(): after = lax.ppermute(send_down, 'gx', down_x)  2.2 us
    pallas_call x1, Pallas kernels, inner(): pl.pallas_call(inner_kernel, out_shape=jax.ShapeDtypeStruct((COUNT,) + ce...  1.95 us
    ppermute x1, starting transfers between devices, on_device(): before = lax.ppermute(send_up, 'gx', up_x)  1.82 us
  transfers between devices with their start and end apart: 5, of which 4 were waited for; matrix products, arithmetic and copies ran while one was open for 0% of the time, Pallas kernels for 32%

profile of v1, /device:TPU:0, one launch (start us, length us, event | category | flops | bytes accessed | tf_op | source)
XLA Modules:
  0.0 58.3 jit_solution(5506009316922286644)
XLA Ops:
  0.6 0.8 %copy-done.5 = f32[8,2048]{1,0:T(8,128)S(1)} copy-done((f32[8,2048]{1,0:T(8,128)S(1)}, f32[8,2048]{1,0:T(8,128)}, u32[]{:S(2)}) %copy-start.5) | copy-done | bytes 65560
  1.5 0.7 %copy-done.7 = s32[2048,1]{0,1:T(1,128)S(1)} copy-done((s32[2048,1]{0,1:T(1,128)S(1)}, s32[2048,1]{0,1:T(1,128)}, u32[]{:S(2)}) %copy-start.7) | copy-done | bytes 8216
  2.2 0.7 %copy-done.8 = s32[2048]{0:T(1024)S(1)} copy-done((s32[2048]{0:T(1024)S(1)}, s32[2048]{0:T(1024)}, u32[]{:S(2)}) %copy-start.8) | copy-done | bytes 8216
  2.9 2.2 %shard_map.88 = f32[288,128]{1,0:T(8,128)} custom-call(f32[8,2048]{1,0:T(8,128)S(1)} %copy-done.5, s32[16,128]{1,0:T(8,128)S(1)} %bitcast.5, s32[16,128]{1,0:T(8,128)S(1)} %bitcast.6), custom_call_target="tpu_custom_call" | custom-call | bytes 1048576 | tf_op jit(solution)/shard_map/pallas_call | solution.py:20
  5.1 7.3 %all-to-all-start = ((f32[32,1,1152]{2,1,0:T(1,128)}), f32[32,1,1152]{2,1,0:T(1,128)S(1)}, u32[]{:S(2)}, u32[]{:S(2)}) async-start(f32[32,1,1152]{2,1,0:T(1,128)} %bitcast.2), calls=%async_computation | async-start | bytes 294912 | tf_op jit(solution)/shard_map/all_to_all | solution.py:435
  12.4 0.0 copy-start
  12.4 1.6 %copy-done = f32[17,8,16,256]{3,2,1,0:T(8,128)S(1)} copy-done((f32[17,8,16,256]{3,2,1,0:T(8,128)S(1)}, f32[17,8,16,256]{3,2,1,0:T(8,128)}, u32[]{:S(2)}) %copy-start) | copy-done | bytes 2228248
  14.0 1.0 %copy-done.4 = f32[8,16384]{1,0:T(8,128)S(1)} copy-done((f32[8,16384]{1,0:T(8,128)S(1)}, f32[8,16384]{1,0:T(8,128)}, u32[]{:S(2)}) %copy-start.4) | copy-done | bytes 524312
  15.0 0.7 %copy-done.6 = s32[2,1024]{1,0:T(2,128)S(1)} copy-done((s32[2,1024]{1,0:T(2,128)S(1)}, s32[2,1024]{1,0:T(2,128)}, u32[]{:S(2)}) %copy-start.6) | copy-done | bytes 8216
  15.7 10.1 %shard_map.86 = (f32[17,16,256]{2,1,0:T(8,128)S(1)}, f32[17,16,256]{2,1,0:T(8,128)S(1)}, f32[15,8,256]{2,1,0:T(8,128)S(1)}, f32[15,8,256]{2,1,0:T(8,128)S(1)}, f32[8,16384]{1,0:T(8,128)S(1)}) custom-call(f32[17,8,16,256]{3,2,1,0:T(8,128)S(1)} %copy-done, f32[8,16384]{1,0:T(8,128)S(1)} %copy-done.4, s32[2,1024]{1,0:T(2,128)S(1)} %copy-done.6), custom_call_target="tpu_custom_call" | custom-call | bytes 6291456 | tf_op jit(solution)/shard_map/pallas_call | solution.py:20
  25.8 1.8 %collective-permute-start.2 = (f32[17,16,256]{2,1,0:T(8,128)S(1)}, f32[17,16,256]{2,1,0:T(8,128)S(1)}, u32[]{:S(2)}, u32[]{:S(2)}) collective-permute-start(f32[17,16,256]{2,1,0:T(8,128)S(1)} %get-tuple-element.11), channel_id=1, source_target_pairs={{0,4},{4,8},{8,12},{12,16},{16,20},{20,24},{24,28},{28,0},{1,5},{5... | collective-permute-start | bytes 835592 | tf_op jit(solution)/shard_map/ppermute | solution.py:427
  27.6 3.0 %collective-permute-start.3 = (f32[17,16,256]{2,1,0:T(8,128)S(1)}, f32[17,16,256]{2,1,0:T(8,128)S(1)}, u32[]{:S(2)}, u32[]{:S(2)}) collective-permute-start(f32[17,16,256]{2,1,0:T(8,128)S(1)} %get-tuple-element.12), channel_id=1, source_target_pairs={{4,0},{8,4},{12,8},{16,12},{20,16},{24,20},{28,24},{0,28},{5,1},{9... | collective-permute-start | bytes 835592 | tf_op jit(solution)/shard_map/ppermute | solution.py:428
  30.6 1.7 %collective-permute-start.1 = (f32[15,8,256]{2,1,0:T(8,128)S(1)}, f32[15,8,256]{2,1,0:T(8,128)S(1)}, u32[]{:S(2)}, u32[]{:S(2)}) collective-permute-start(f32[15,8,256]{2,1,0:T(8,128)S(1)} %get-tuple-element.10), channel_id=1, source_target_pairs={{1,0},{2,1},{3,2},{0,3},{5,4},{6,5},{7,6},{4,7},{9,8},{10,9},{11,1... | collective-permute-start | bytes 368648 | tf_op jit(solution)/shard_map/ppermute | solution.py:430
  32.3 0.8 %shard_map.90 = (s32[128,128]{1,0:T(8,128)S(1)}, s32[128,128]{1,0:T(8,128)S(1)}) custom-call(s32[2,1024]{1,0:T(2,128)S(1)} %copy-done.6), custom_call_target="tpu_custom_call" | custom-call | flops 134217728 | bytes 1048576 | tf_op jit(solution)/shard_map/pallas_call | solution.py:20
  33.1 1.8 %collective-permute-done.low_ref = f32[15,8,256]{2,1,0:T(8,128)S(1)} collective-permute-done((f32[15,8,256]{2,1,0:T(8,128)S(1)}, f32[15,8,256]{2,1,0:T(8,128)S(1)}, u32[]{:S(2)}, u32[]{:S(2)}) %collective-permute-start) | collective-permute-done | bytes 122912 | tf_op jit(solution)/shard_map/ppermute | solution.py:429
  34.9 0.6 %collective-permute-done.1.high_ref = f32[15,8,256]{2,1,0:T(8,128)S(1)} collective-permute-done((f32[15,8,256]{2,1,0:T(8,128)S(1)}, f32[15,8,256]{2,1,0:T(8,128)S(1)}, u32[]{:S(2)}, u32[]{:S(2)}) %collective-permute-start.1) | collective-permute-done | bytes 122912 | tf_op jit(solution)/shard_map/ppermute | solution.py:430
  35.5 1.9 %shard_map.87.inner_ref = f32[14,8,16,256]{3,2,1,0:T(8,128)S(1)} custom-call(f32[17,8,16,256]{3,2,1,0:T(8,128)S(1)} %copy-done.1, f32[15,8,256]{2,1,0:T(8,128)S(1)} %collective-permute-done.low_ref, f32[15,8,256]{2,1,0:T(8,128)S(1)} %collective-permute-done.1.high_ref, f32[8]{0:T(128)S(1)} %copy-done.9), custom_call_target="tpu_custom_call" | custom-call | flops 20971520 | bytes 4194304 | tf_op jit(solution)/shard_map/pallas_call | solution.py:327
  37.5 0.0 copy-start.2
  37.5 1.2 %copy-done.2 = f32[14,8,16,256]{3,2,1,0:T(8,128)} copy-done((f32[14,8,16,256]{3,2,1,0:T(8,128)}, f32[14,8,16,256]{3,2,1,0:T(8,128)S(1)}, u32[]{:S(2)}) %copy-start.2) | copy-done | bytes 1835032
  38.7 1.1 %collective-permute-done.2.before_ref = f32[17,16,256]{2,1,0:T(8,128)S(1)} collective-permute-done((f32[17,16,256]{2,1,0:T(8,128)S(1)}, f32[17,16,256]{2,1,0:T(8,128)S(1)}, u32[]{:S(2)}, u32[]{:S(2)}) %collective-permute-start.2) | collective-permute-done | bytes 278560 | tf_op jit(solution)/shard_map/ppermute | solution.py:427
  39.8 2.2 %collective-permute-done.3.after_ref = f32[17,16,256]{2,1,0:T(8,128)S(1)} collective-permute-done((f32[17,16,256]{2,1,0:T(8,128)S(1)}, f32[17,16,256]{2,1,0:T(8,128)S(1)}, u32[]{:S(2)}, u32[]{:S(2)}) %collective-permute-start.3) | collective-permute-done | bytes 278560 | tf_op jit(solution)/shard_map/ppermute | solution.py:428
  42.0 5.8 %shard_map.91 = f32[8,16384]{1,0:T(8,128)} custom-call(f32[8,16384]{1,0:T(8,128)S(1)} %get-tuple-element.13.advanced_ref, s32[128,128]{1,0:T(8,128)S(1)} %get-tuple-element.14.high_ref, s32[128,128]{1,0:T(8,128)S(1)} %get-tuple-element.15.low_ref, f32[17,16,256]{2,1,0:T(8,128)S(1)} %collective-permute-done.2.before_ref, ...), custom_call_target="tpu_custom_call" | custom-call | bytes 4194304 | tf_op jit(solution)/shard_map/pallas_call | solution.py:20
  47.8 1.5 %copy-done.3 = f32[14,8,16,256]{3,2,1,0:T(8,128)S(1)} copy-done((f32[14,8,16,256]{3,2,1,0:T(8,128)S(1)}, f32[14,8,16,256]{3,2,1,0:T(8,128)}, u32[]{:S(2)}) %copy-start.3) | copy-done | bytes 1835032
  49.3 9.0 %shard_map.89 = f32[14,8,16,256]{3,2,1,0:T(8,128)} custom-call(f32[17,8,16,256]{3,2,1,0:T(8,128)S(1)} %copy-done.1, f32[14,8,16,256]{3,2,1,0:T(8,128)S(1)} %copy-done.3, f32[17,16,256]{2,1,0:T(8,128)S(1)} %collective-permute-done.2.before_ref, f32[17,16,256]{2,1,0:T(8,128)S(1)} %collective-permute-done.3.after_ref, ...), custom_call_target="tpu_custom_call" | custom-call | flops 4294967296 | bytes 6291456 | tf_op jit(solution)/shard_map/pallas_call | solution.py:403
  (12 shorter events, 0.0 us)
Async XLA Ops:
  0.6 0.8 %copy-start.5 = (f32[8,2048]{1,0:T(8,128)S(1)}, f32[8,2048]{1,0:T(8,128)}, u32[]{:S(2)}) copy-start(f32[8,2048]{1,0:T(8,128)} %mass_ref.1) | copy-start | bytes 196612
  1.5 0.7 %copy-start.7 = (s32[2048,1]{0,1:T(1,128)S(1)}, s32[2048,1]{0,1:T(1,128)}, u32[]{:S(2)}) copy-start(s32[2048,1]{0,1:T(1,128)} %param.12) | copy-start | bytes 24580
  2.2 0.7 %copy-start.8 = (s32[2048]{0:T(1024)S(1)}, s32[2048]{0:T(1024)}, u32[]{:S(2)}) copy-start(s32[2048]{0:T(1024)} %param.13) | copy-start | bytes 24580
  5.1 30.4 %copy-start.9 = (f32[8]{0:T(128)S(1)}, f32[8]{0:T(128)}, u32[]{:S(2)}) copy-start(f32[8]{0:T(128)} %rate_ref.3) | copy-start | bytes 100
  5.1 42.7 %all-to-all-start = ((f32[32,1,1152]{2,1,0:T(1,128)}), f32[32,1,1152]{2,1,0:T(1,128)S(1)}, u32[]{:S(2)}, u32[]{:S(2)}) async-start(f32[32,1,1152]{2,1,0:T(1,128)} %bitcast.2), calls=%async_computation | async-start | bytes 294912 | tf_op jit(solution)/shard_map/all_to_all | solution.py:435
  12.4 1.6 %copy-start = (f32[17,8,16,256]{3,2,1,0:T(8,128)S(1)}, f32[17,8,16,256]{3,2,1,0:T(8,128)}, u32[]{:S(2)}) copy-start(f32[17,8,16,256]{3,2,1,0:T(8,128)} %cells_ref.5) | copy-start | bytes 6684676
  14.0 1.0 %copy-start.4 = (f32[8,16384]{1,0:T(8,128)S(1)}, f32[8,16384]{1,0:T(8,128)}, u32[]{:S(2)}) copy-start(f32[8,16384]{1,0:T(8,128)} %parcels_ref.1) | copy-start | bytes 1572868
  15.0 0.7 %copy-start.6 = (s32[2,1024]{1,0:T(2,128)S(1)}, s32[2,1024]{1,0:T(2,128)}, u32[]{:S(2)}) copy-start(s32[2,1024]{1,0:T(2,128)} %crossing_ref.3) | copy-start | bytes 24580
  15.7 19.8 %copy-start.1 = (f32[17,8,16,256]{3,2,1,0:T(8,128)S(1)}, f32[17,8,16,256]{3,2,1,0:T(8,128)}, u32[]{:S(2)}) copy-start(f32[17,8,16,256]{3,2,1,0:T(8,128)} %cells_ref.5) | copy-start | bytes 6684676
  25.8 14.0 %collective-permute-start.2 = (f32[17,16,256]{2,1,0:T(8,128)S(1)}, f32[17,16,256]{2,1,0:T(8,128)S(1)}, u32[]{:S(2)}, u32[]{:S(2)}) collective-permute-start(f32[17,16,256]{2,1,0:T(8,128)S(1)} %get-tuple-element.11), channel_id=1, source_target_pairs={{0,4},{4,8},{8,12},{12,16},{16,20},{20,24},{24,28},{28,0},{1,5},{5... | collective-permute-start | bytes 835592 | tf_op jit(solution)/shard_map/ppermute | solution.py:427
  27.6 14.4 %collective-permute-start.3 = (f32[17,16,256]{2,1,0:T(8,128)S(1)}, f32[17,16,256]{2,1,0:T(8,128)S(1)}, u32[]{:S(2)}, u32[]{:S(2)}) collective-permute-start(f32[17,16,256]{2,1,0:T(8,128)S(1)} %get-tuple-element.12), channel_id=1, source_target_pairs={{4,0},{8,4},{12,8},{16,12},{20,16},{24,20},{28,24},{0,28},{5,1},{9... | collective-permute-start | bytes 835592 | tf_op jit(solution)/shard_map/ppermute | solution.py:428
  30.6 4.3 %collective-permute-start = (f32[15,8,256]{2,1,0:T(8,128)S(1)}, f32[15,8,256]{2,1,0:T(8,128)S(1)}, u32[]{:S(2)}, u32[]{:S(2)}) collective-permute-start(f32[15,8,256]{2,1,0:T(8,128)S(1)} %get-tuple-element.9), channel_id=1, source_target_pairs={{0,1},{1,2},{2,3},{3,0},{4,5},{5,6},{6,7},{7,4},{8,9},{9,10},{10,1... | collective-permute-start | bytes 368648 | tf_op jit(solution)/shard_map/ppermute | solution.py:429
  30.6 4.9 %collective-permute-start.1 = (f32[15,8,256]{2,1,0:T(8,128)S(1)}, f32[15,8,256]{2,1,0:T(8,128)S(1)}, u32[]{:S(2)}, u32[]{:S(2)}) collective-permute-start(f32[15,8,256]{2,1,0:T(8,128)S(1)} %get-tuple-element.10), channel_id=1, source_target_pairs={{1,0},{2,1},{3,2},{0,3},{5,4},{6,5},{7,6},{4,7},{9,8},{10,9},{11,1... | collective-permute-start | bytes 368648 | tf_op jit(solution)/shard_map/ppermute | solution.py:430
  37.5 1.2 %copy-start.2 = (f32[14,8,16,256]{3,2,1,0:T(8,128)}, f32[14,8,16,256]{3,2,1,0:T(8,128)S(1)}, u32[]{:S(2)}) copy-start(f32[14,8,16,256]{3,2,1,0:T(8,128)S(1)} %shard_map.87.inner_ref) | copy-start | bytes 5505028
  47.8 1.5 %copy-start.3 = (f32[14,8,16,256]{3,2,1,0:T(8,128)S(1)}, f32[14,8,16,256]{3,2,1,0:T(8,128)}, u32[]{:S(2)}) copy-start(f32[14,8,16,256]{3,2,1,0:T(8,128)} %copy-done.2) | copy-start | bytes 5505028

commit v2 on v1

--- a/solution.py
+++ b/solution.py
@@ -36,79 +36,127 @@
     return jnp.take_along_axis(values, index, axis=1, mode="promise_in_bounds")
 
 
+def split(value):
+    coarse = value.astype(BF16)
+    return coarse, (value - coarse.astype(F32)).astype(BF16)
+
+
 def advance_block(block):
-    diameter = block[6:7]
-    warmth = block[7:8]
-    velocity = block[3:6]
+    row = iota(block.shape, 0)
+    diameter = jnp.broadcast_to(block[6:7], block.shape)
+    warmth = jnp.broadcast_to(block[7:8], block.shape)
     factor = 0.8 / (1.0 + diameter * diameter)
-    velocity_new = velocity * (1.0 - factor)
-    position_new = block[0:3] + 0.5 * (velocity + velocity_new)
-    diameter_new = diameter * (1.0 - 0.05 * warmth)
-    warmth_new = warmth + factor * (1.0 - warmth)
-    return jnp.concatenate([position_new, velocity_new, diameter_new, warmth_new], axis=0)
-
-
-def advance_all(parcels_ref, advanced_ref):
-    diameter = parcels_ref[6:7, :]
-    warmth = parcels_ref[7:8, :]
-    velocity = parcels_ref[3:6, :]
-    factor = 0.8 / (1.0 + diameter * diameter)
-    velocity_new = velocity * (1.0 - factor)
-    advanced_ref[0:3, :] = parcels_ref[0:3, :] + 0.5 * (velocity + velocity_new)
-    advanced_ref[3:6, :] = velocity_new
-    advanced_ref[6:7, :] = diameter * (1.0 - 0.05 * warmth)
-    advanced_ref[7:8, :] = warmth + factor * (1.0 - warmth)
-
-
-def prepare_kernel(cells_ref, parcels_ref, crossing_ref, up_ref, down_ref, yup_ref, ydown_ref, advanced_ref):
+    slowed = block * (1.0 - factor)
+    travel = pltpu.roll(0.5 * (block + slowed), 5, 0)
+    shrunk = block * (1.0 - 0.05 * warmth)
+    warmed = block + factor * (1.0 - block)
+    return jnp.where(row < 3, block + travel, jnp.where(row < 6, slowed, jnp.where(row == 6, shrunk, warmed)))
+
+
+def prepare_kernel(
+    cells_hbm, parcels_hbm, crossing_hbm, mass_hbm, owner_hbm, cell_hbm,
+    up_ref, down_ref, yup_ref, ydown_ref, cells_ref, advanced_ref, crossing_ref, mass_ref, owner_ref, cell_ref,
+    parcels_ref, parts_ref, hot_ref, sems,
+):
     size_x, size_y, size_z = cells_ref.shape[1:]
-    up_ref[: COUNT + 1] = cells_ref[: COUNT + 1, size_x - 1]
-    down_ref[: COUNT + 1] = cells_ref[: COUNT + 1, 0]
+    face = slice(0, COUNT + 1)
+    copies = [
+        pltpu.make_async_copy(source, target, sems.at[i])
+        for i, (source, target) in enumerate(
+            (
+                (crossing_hbm, crossing_ref),
+                (parcels_hbm, parcels_ref),
+                (cells_hbm, cells_ref),
+                (cells_hbm.at[face, size_x - 1], up_ref.at[face]),
+                (cells_hbm.at[face, 0], down_ref.at[face]),
+                (mass_hbm, mass_ref),
+                (owner_hbm, owner_ref),
+                (cell_hbm, cell_ref),
+            )
+        )
+    ]
+    for copy in copies:
+        copy.start()
+    cross = crossing_ref.shape[1]
+    slot_total = parcels_ref.shape[1]
+    copies[0].wait()
+    for side in range(2):
+        for first in range(0, cross, LANES):
+            lower = jnp.broadcast_to(crossing_ref[side : side + 1, first : first + LANES] % LANES, (LANES, LANES))
+            hot = jnp.where(lower == iota((LANES, LANES), 0), 1.0, 0.0).astype(BF16)
+            at = slice(side * cross + first, side * cross + first + LANES)
+            hot_ref[:LANES, at] = hot
+            hot_ref[LANES:, at] = hot
+    copies[1].wait()
+
+    def advance_pair(i, unused):
+        first = pl.multiple_of(i * 2 * LANES, 2 * LANES)
+        blocks = []
+        for offset in (0, LANES):
+            at = pl.ds(pl.multiple_of(first + offset, LANES), LANES)
+            block = advance_block(parcels_ref[:, at])
+            advanced_ref[:, at] = block
+            blocks.append(block)
+        coarse, fine = split(jnp.concatenate(blocks, axis=0))
+        rows = pl.ds(pl.multiple_of(i * 16, 16), 16)
+        parts_ref[rows, :LANES] = coarse
+        parts_ref[rows, LANES:] = fine
+        return unused
+
+    lax.fori_loop(0, slot_total // (2 * LANES), advance_pair, 0, unroll=8)
+
+    halves_y, halves_z = size_y // 8, size_z // LANES
+    width = 2 * LANES
+    part_rows = parts_ref.shape[0]
+    step_rows = min(256, part_rows)
+    for side, out_ref in ((0, up_ref), (1, down_ref)):
+        for first in range(0, cross, width):
+            upper = jnp.broadcast_to(crossing_ref[side : side + 1, first : first + width] // LANES, (8, width))
+            total = jnp.zeros((8, width), F32)
+            at = slice(side * cross + first, side * cross + first + width)
+            for rows in range(0, part_rows, step_rows):
+                picked = jnp.dot(parts_ref[rows : rows + step_rows], hot_ref[:, at], preferred_element_type=F32)
+                for i in range(0, step_rows, 8):
+                    total = jnp.where(upper == (rows + i) // 8, picked[i : i + 8], total)
+            for offset in range(0, width, LANES):
+                layer, rest = divmod((first + offset) // LANES, halves_y * halves_z)
+                half_y, half_z = divmod(rest, halves_z)
+                out_ref[
+                    COUNT + 1 + layer, 8 * half_y : 8 * half_y + 8, LANES * half_z : LANES * (half_z + 1)
+                ] = total[:, offset : offset + LANES]
+
+    copies[2].wait()
     for c in range(COUNT + 1):
         source = c if c < COUNT else COUNT + 1
         yup_ref[c] = cells_ref[source, :, size_y - 1, :]
         ydown_ref[c] = cells_ref[source, :, 0, :]
-    advance_all(parcels_ref, advanced_ref)
-    slot_total = parcels_ref.shape[1]
-    cross = crossing_ref.shape[1]
-    halves_y, halves_z = size_y // 8, size_z // LANES
-    for side, out_ref in ((0, up_ref), (1, down_ref)):
-        for start in range(0, cross, 4 * LANES):
-            blocks = range(start, min(start + 4 * LANES, cross), LANES)
-            picks = []
-            for first in blocks:
-                slots = jnp.broadcast_to(crossing_ref[side : side + 1, first : first + LANES], (8, LANES))
-                picks.append((slots // LANES, slots % LANES))
-
-            def step(h, totals, picks=picks):
-                block = advanced_ref[:, pl.ds(pl.multiple_of(h * LANES, LANES), LANES)]
-                return tuple(
-                    jnp.where(high == h, lane_pick(block, low), total)
-                    for (high, low), total in zip(picks, totals)
-                )
-
-            totals = lax.fori_loop(
-                0, slot_total // LANES, step, tuple(jnp.zeros((8, LANES), F32) for unused in picks), unroll=8
-            )
-            for first, total in zip(blocks, totals):
-                at = first // LANES
-                layer, rest = divmod(at, halves_y * halves_z)
-                half_y, half_z = divmod(rest, halves_z)
-                out_ref[
-                    COUNT + 1 + layer, 8 * half_y : 8 * half_y + 8, LANES * half_z : LANES * (half_z + 1)
-                ] = total
-
-
-def prepare(cells, parcels, crossing):
+    for copy in copies[3:]:
+        copy.wait()
+
+
+HBM = pl.BlockSpec(memory_space=pltpu.HBM)
+
+
+def prepare(cells, parcels, crossing, mass, owner, cell):
     size_x, size_y, size_z = cells.shape[1:]
     layers = COUNT + 1 + 8 * crossing.shape[1] // (size_y * size_z)
     face = jax.ShapeDtypeStruct((layers, size_y, size_z), F32)
     side = jax.ShapeDtypeStruct((COUNT + 1, size_x, size_z), F32)
-    advanced = jax.ShapeDtypeStruct(parcels.shape, F32)
-    return call(
-        prepare_kernel, (face, face, side, side, advanced), (cells, parcels, crossing),
-        moved_bytes=6 << 20,
-    )
+    kept = [jax.ShapeDtypeStruct(a.shape, a.dtype) for a in (cells, parcels, crossing, mass, owner, cell)]
+    return pl.pallas_call(
+        prepare_kernel,
+        out_shape=[face, face, side, side] + kept,
+        in_specs=[HBM] * 6,
+        out_specs=[VMEM] * 10,
+        scratch_shapes=[
+            pltpu.VMEM(parcels.shape, F32),
+            pltpu.VMEM((8 * parcels.shape[1] // LANES, 2 * LANES), BF16),
+            pltpu.VMEM((2 * LANES, crossing.size), BF16),
+            pltpu.SemaphoreType.DMA((8,)),
+        ],
+        compiler_params=pltpu.CompilerParams(vmem_limit_bytes=24 << 20),
+        cost_estimate=pl.CostEstimate(flops=1 << 30, bytes_accessed=6 << 20, transcendentals=0),
+    )(cells, parcels, crossing, mass, owner, cell)
 
 
 def inverse_kernel(crossing_ref, high_ref, low_ref, hot_ref, value_ref):
@@ -144,35 +192,43 @@
     )
 
 
-def arrive_kernel(advanced_ref, high_ref, low_ref, before_ref, after_ref, out_ref):
+def arrive_kernel(advanced_ref, high_ref, low_ref, before_ref, after_ref, out_ref, parts_ref):
     slot_total = advanced_ref.shape[1]
     size_y, size_z = before_ref.shape[1:]
     halves_y, halves_z = size_y // 8, size_z // LANES
-    blocks = []
-    for ref in (before_ref, after_ref):
-        for layer in range(COUNT + 1, ref.shape[0]):
-            for half_y in range(halves_y):
-                for half_z in range(halves_z):
-                    blocks.append(
-                        (ref, layer, slice(8 * half_y, 8 * half_y + 8), slice(LANES * half_z, LANES * (half_z + 1)))
-                    )
-
-    def step(h, unused):
-        at = pl.ds(pl.multiple_of(h * LANES, LANES), LANES)
-        high = jnp.broadcast_to(high_ref[pl.ds(h, 1), :], (8, LANES))
-        low = jnp.broadcast_to(low_ref[pl.ds(h, 1), :], (8, LANES))
+    blocks = [
+        ref[layer, 8 * half_y : 8 * half_y + 8, LANES * half_z : LANES * (half_z + 1)]
+        for ref in (before_ref, after_ref)
+        for layer in range(COUNT + 1, before_ref.shape[0])
+        for half_y in range(halves_y)
+        for half_z in range(halves_z)
+    ]
+    for i in range(0, len(blocks), 2):
+        coarse, fine = split(jnp.concatenate(blocks[i : i + 2], axis=0))
+        parts_ref[8 * i : 8 * i + 16, :LANES] = coarse
+        parts_ref[8 * i : 8 * i + 16, LANES:] = fine
+    width = 2 * LANES
+
+    def step(i, unused):
+        at = pl.ds(pl.multiple_of(i * width, width), width)
+        high = jnp.concatenate([high_ref[pl.ds(2 * i, 1), :], high_ref[pl.ds(2 * i + 1, 1), :]], axis=1)
+        low = jnp.concatenate([low_ref[pl.ds(2 * i, 1), :], low_ref[pl.ds(2 * i + 1, 1), :]], axis=1)
+        hot = jnp.where(jnp.broadcast_to(low, (LANES, width)) == iota((LANES, width), 0), 1.0, 0.0).astype(BF16)
+        picked = jnp.dot(parts_ref[...], jnp.concatenate([hot, hot], axis=0), preferred_element_type=F32)
+        high = jnp.broadcast_to(high, (8, width))
         total = advanced_ref[:, at]
-        for number, (ref, layer, rows, lanes) in enumerate(blocks):
-            total = jnp.where(high == number + 1, lane_pick(ref[layer, rows, lanes], low), total)
+        for number in range(len(blocks)):
+            total = jnp.where(high == number + 1, picked[8 * number : 8 * number + 8], total)
         out_ref[:, at] = total
         return unused
 
-    lax.fori_loop(0, slot_total // LANES, step, 0, unroll=4)
+    lax.fori_loop(0, slot_total // width, step, 0, unroll=4)
 
 
 def arrive(advanced, high, low, before, after):
     return call(
         arrive_kernel, jax.ShapeDtypeStruct(advanced.shape, F32), (advanced, high, low, before, after),
+        scratch=(pltpu.VMEM((8 * 2 * (before.shape[0] - COUNT - 1) * before.shape[1] * before.shape[2] // (8 * LANES), 2 * LANES), BF16),),
         moved_bytes=4 << 20,
     )
 
@@ -230,7 +286,7 @@
     return call(
         functools.partial(bucket_kernel, owner_total, capacity),
         jax.ShapeDtypeStruct((9 * rows_out, LANES), F32),
-        (mass, owner.reshape(-1, LANES), cell.reshape(-1, LANES)),
+        (mass, owner, cell),
         scratch=(pltpu.VMEM((LANES, rows), BF16), pltpu.VMEM((2 * rows_out, rows), BF16)),
         moved_bytes=1 << 20,
     )
@@ -334,7 +390,7 @@
     )(cells, low, high, rate)
 
 
-def final_kernel(cells_ref, inner_ref, before_ref, after_ref, low_ref, high_ref, routed_ref, rate_ref, out_ref, depth_ref, spread_ref):
+def final_kernel(cells_ref, inner_ref, before_ref, after_ref, low_ref, high_ref, routed_ref, rate_ref, out_ref, depth_ref, spread_ref, mass_ref, plane_ref):
     size_x, size_y, size_z = cells_ref.shape[1:]
     groups = routed_ref.shape[0] // 9
     cell_rows = jnp.concatenate([routed_ref[9 * g + 8 : 9 * g + 9, :] for g in range(groups)], axis=0).astype(jnp.int32)
@@ -366,21 +422,25 @@
         ),
     }
     half = SECTIONS * size_y
+    planes = (cell_rows // size_z).astype(F32)
+    for g in range(groups):
+        at = slice(g * LANES, (g + 1) * LANES)
+        plane_ref[:, at] = jnp.broadcast_to(planes[g : g + 1], (size_y, LANES)).astype(BF16)
+        for s in range(SECTIONS):
+            coarse, fine = split(routed_ref[9 * g + s : 9 * g + s + 1, :])
+            mass_ref[s * size_y : (s + 1) * size_y, at] = jnp.broadcast_to(coarse.astype(F32), (size_y, LANES)).astype(BF16)
+            mass_ref[half + s * size_y : half + (s + 1) * size_y, at] = jnp.broadcast_to(
+                fine.astype(F32), (size_y, LANES)
+            ).astype(BF16)
+    zero = jnp.zeros((size_y, LANES), BF16)
     for x in range(size_x):
+        rows_y = (iota((size_y, LANES), 0) + x * size_y).astype(F32).astype(BF16)
         for g in range(groups):
             at = slice(g * LANES, (g + 1) * LANES)
-            plane = jnp.broadcast_to(cell_rows[g : g + 1] // size_z, (size_y, LANES))
-            hit = plane == x * size_y + iota((size_y, LANES), 0)
-            for s in range(SECTIONS):
-                mass = routed_ref[9 * g + s : 9 * g + s + 1, :]
-                coarse = mass.astype(BF16)
-                fine = (mass - coarse.astype(F32)).astype(BF16)
-                spread_ref[s * size_y : (s + 1) * size_y, at] = jnp.where(
-                    hit, jnp.broadcast_to(coarse.astype(F32), hit.shape), 0.0
-                ).astype(BF16)
-                spread_ref[half + s * size_y : half + (s + 1) * size_y, at] = jnp.where(
-                    hit, jnp.broadcast_to(fine.astype(F32), hit.shape), 0.0
-                ).astype(BF16)
+            hit = plane_ref[:, at] == rows_y
+            for s in range(2 * SECTIONS):
+                rows = slice(s * size_y, (s + 1) * size_y)
+                spread_ref[rows, at] = jnp.where(hit, mass_ref[rows, at], zero)
         added = jnp.dot(spread_ref[...], depth_ref[...], preferred_element_type=F32)
         if x in edge:
             edge[x]()
@@ -405,7 +465,12 @@
         out_shape=jax.ShapeDtypeStruct(inner_cells.shape, F32),
         in_specs=[VMEM] * 7 + [SMEM],
         out_specs=VMEM,
-        scratch_shapes=[pltpu.VMEM((rows, size_z), BF16), pltpu.VMEM((2 * SECTIONS * size_y, rows), BF16)],
+        scratch_shapes=[
+            pltpu.VMEM((rows, size_z), BF16),
+            pltpu.VMEM((2 * SECTIONS * size_y, rows), BF16),
+            pltpu.VMEM((2 * SECTIONS * size_y, rows), BF16),
+            pltpu.VMEM((size_y, rows), BF16),
+        ],
         compiler_params=pltpu.CompilerParams(vmem_limit_bytes=32 << 20),
         cost_estimate=pl.CostEstimate(flops=4 << 30, bytes_accessed=6 << 20, transcendentals=0),
     )(cells, inner_cells, before, after, low, high, routed, rate)
@@ -423,22 +488,24 @@
     up_x, down_x = ring(lax.axis_size("gx"))
     up_y, down_y = ring(lax.axis_size("gy"))
 
-    send_up, send_down, side_up, side_down, advanced = prepare(cell_state, parcels, crossing)
+    send_up, send_down, side_up, side_down, cells, advanced, slots, mass, owner, cell = prepare(
+        cell_state, parcels, crossing, conv_mass, conv_owner.reshape(-1, LANES), conv_cell.reshape(-1, LANES)
+    )
     before = lax.ppermute(send_up, "gx", up_x)
     after = lax.ppermute(send_down, "gx", down_x)
     low = lax.ppermute(side_up, "gy", up_y)
     high = lax.ppermute(side_down, "gy", down_y)
 
-    filled = bucket(conv_mass, conv_owner, conv_cell, owner_total, capacity)
+    filled = bucket(mass, owner, cell, owner_total, capacity)
     fold = LANES // capacity
     filled = filled.reshape(-1, 9, fold, capacity).transpose(0, 2, 1, 3).reshape(owner_total, 1, 9 * capacity)
     routed = lax.all_to_all(filled, ("gx", "gy"), split_axis=0, concat_axis=0, tiled=True)
     routed = routed.reshape(-1, fold, 9, capacity).transpose(0, 2, 1, 3).reshape(-1, LANES)
 
-    high_map, low_map = inverse_map(crossing, parcels.shape[1])
-    inner_cells = inner(cell_state, low, high, evap_rate)
+    high_map, low_map = inverse_map(slots, parcels.shape[1])
+    inner_cells = inner(cells, low, high, evap_rate)
     new_parcels = arrive(advanced, high_map, low_map, before, after)
-    new_cells = final(cell_state, inner_cells, before, after, low, high, routed, evap_rate)
+    new_cells = final(cells, inner_cells, before, after, low, high, routed, evap_rate)
     return (new_cells, new_parcels)
 
 

time: 58.8 us -> 56.8 us (0.966)
  Pallas kernels: 29.7 us -> 23.3 us
  local copies, waits for them, and re-layouts: 8.32 us -> 11.5 us
  waiting for transfers between devices: 5.73 us -> 7.02 us
    pallas_call x4 -> x3, Pallas kernels: 18.8 us -> 8.24 us  [call(): pl.pallas_call(kernel, out_shape=out_shape, in_specs=[VMEM] * len(operand...]
    pallas_call x0 -> x1, Pallas kernels: none -> 3.4 us  [prepare(): pl.pallas_call(prepare_kernel, out_shape=[face, face, side, side] + kept,...]
    unnamed x20 -> x32, local copies, waits for them, and re-layouts: 8.32 us -> 11.5 us
    ppermute x1, waiting for transfers between devices: 1.13 us -> 2.31 us  [on_device(): before = lax.ppermute(send_up, 'gx', up_x)]
    pallas_call x1, Pallas kernels: 8.99 us -> 9.7 us  [final(): pl.pallas_call(final_kernel, out_shape=jax.ShapeDtypeStruct(inner_cells.s...]
  transfers between devices with their start and end apart: 5 -> 5, of which waited for: 4 -> 4; matrix products, arithmetic and copies ran while one was open for 0% -> 0% of each run, Pallas kernels for 32% -> 14%
where the time goes in v2:
time: 56.8 us; the launch traced here: 56.3 us
  Pallas kernels  23.3 us (41%)
  starting transfers between devices  13.8 us (24%)
  local copies, waits for them, and re-layouts  11.5 us (20%)
  waiting for transfers between devices  7.02 us (12%)
  between operations  0.7 us (1%)
    unnamed x32, local copies, waits for them, and re-layouts  11.5 us
    pallas_call x1, Pallas kernels, final(): pl.pallas_call(final_kernel, out_shape=jax.ShapeDtypeStruct(inner_cells.s...  9.7 us
    pallas_call x3, Pallas kernels, call(): pl.pallas_call(kernel, out_shape=out_shape, in_specs=[VMEM] * len(operand...  8.24 us
    all_to_all x1, starting transfers between devices, on_device(): lax.all_to_all(filled, ('gx', 'gy'), split_axis=0, concat_axis=0, tiled=T...  7.3 us
    pallas_call x1, Pallas kernels, prepare(): pl.pallas_call(prepare_kernel, out_shape=[face, face, side, side] + kept,...  3.4 us
    ppermute x1, starting transfers between devices, on_device(): after = lax.ppermute(send_down, 'gx', down_x)  2.95 us
    ppermute x1, waiting for transfers between devices, on_device(): before = lax.ppermute(send_up, 'gx', up_x)  2.31 us
    ppermute x1, waiting for transfers between devices, on_device(): after = lax.ppermute(send_down, 'gx', down_x)  2.01 us
  transfers between devices with their start and end apart: 5, of which 4 were waited for; matrix products, arithmetic and copies ran while one was open for 0% of the time, Pallas kernels for 14%

profile of v2, /device:TPU:0, one launch (start us, length us, event | category | flops | bytes accessed | tf_op | source)
XLA Modules:
  0.0 56.3 jit_solution(9184417977195032321)
XLA Ops:
  0.6 1.6 %copy-done.7 = f32[17,8,16,256]{3,2,1,0:T(8,128)S(1)} copy-done((f32[17,8,16,256]{3,2,1,0:T(8,128)S(1)}, f32[17,8,16,256]{3,2,1,0:T(8,128)}, u32[]{:S(2)}) %copy-start.7) | copy-done | bytes 2228248
  2.3 1.0 %copy-done.8 = f32[8,16384]{1,0:T(8,128)S(1)} copy-done((f32[8,16384]{1,0:T(8,128)S(1)}, f32[8,16384]{1,0:T(8,128)}, u32[]{:S(2)}) %copy-start.8) | copy-done | bytes 524312
  3.3 0.8 %copy-done.12 = f32[8,2048]{1,0:T(8,128)S(1)} copy-done((f32[8,2048]{1,0:T(8,128)S(1)}, f32[8,2048]{1,0:T(8,128)}, u32[]{:S(2)}) %copy-start.12) | copy-done | bytes 65560
  4.1 0.7 %copy-done.13 = s32[2,1024]{1,0:T(2,128)S(1)} copy-done((s32[2,1024]{1,0:T(2,128)S(1)}, s32[2,1024]{1,0:T(2,128)}, u32[]{:S(2)}) %copy-start.13) | copy-done | bytes 8216
  4.8 0.7 %copy-done.14 = s32[2048,1]{0,1:T(1,128)S(1)} copy-done((s32[2048,1]{0,1:T(1,128)S(1)}, s32[2048,1]{0,1:T(1,128)}, u32[]{:S(2)}) %copy-start.14) | copy-done | bytes 8216
  6.2 3.4 %shard_map.86 = (f32[17,16,256]{2,1,0:T(8,128)}, f32[17,16,256]{2,1,0:T(8,128)S(1)}, f32[15,8,256]{2,1,0:T(8,128)S(1)}, f32[15,8,256]{2,1,0:T(8,128)S(1)}, f32[1...) custom-call(f32[17,8,16,256]{3,2,1,0:T(8,128)S(1)} %copy-done.7, ...), custom_call_target="tpu_custom_call" | custom-call | flops 1073741824 | bytes 6291456 | tf_op jit(solution)/shard_map/pallas_call | solution.py:146
  9.7 0.7 %copy-done.9 = f32[17,16,256]{2,1,0:T(8,128)} copy-done((f32[17,16,256]{2,1,0:T(8,128)}, f32[17,16,256]{2,1,0:T(8,128)S(1)}, u32[]{:S(2)}) %copy-start.9) | copy-done | bytes 278552
  11.0 2.2 %shard_map.88 = f32[288,128]{1,0:T(8,128)} custom-call(f32[8,2048]{1,0:T(8,128)S(1)} %get-tuple-element.19.mass_ref, s32[16,128]{1,0:T(8,128)S(1)} %get-tuple-element.20.owner_ref, s32[16,128]{1,0:T(8,128)S(1)} %get-tuple-element.21.cell_ref), custom_call_target="tpu_custom_call" | custom-call | bytes 1048576 | tf_op jit(solution)/shard_map/pallas_call | solution.py:20
  13.2 7.3 %all-to-all-start = ((f32[32,1,1152]{2,1,0:T(1,128)}), f32[32,1,1152]{2,1,0:T(1,128)S(1)}, u32[]{:S(2)}, u32[]{:S(2)}) async-start(f32[32,1,1152]{2,1,0:T(1,128)} %bitcast.2), calls=%async_computation | async-start | bytes 294912 | tf_op jit(solution)/shard_map/all_to_all | solution.py:502
  20.5 1.8 %collective-permute-start.2 = (f32[17,16,256]{2,1,0:T(8,128)}, f32[17,16,256]{2,1,0:T(8,128)S(1)}, u32[]{:S(2)}, u32[]{:S(2)}) collective-permute-start(f32[17,16,256]{2,1,0:T(8,128)} %get-tuple-element.17), channel_id=1, source_target_pairs={{0,4},{4,8},{8,12},{12,16},{16,20},{20,24},{24,28},{28,0},{1,5},{5... | collective-permute-start | bytes 835592 | tf_op jit(solution)/shard_map/ppermute | solution.py:494
  22.3 3.0 %collective-permute-start.3 = (f32[17,16,256]{2,1,0:T(8,128)}, f32[17,16,256]{2,1,0:T(8,128)S(1)}, u32[]{:S(2)}, u32[]{:S(2)}) collective-permute-start(f32[17,16,256]{2,1,0:T(8,128)} %copy-done.9), channel_id=1, source_target_pairs={{4,0},{8,4},{12,8},{16,12},{20,16},{24,20},{28,24},{0,28},{5,1},{9... | collective-permute-start | bytes 835592 | tf_op jit(solution)/shard_map/ppermute | solution.py:495
  25.3 1.7 %collective-permute-start.1 = (f32[15,8,256]{2,1,0:T(8,128)}, f32[15,8,256]{2,1,0:T(8,128)S(1)}, u32[]{:S(2)}, u32[]{:S(2)}) collective-permute-start(f32[15,8,256]{2,1,0:T(8,128)} %copy-done.10), channel_id=1, source_target_pairs={{1,0},{2,1},{3,2},{0,3},{5,4},{6,5},{7,6},{4,7},{9,8},{10,9},{11,1... | collective-permute-start | bytes 368648 | tf_op jit(solution)/shard_map/ppermute | solution.py:497
  27.0 0.8 %shard_map.90 = (s32[128,128]{1,0:T(8,128)S(1)}, s32[128,128]{1,0:T(8,128)S(1)}) custom-call(s32[2,1024]{1,0:T(2,128)S(1)} %get-tuple-element.23.crossing_ref), custom_call_target="tpu_custom_call" | custom-call | flops 134217728 | bytes 1048576 | tf_op jit(solution)/shard_map/pallas_call | solution.py:20
  27.8 2.0 %collective-permute-done.low_ref = f32[15,8,256]{2,1,0:T(8,128)S(1)} collective-permute-done((f32[15,8,256]{2,1,0:T(8,128)}, f32[15,8,256]{2,1,0:T(8,128)S(1)}, u32[]{:S(2)}, u32[]{:S(2)}) %collective-permute-start) | collective-permute-done | bytes 122912 | tf_op jit(solution)/shard_map/ppermute | solution.py:496
  29.8 0.7 %collective-permute-done.1.high_ref = f32[15,8,256]{2,1,0:T(8,128)S(1)} collective-permute-done((f32[15,8,256]{2,1,0:T(8,128)}, f32[15,8,256]{2,1,0:T(8,128)S(1)}, u32[]{:S(2)}, u32[]{:S(2)}) %collective-permute-start.1) | collective-permute-done | bytes 122912 | tf_op jit(solution)/shard_map/ppermute | solution.py:497
  30.5 2.0 %shard_map.87.inner_ref = f32[14,8,16,256]{3,2,1,0:T(8,128)S(1)} custom-call(f32[17,8,16,256]{3,2,1,0:T(8,128)S(1)} %get-tuple-element.14.cells_ref, f32[15,8,256]{2,1,0:T(8,128)S(1)} %collective-permute-done.low_ref, f32[15,8,256]{2,1,0:T(8,128)S(1)} %collective-permute-done.1.high_ref, f32[8]{0:T(128)S(1)} %copy-done.6), custom_call_target="tpu_custom_call" | custom-call | flops 20971520 | bytes 4194304 | tf_op jit(solution)/shard_map/pallas_call | solution.py:383
  32.5 1.2 %copy-done = f32[14,8,16,256]{3,2,1,0:T(8,128)} copy-done((f32[14,8,16,256]{3,2,1,0:T(8,128)}, f32[14,8,16,256]{3,2,1,0:T(8,128)S(1)}, u32[]{:S(2)}) %copy-start) | copy-done | bytes 1835032
  33.7 2.3 %collective-permute-done.2.before_ref = f32[17,16,256]{2,1,0:T(8,128)S(1)} collective-permute-done((f32[17,16,256]{2,1,0:T(8,128)}, f32[17,16,256]{2,1,0:T(8,128)S(1)}, u32[]{:S(2)}, u32[]{:S(2)}) %collective-permute-start.2) | collective-permute-done | bytes 278560 | tf_op jit(solution)/shard_map/ppermute | solution.py:494
  36.0 2.0 %collective-permute-done.3.after_ref = f32[17,16,256]{2,1,0:T(8,128)S(1)} collective-permute-done((f32[17,16,256]{2,1,0:T(8,128)}, f32[17,16,256]{2,1,0:T(8,128)S(1)}, u32[]{:S(2)}, u32[]{:S(2)}) %collective-permute-start.3) | collective-permute-done | bytes 278560 | tf_op jit(solution)/shard_map/ppermute | solution.py:495
  38.0 5.3 %shard_map.91 = f32[8,16384]{1,0:T(8,128)} custom-call(f32[8,16384]{1,0:T(8,128)S(1)} %get-tuple-element.22.advanced_ref, s32[128,128]{1,0:T(8,128)S(1)} %get-tuple-element.24.high_ref, s32[128,128]{1,0:T(8,128)S(1)} %get-tuple-element.25.low_ref, f32[17,16,256]{2,1,0:T(8,128)S(1)} %collective-permute-done.2.before_ref, ...), custom_call_target="tpu_custom_call" | custom-call | bytes 4194304 | tf_op jit(solution)/shard_map/pallas_call | solution.py:20
  43.3 1.5 %copy-done.1 = f32[14,8,16,256]{3,2,1,0:T(8,128)S(1)} copy-done((f32[14,8,16,256]{3,2,1,0:T(8,128)S(1)}, f32[14,8,16,256]{3,2,1,0:T(8,128)}, u32[]{:S(2)}) %copy-start.1) | copy-done | bytes 1835032
  44.8 0.9 %copy-done.3 = f32[15,8,256]{2,1,0:T(8,128)S(1)} copy-done((f32[15,8,256]{2,1,0:T(8,128)S(1)}, f32[15,8,256]{2,1,0:T(8,128)}, u32[]{:S(2)}) %copy-start.3) | copy-done | bytes 122904
  45.7 0.9 %copy-done.5 = f32[15,8,256]{2,1,0:T(8,128)S(1)} copy-done((f32[15,8,256]{2,1,0:T(8,128)S(1)}, f32[15,8,256]{2,1,0:T(8,128)}, u32[]{:S(2)}) %copy-start.5) | copy-done | bytes 122904
  46.6 9.7 %shard_map.89 = f32[14,8,16,256]{3,2,1,0:T(8,128)} custom-call(f32[17,8,16,256]{3,2,1,0:T(8,128)S(1)} %get-tuple-element.14.cells_ref, f32[14,8,16,256]{3,2,1,0:T(8,128)S(1)} %copy-done.1, f32[17,16,256]{2,1,0:T(8,128)S(1)} %collective-permute-done.2.before_ref, f32[17,16,256]{2,1,0:T(8,128)S(1)} %collective-permute-done.3.after_ref, ...), custom_call_target="tpu_custom_call" | custom-call | flops 4294967296 | bytes 6291456 | tf_op jit(solution)/shard_map/pallas_call | solution.py:463
  (24 shorter events, 1.4 us)
Async XLA Ops:
  0.6 1.6 %copy-start.7 = (f32[17,8,16,256]{3,2,1,0:T(8,128)S(1)}, f32[17,8,16,256]{3,2,1,0:T(8,128)}, u32[]{:S(2)}) copy-start(f32[17,8,16,256]{3,2,1,0:T(8,128)} %cells_hbm.1) | copy-start | bytes 6684676
  2.3 1.0 %copy-start.8 = (f32[8,16384]{1,0:T(8,128)S(1)}, f32[8,16384]{1,0:T(8,128)}, u32[]{:S(2)}) copy-start(f32[8,16384]{1,0:T(8,128)} %parcels_hbm.1) | copy-start | bytes 1572868
  3.3 0.8 %copy-start.12 = (f32[8,2048]{1,0:T(8,128)S(1)}, f32[8,2048]{1,0:T(8,128)}, u32[]{:S(2)}) copy-start(f32[8,2048]{1,0:T(8,128)} %mass_hbm.1) | copy-start | bytes 196612
  4.1 0.7 %copy-start.13 = (s32[2,1024]{1,0:T(2,128)S(1)}, s32[2,1024]{1,0:T(2,128)}, u32[]{:S(2)}) copy-start(s32[2,1024]{1,0:T(2,128)} %crossing_hbm.1) | copy-start | bytes 24580
  4.8 0.7 %copy-start.14 = (s32[2048,1]{0,1:T(1,128)S(1)}, s32[2048,1]{0,1:T(1,128)}, u32[]{:S(2)}) copy-start(s32[2048,1]{0,1:T(1,128)} %param.12) | copy-start | bytes 24580
  5.5 0.7 %copy-start.15 = (s32[2048]{0:T(1024)S(1)}, s32[2048]{0:T(1024)}, u32[]{:S(2)}) copy-start(s32[2048]{0:T(1024)} %param.13) | copy-start | bytes 24580
  6.2 24.3 %copy-start.6 = (f32[8]{0:T(128)S(1)}, f32[8]{0:T(128)}, u32[]{:S(2)}) copy-start(f32[8]{0:T(128)} %rate_ref.3) | copy-start | bytes 100
  9.6 0.7 %copy-start.9 = (f32[17,16,256]{2,1,0:T(8,128)}, f32[17,16,256]{2,1,0:T(8,128)S(1)}, u32[]{:S(2)}) copy-start(f32[17,16,256]{2,1,0:T(8,128)S(1)} %get-tuple-element.18) | copy-start | bytes 835588
  10.4 0.6 %copy-start.11 = (f32[15,8,256]{2,1,0:T(8,128)}, f32[15,8,256]{2,1,0:T(8,128)S(1)}, u32[]{:S(2)}) copy-start(f32[15,8,256]{2,1,0:T(8,128)S(1)} %get-tuple-element.15) | copy-start | bytes 368644
  11.0 2.2 %copy-start.10 = (f32[15,8,256]{2,1,0:T(8,128)}, f32[15,8,256]{2,1,0:T(8,128)S(1)}, u32[]{:S(2)}) copy-start(f32[15,8,256]{2,1,0:T(8,128)S(1)} %get-tuple-element.16) | copy-start | bytes 368644
  13.2 30.1 %all-to-all-start = ((f32[32,1,1152]{2,1,0:T(1,128)}), f32[32,1,1152]{2,1,0:T(1,128)S(1)}, u32[]{:S(2)}, u32[]{:S(2)}) async-start(f32[32,1,1152]{2,1,0:T(1,128)} %bitcast.2), calls=%async_computation | async-start | bytes 294912 | tf_op jit(solution)/shard_map/all_to_all | solution.py:502
  20.5 15.5 %collective-permute-start.2 = (f32[17,16,256]{2,1,0:T(8,128)}, f32[17,16,256]{2,1,0:T(8,128)S(1)}, u32[]{:S(2)}, u32[]{:S(2)}) collective-permute-start(f32[17,16,256]{2,1,0:T(8,128)} %get-tuple-element.17), channel_id=1, source_target_pairs={{0,4},{4,8},{8,12},{12,16},{16,20},{20,24},{24,28},{28,0},{1,5},{5... | collective-permute-start | bytes 835592 | tf_op jit(solution)/shard_map/ppermute | solution.py:494
  22.3 15.7 %collective-permute-start.3 = (f32[17,16,256]{2,1,0:T(8,128)}, f32[17,16,256]{2,1,0:T(8,128)S(1)}, u32[]{:S(2)}, u32[]{:S(2)}) collective-permute-start(f32[17,16,256]{2,1,0:T(8,128)} %copy-done.9), channel_id=1, source_target_pairs={{4,0},{8,4},{12,8},{16,12},{20,16},{24,20},{28,24},{0,28},{5,1},{9... | collective-permute-start | bytes 835592 | tf_op jit(solution)/shard_map/ppermute | solution.py:495
  25.3 4.5 %collective-permute-start = (f32[15,8,256]{2,1,0:T(8,128)}, f32[15,8,256]{2,1,0:T(8,128)S(1)}, u32[]{:S(2)}, u32[]{:S(2)}) collective-permute-start(f32[15,8,256]{2,1,0:T(8,128)} %copy-done.11), channel_id=1, source_target_pairs={{0,1},{1,2},{2,3},{3,0},{4,5},{5,6},{6,7},{7,4},{8,9},{9,10},{10,1... | collective-permute-start | bytes 368648 | tf_op jit(solution)/shard_map/ppermute | solution.py:496
  25.3 5.2 %collective-permute-start.1 = (f32[15,8,256]{2,1,0:T(8,128)}, f32[15,8,256]{2,1,0:T(8,128)S(1)}, u32[]{:S(2)}, u32[]{:S(2)}) collective-permute-start(f32[15,8,256]{2,1,0:T(8,128)} %copy-done.10), channel_id=1, source_target_pairs={{1,0},{2,1},{3,2},{0,3},{5,4},{6,5},{7,6},{4,7},{9,8},{10,9},{11,1... | collective-permute-start | bytes 368648 | tf_op jit(solution)/shard_map/ppermute | solution.py:497
  29.8 8.2 %copy-start.2 = (f32[15,8,256]{2,1,0:T(8,128)}, f32[15,8,256]{2,1,0:T(8,128)S(1)}, u32[]{:S(2)}) copy-start(f32[15,8,256]{2,1,0:T(8,128)S(1)} %collective-permute-done.low_ref) | copy-start | bytes 368644
  30.5 7.5 %copy-start.4 = (f32[15,8,256]{2,1,0:T(8,128)}, f32[15,8,256]{2,1,0:T(8,128)S(1)}, u32[]{:S(2)}) copy-start(f32[15,8,256]{2,1,0:T(8,128)S(1)} %collective-permute-done.1.high_ref) | copy-start | bytes 368644
  32.5 1.2 %copy-start = (f32[14,8,16,256]{3,2,1,0:T(8,128)}, f32[14,8,16,256]{3,2,1,0:T(8,128)S(1)}, u32[]{:S(2)}) copy-start(f32[14,8,16,256]{3,2,1,0:T(8,128)S(1)} %shard_map.87.inner_ref) | copy-start | bytes 5505028
  43.3 1.5 %copy-start.1 = (f32[14,8,16,256]{3,2,1,0:T(8,128)S(1)}, f32[14,8,16,256]{3,2,1,0:T(8,128)}, u32[]{:S(2)}) copy-start(f32[14,8,16,256]{3,2,1,0:T(8,128)} %copy-done) | copy-start | bytes 5505028
  44.8 0.9 %copy-start.3 = (f32[15,8,256]{2,1,0:T(8,128)S(1)}, f32[15,8,256]{2,1,0:T(8,128)}, u32[]{:S(2)}) copy-start(f32[15,8,256]{2,1,0:T(8,128)} %copy-done.2) | copy-start | bytes 368644
  45.7 0.9 %copy-start.5 = (f32[15,8,256]{2,1,0:T(8,128)S(1)}, f32[15,8,256]{2,1,0:T(8,128)}, u32[]{:S(2)}) copy-start(f32[15,8,256]{2,1,0:T(8,128)} %copy-done.4) | copy-start | bytes 368644

commit v3 on v1

v3 whole, which is shorter than its diff:
```python
import functools

import jax
import jax.numpy as jnp
from jax import lax
from jax.experimental import pallas as pl
from jax.experimental.pallas import tpu as pltpu
from jax.sharding import PartitionSpec as P

SECTIONS = 8
SPECIES = 6
COUNT = SECTIONS + SPECIES
LANES = 128
WIDE = 256
WINDOW = 4
F32 = jnp.float32
BF16 = jnp.bfloat16
ANY = pl.BlockSpec(memory_space=pl.ANY)
SMEM = pl.BlockSpec(memory_space=pltpu.SMEM)
ALL = 63 << 20
MOST = 40 << 20


def call(kernel, out_shape, operands, scratch, in_specs=None, aliases=None, flops=0, moved_bytes=0, grant=MOST):
    many = isinstance(out_shape, (list, tuple))
    return pl.pallas_call(
        kernel,
        out_shape=out_shape,
        in_specs=in_specs or [ANY] * len(operands),
        out_specs=[ANY] * len(out_shape) if many else ANY,
        scratch_shapes=scratch,
        input_output_aliases=aliases or {},
        compiler_params=pltpu.CompilerParams(vmem_limit_bytes=grant),
        cost_estimate=pl.CostEstimate(flops=flops, bytes_accessed=moved_bytes, transcendentals=0),
    )(*operands)


def iota(shape, axis):
    return lax.broadcasted_iota(jnp.int32, shape, axis)


def packed(value):
    return value.astype(F32).astype(BF16)


def split(value):
    coarse = value.astype(BF16)
    return coarse, (value - coarse.astype(F32)).astype(BF16)


def rows_of(row, count):
    return jnp.broadcast_to(row, (count, row.shape[1])).astype(BF16)


def hot_columns(lower, count):
    return jnp.where(rows_of(lower.astype(F32), count) == packed(iota((count, LANES), 0)), 1.0, 0.0).astype(BF16)


def contract_lanes(left, right):
    return lax.dot_general(left, right, (((1,), (1,)), ((), ())), preferred_element_type=F32)


def advance_block(block):
    row = iota(block.shape, 0)
    diameter = jnp.broadcast_to(block[6:7], block.shape)
    warmth = jnp.broadcast_to(block[7:8], block.shape)
    factor = 0.8 / (1.0 + diameter * diameter)
    slowed = block * (1.0 - factor)
    travel = pltpu.roll(0.5 * (block + slowed), 5, 0)
    shrunk = block * (1.0 - 0.05 * warmth)
    warmed = block + factor * (1.0 - block)
    return jnp.where(row < 3, block + travel, jnp.where(row < 6, slowed, jnp.where(row == 6, shrunk, warmed)))


def scatter_left(left_ref, at, upper, uppers, coarse, fine):
    upper = rows_of(upper.astype(F32), 16)
    twice_coarse = jnp.concatenate([coarse.astype(F32)] * 2, axis=0).astype(BF16)
    twice_fine = jnp.concatenate([fine.astype(F32)] * 2, axis=0).astype(BF16)
    zero = jnp.zeros((16, LANES), BF16)
    pair = iota((16, LANES), 0) // 8
    for u in range(0, uppers, 2):
        hit = upper == packed(pair + u)
        left_ref[8 * u : 8 * u + 16, at] = jnp.where(hit, twice_coarse, zero)
        left_ref[8 * (uppers + u) : 8 * (uppers + u) + 16, at] = jnp.where(hit, twice_fine, zero)


def bucket_into(owner_total, capacity, mass_ref, owner_ref, cell_ref, out_ref, left_ref, hot_ref):
    blocks = owner_ref.shape[0]
    uppers = out_ref.shape[0] // 9 // 2
    strict = iota((LANES, 2 * LANES), 0) < iota((LANES, 2 * LANES), 1)
    strict = jnp.where(strict, 1.0, 0.0).astype(BF16)
    owners = owner_ref[...]
    cells = cell_ref[...]
    hots = [
        jnp.where(jnp.broadcast_to(owners[b : b + 1], (owner_total, LANES)) == iota((owner_total, LANES), 0), 1.0, 0.0)
        for b in range(blocks)
    ]
    ranks = jnp.dot(jnp.concatenate(hots, axis=0).astype(BF16), strict, preferred_element_type=F32)
    carry = jnp.zeros((owner_total, LANES), F32)
    base = 16 * uppers
    for b in range(blocks):
        part = ranks[b * owner_total : (b + 1) * owner_total]
        rank = jnp.sum(hots[b] * (part[:, :LANES] + carry), axis=0, keepdims=True).astype(jnp.int32)
        carry = carry + part[:, LANES:]
        spot = owners[b : b + 1] * capacity + rank
        at = slice(b * LANES, (b + 1) * LANES)
        hot_ref[:, at] = hot_columns(spot % WIDE, WIDE)
        coarse, fine = split(mass_ref[:, at])
        upper = spot // WIDE
        scatter_left(left_ref, at, upper, uppers, coarse, fine)
        hit = rows_of(upper.astype(F32), uppers) == packed(iota((uppers, LANES), 0))
        zero = jnp.zeros((uppers, LANES), BF16)
        cell = cells[b : b + 1]
        left_ref[base : base + uppers, at] = jnp.where(hit, rows_of((cell // WIDE).astype(F32), uppers), zero)
        left_ref[base + uppers : base + 2 * uppers, at] = jnp.where(
            hit, rows_of((cell % WIDE).astype(F32), uppers), zero
        )
        left_ref[base + 2 * uppers : base + 3 * uppers, at] = jnp.where(hit, 1.0, 0.0).astype(BF16)
    placed = contract_lanes(left_ref[...], hot_ref[...])
    cell = placed[base : base + uppers] * float(WIDE) + placed[base + uppers : base + 2 * uppers]
    cell = jnp.where(placed[base + 2 * uppers : base + 3 * uppers] > 0.5, cell, -1.0)
    for u in range(uppers):
        mass = placed[8 * u : 8 * u + 8] + placed[8 * (uppers + u) : 8 * (uppers + u) + 8]
        for half in range(2):
            row = 9 * (2 * u + half)
            lanes = slice(half * LANES, (half + 1) * LANES)
            out_ref[row : row + 8, :] = mass[:, lanes]
            out_ref[row + 8 : row + 9, :] = cell[u : u + 1, lanes]


def prepare_kernel(
    owner_total, capacity,
    cells_hbm, parcels_hbm, crossing_hbm, mass_hbm, owner_hbm, cell_hbm,
    up_hbm, down_hbm, yup_hbm, ydown_hbm, advanced_hbm, hot_hbm, filled_hbm,
    cells_ref, parcels_ref, crossing_ref, mass_ref, owner_ref, cell_ref,
    leave_ref, yup_ref, ydown_ref, advanced_ref, hot_ref, filled_ref,
    parts_ref, left_ref, spot_ref, sems,
):
    size_x, size_y, size_z = cells_hbm.shape[1:]
    face = slice(0, COUNT + 1)
    tail = slice(COUNT + 1, up_hbm.shape[0])
    pairs = [
        (crossing_hbm, crossing_ref),
        (owner_hbm, owner_ref),
        (cell_hbm, cell_ref),
        (mass_hbm, mass_ref),
        (parcels_hbm, parcels_ref),
        (cells_hbm, cells_ref),
        (cells_hbm.at[face, size_x - 1], up_hbm.at[face]),
        (cells_hbm.at[face, 0], down_hbm.at[face]),
        (filled_ref, filled_hbm),
        (hot_ref, hot_hbm),
        (advanced_ref, advanced_hbm),
        (leave_ref.at[0], up_hbm.at[tail]),
        (leave_ref.at[1], down_hbm.at[tail]),
        (yup_ref, yup_hbm),
        (ydown_ref, ydown_hbm),
    ]
    copies = [pltpu.make_async_copy(source, target, sems.at[i]) for i, (source, target) in enumerate(pairs)]
    for copy in copies[:8]:
        copy.start()
    cross = crossing_ref.shape[1]
    slot_total = parcels_ref.shape[1]
    for copy in copies[:4]:
        copy.wait()
    for side in range(2):
        for first in range(0, cross, LANES):
            lower = crossing_ref[side : side + 1, first : first + LANES] % WIDE
            hot_ref[:, side * cross + first : side * cross + first + LANES] = hot_columns(lower, WIDE)
    copies[9].start()
    bucket_into(owner_total, capacity, mass_ref, owner_ref, cell_ref, filled_ref, left_ref, spot_ref)
    copies[8].start()
    copies[4].wait()

    def advance_pair(i, unused):
        for number in range(2):
            blocks = []
            for half in range(2):
                at = pl.ds(pl.multiple_of((4 * i + 2 * number + half) * LANES, LANES), LANES)
                block = advance_block(parcels_ref[:, at])
                advanced_ref[:, at] = block
                blocks.append(block)
            parts_ref[pl.ds(pl.multiple_of((2 * i + number) * 8, 8), 8), :] = jnp.concatenate(blocks, axis=1)
        return unused

    lax.fori_loop(0, slot_total // (4 * LANES), advance_pair, 0, unroll=4)
    copies[10].start()

    halves_y, halves_z = size_y // 8, size_z // LANES
    part_rows = parts_ref.shape[0]
    step_rows = min(256, part_rows)
    for rows in range(0, part_rows, step_rows):
        coarse, fine = split(parts_ref[rows : rows + step_rows])
        for side in range(2):
            for first in range(0, cross, WIDE):
                upper = jnp.broadcast_to(crossing_ref[side : side + 1, first : first + WIDE] // WIDE, (8, WIDE))
                hot = hot_ref[:, side * cross + first : side * cross + first + WIDE]
                picked = jnp.dot(coarse, hot, preferred_element_type=F32) + jnp.dot(
                    fine, hot, preferred_element_type=F32
                )
                spots = []
                for offset in range(0, WIDE, LANES):
                    layer, rest = divmod((first + offset) // LANES, halves_y * halves_z)
                    half_y, half_z = divmod(rest, halves_z)
                    spots.append((side, layer, slice(8 * half_y, 8 * half_y + 8), slice(LANES * half_z, LANES * (half_z + 1))))
                if rows:
                    total = jnp.concatenate([leave_ref[spot] for spot in spots], axis=1)
                else:
                    total = jnp.zeros((8, WIDE), F32)
                for i in range(0, step_rows, 8):
                    total = jnp.where(upper == (rows + i) // 8, picked[i : i + 8], total)
                for number, spot in enumerate(spots):
                    leave_ref[spot] = total[:, number * LANES : (number + 1) * LANES]
    copies[11].start()
    copies[12].start()

    copies[5].wait()
    for c in range(COUNT + 1):
        source = c if c < COUNT else COUNT + 1
        yup_ref[c] = cells_ref[source, :, size_y - 1, :]
        ydown_ref[c] = cells_ref[source, :, 0, :]
    copies[13].start()
    copies[14].start()
    for copy in copies[6:]:
        copy.wait()


def prepare(cells, parcels, crossing, mass, owner, cell, owner_total, capacity):
    size_x, size_y, size_z = cells.shape[1:]
    extra = 8 * crossing.shape[1] // (size_y * size_z)
    places = owner_total * capacity
    shape = jax.ShapeDtypeStruct
    face = shape((COUNT + 1 + extra, size_y, size_z), F32)
    side = shape((COUNT + 1, size_x, size_z), F32)
    advanced = shape(parcels.shape, F32)
    hot = shape((WIDE, crossing.size), BF16)
    filled = shape((9 * places // LANES, LANES), F32)
    operands = (cells, parcels, crossing, mass, owner, cell)
    scratch = [pltpu.VMEM(a.shape, a.dtype) for a in operands]
    scratch += [pltpu.VMEM((2, extra, size_y, size_z), F32)]
    scratch += [pltpu.VMEM(a.shape, a.dtype) for a in (side, side, advanced, hot, filled)]
    scratch += [
        pltpu.VMEM((8 * parcels.shape[1] // WIDE, WIDE), F32),
        pltpu.VMEM((19 * places // WIDE, mass.shape[1]), BF16),
        pltpu.VMEM((WIDE, mass.shape[1]), BF16),
        pltpu.SemaphoreType.DMA((15,)),
    ]
    return call(
        functools.partial(prepare_kernel, owner_total, capacity),
        [face, face, side, side, advanced, hot, filled], operands, scratch,
        flops=2 << 30, moved_bytes=6 << 20, grant=ALL,
    )


def arrive_kernel(
    advanced_hbm, hot_hbm, crossing_hbm, before_hbm, after_hbm, out_hbm,
    advanced_ref, hot_ref, crossing_ref, come_ref, out_ref, left_ref, sems,
):
    cross = crossing_ref.shape[1]
    uppers = advanced_ref.shape[1] // WIDE
    tail = slice(COUNT + 1, before_hbm.shape[0])
    pairs = [
        (crossing_hbm, crossing_ref),
        (before_hbm.at[tail], come_ref.at[0]),
        (after_hbm.at[tail], come_ref.at[1]),
        (hot_hbm, hot_ref),
        (advanced_hbm, advanced_ref),
    ]
    copies = [pltpu.make_async_copy(source, target, sems.at[i]) for i, (source, target) in enumerate(pairs)]
    for copy in copies:
        copy.start()
    for copy in copies[:3]:
        copy.wait()
    size_y, size_z = come_ref.shape[2:]
    halves_y, halves_z = size_y // 8, size_z // LANES
    for side in range(2):
        for first in range(0, cross, LANES):
            layer, rest = divmod(first // LANES, halves_y * halves_z)
            half_y, half_z = divmod(rest, halves_z)
            block = come_ref[side, layer, 8 * half_y : 8 * half_y + 8, LANES * half_z : LANES * (half_z + 1)]
            coarse, fine = split(block)
            upper = crossing_ref[side : side + 1, first : first + LANES] // WIDE
            at = slice(side * cross + first, side * cross + first + LANES)
            scatter_left(left_ref, at, upper, uppers, coarse, fine)
            hit = rows_of(upper.astype(F32), uppers) == packed(iota((uppers, LANES), 0))
            left_ref[16 * uppers :, at] = jnp.where(hit, 1.0, 0.0).astype(BF16)
    copies[3].wait()
    hit = contract_lanes(left_ref[16 * uppers :], hot_ref[...])
    copies[4].wait()
    step = min(32, uppers)
    outs = []
    for u in range(0, uppers, step):
        total = contract_lanes(left_ref[8 * u : 8 * (u + step)], hot_ref[...]) + contract_lanes(
            left_ref[8 * (uppers + u) : 8 * (uppers + u + step)], hot_ref[...]
        )
        for i in range(step):
            at = slice((u + i) * WIDE, (u + i + 1) * WIDE)
            taken = jnp.broadcast_to(hit[u + i : u + i + 1], (8, WIDE)) > 0.5
            out_ref[:, at] = jnp.where(taken, total[8 * i : 8 * i + 8], advanced_ref[:, at])
        at = slice(u * WIDE, (u + step) * WIDE)
        out = pltpu.make_async_copy(out_ref.at[:, at], out_hbm.at[:, at], sems.at[len(pairs) + len(outs)])
        out.start()
        outs.append(out)
    for out in outs:
        out.wait()


def arrive(advanced, hot, crossing, before, after):
    uppers = advanced.shape[1] // WIDE
    extra = before.shape[0] - COUNT - 1
    return call(
        arrive_kernel, jax.ShapeDtypeStruct(advanced.shape, F32), (advanced, hot, crossing, before, after),
        [
            pltpu.VMEM(advanced.shape, F32),
            pltpu.VMEM(hot.shape, BF16),
            pltpu.VMEM(crossing.shape, crossing.dtype),
            pltpu.VMEM((2, extra) + before.shape[1:], F32),
            pltpu.VMEM(advanced.shape, F32),
            pltpu.VMEM((17 * uppers, crossing.size), BF16),
            pltpu.SemaphoreType.DMA((5 + -(-uppers // 32),)),
        ],
        flops=1 << 30, moved_bytes=3 << 20,
    )


def shift_up(value, axis):
    return pltpu.roll(value, value.shape[axis] - 1, axis)


def shift_down(value, axis):
    return pltpu.roll(value, 1, axis)


def slab_update(left, center, right, side_low, side_high, rate_ref, write):
    course = center(COUNT)
    size_y, size_z = course.shape
    first_row = iota((size_y, size_z), 0) == 0
    last_row = iota((size_y, size_z), 0) == size_y - 1

    def row_up(value, edge):
        return jnp.where(last_row, edge, shift_up(value, 0))

    def row_down(value, edge):
        return jnp.where(first_row, edge, shift_down(value, 0))

    face_x = 0.5 * (course + right(COUNT))
    face_x_low = 0.5 * (left(COUNT) + course)
    course_y = center(COUNT + 1)
    face_y = 0.5 * (course_y + row_up(course_y, side_high(COUNT)))
    face_y_low = 0.5 * (row_down(course_y, side_low(COUNT)) + course_y)
    course_z = center(COUNT + 2)
    lane = iota((size_y, size_z), 1)
    face_z = jnp.where(lane == size_z - 1, 0.0, 0.5 * (course_z + shift_up(course_z, 1)))
    face_z_low = jnp.where(lane == 0, 0.0, 0.5 * (shift_down(course_z, 1) + course_z))
    from_x_up, from_x_low = jnp.minimum(face_x, 0.0), jnp.maximum(face_x_low, 0.0)
    from_y_up, from_y_low = jnp.minimum(face_y, 0.0), jnp.maximum(face_y_low, 0.0)
    from_z_up, from_z_low = jnp.minimum(face_z, 0.0), jnp.maximum(face_z_low, 0.0)
    own = 1.0 - (
        (jnp.maximum(face_x, 0.0) - jnp.minimum(face_x_low, 0.0))
        + (jnp.maximum(face_y, 0.0) - jnp.minimum(face_y_low, 0.0))
        + (jnp.maximum(face_z, 0.0) - jnp.minimum(face_z_low, 0.0))
    )

    def moved(c):
        amount = center(c)
        total = own * amount
        total = total - from_x_up * right(c) + from_x_low * left(c)
        total = total - from_y_up * row_up(amount, side_high(c)) + from_y_low * row_down(amount, side_low(c))
        return total - from_z_up * shift_up(amount, 1) + from_z_low * shift_down(amount, 1)

    vapour = moved(SECTIONS)
    beside = 1.0 + vapour
    later = None
    gained = None
    for s in reversed(range(SECTIONS)):
        section = moved(s)
        loss = rate_ref[s] * section / beside
        value = section - loss
        if later is not None:
            value = value + 0.5 * later
            gained = later if gained is None else gained + later
        write(s, value)
        later = loss
    write(SECTIONS, vapour + later + 0.5 * gained)
    for c in range(SECTIONS + 1, COUNT):
        write(c, moved(c))


def inner_kernel(cells_hbm, low_hbm, high_hbm, rate_ref, out_hbm, cells_ref, low_ref, high_ref, out_ref, sems, out_sems):
    size_x = cells_hbm.shape[1]
    sides = [
        pltpu.make_async_copy(low_hbm, low_ref, sems.at[size_x]),
        pltpu.make_async_copy(high_hbm, high_ref, sems.at[size_x + 1]),
    ]

    def fetch(x):
        return pltpu.make_async_copy(cells_hbm.at[:, x], cells_ref.at[:, x], sems.at[x])

    def store(x):
        return pltpu.make_async_copy(out_ref.at[:, x], out_hbm.at[:, x], out_sems.at[x])

    for copy in sides:
        copy.start()
    for x in range(size_x):
        fetch(x).start()
    for copy in sides:
        copy.wait()
    fetch(0).wait()
    fetch(1).wait()

    def layer(x, unused):
        fetch(x + 1).wait()

        def write(c, value):
            out_ref[c, x] = value

        slab_update(
            lambda c: cells_ref[c, x - 1],
            lambda c: cells_ref[c, x],
            lambda c: cells_ref[c, x + 1],
            lambda c: low_ref[c, pl.ds(x, 1), :],
            lambda c: high_ref[c, pl.ds(x, 1), :],
            rate_ref,
            write,
        )
        store(x).start()
        return unused

    lax.fori_loop(1, size_x - 1, layer, 0)
    for x in range(1, size_x - 1):
        store(x).wait()


def inner(cells, low, high, rate):
    size_x = cells.shape[1]
    out = jax.ShapeDtypeStruct((COUNT,) + cells.shape[1:], F32)
    return call(
        inner_kernel, out, (cells, low, high, rate),
        [pltpu.VMEM(a.shape, F32) for a in (cells, low, high, out)]
        + [pltpu.SemaphoreType.DMA((size_x + 2,)), pltpu.SemaphoreType.DMA((size_x,))],
        in_specs=[ANY, ANY, ANY, SMEM],
        flops=20 << 20, moved_bytes=4 << 20,
    )


def put(ref, x, c, value):
    ref[c, x] = value


def final_kernel(
    cells_hbm, inner_hbm, before_hbm, after_hbm, low_hbm, high_hbm, routed_hbm, rate_ref, out_hbm,
    edge_ref, before_ref, after_ref, low_ref, high_ref, routed_ref, section_ref, species_ref,
    mass_ref, place_ref, spread_ref, depth_ref, sems,
):
    size_x, size_y, size_z = cells_hbm.shape[1:]
    last = size_x - 1
    face = slice(0, COUNT + 1)
    middle = slice(1, last)
    sections = slice(0, SECTIONS)
    others = slice(SECTIONS, COUNT)
    pairs = [
        (routed_hbm, routed_ref),
        (low_hbm, low_ref),
        (high_hbm, high_ref),
        (before_hbm.at[face], before_ref),
        (after_hbm.at[face], after_ref),
        (cells_hbm.at[:, 0:2], edge_ref.at[:, 0:2]),
        (cells_hbm.at[:, last - 1 : last + 1], edge_ref.at[:, 2:4]),
        (inner_hbm.at[sections, middle], section_ref.at[:, middle]),
        (species_ref.at[:, 0], out_hbm.at[others, 0]),
        (species_ref.at[:, 1], out_hbm.at[others, last]),
        (section_ref.at[:, 0:size_x], out_hbm.at[sections]),
    ]
    copies = [pltpu.make_async_copy(source, target, sems.at[i]) for i, (source, target) in enumerate(pairs)]
    for copy in copies[:8]:
        copy.start()

    copies[0].wait()
    groups = routed_ref.shape[0] // 9
    per = groups // 8
    span = LANES // per
    lane = iota((8, LANES), 1)
    for v in range(9):
        rows = routed_ref[pl.ds(v, groups, stride=9), :]
        for q in range(per):
            total = None
            for g in range(per):
                block = rows[8 * g : 8 * g + 8]
                if g != q:
                    block = pltpu.roll(block, (span * (g - q)) % LANES, 1)
                total = block if total is None else jnp.where(lane // span == g, block, total)
            mass_ref[q, v] = total

    bounds = []
    for q in range(per):
        cell = mass_ref[q, SECTIONS].astype(jnp.int32)
        layer = cell // (size_y * size_z)
        valid = cell >= 0
        bounds.append((jnp.min(jnp.where(valid, layer, size_x)), jnp.max(jnp.where(valid, layer, -1))))

    half = SECTIONS * WINDOW * size_y
    zero = jnp.zeros((size_y, LANES), BF16)

    def spread(q, first):
        cell = mass_ref[q, SECTIONS].astype(jnp.int32)
        plane = jnp.where(cell >= 0, cell // size_z - first * size_y, -1).astype(F32)
        depth = cell % size_z
        parts = [split(mass_ref[q, s]) for s in range(SECTIONS)]
        for i in range(8):
            at = slice(i * LANES, (i + 1) * LANES)
            depth_ref[q % 2, :, at] = hot_columns(depth[i : i + 1], size_z)
            plane_rows = rows_of(plane[i : i + 1], size_y)
            rows = [[rows_of(part[i : i + 1].astype(F32), size_y) for part in pair] for pair in parts]
            for w in range(WINDOW):
                hit = plane_rows == packed(iota((size_y, LANES), 0) + w * size_y)
                for s in range(SECTIONS):
                    base = (s * WINDOW + w) * size_y
                    for part in range(2):
                        spread_ref[q % 2, part * half + base : part * half + base + size_y, at] = jnp.where(
                            hit, rows[s][part], zero
                        )

    def deposit(q, first):
        added = contract_lanes(spread_ref[q % 2], depth_ref[q % 2])
        for s in range(SECTIONS):
            base = s * WINDOW * size_y
            rows = added[base : base + WINDOW * size_y] + added[half + base : half + base + WINDOW * size_y]
            at = pl.ds(first, WINDOW)
            section_ref[s, at] = section_ref[s, at] + rows.reshape(WINDOW, size_y, size_z)

    for copy in copies[1:8]:
        copy.wait()

    def write(x, number, c, value):
        if c < SECTIONS:
            section_ref[c, x] = value
        else:
            species_ref[c - SECTIONS, number] = value

    slab_update(
        lambda c: before_ref[c], lambda c: edge_ref[c, 0], lambda c: edge_ref[c, 1],
        lambda c: low_ref[c, 0:1, :], lambda c: high_ref[c, 0:1, :],
        rate_ref, functools.partial(write, 0, 0),
    )
    slab_update(
        lambda c: edge_ref[c, 2], lambda c: edge_ref[c, 3], lambda c: after_ref[c],
        lambda c: low_ref[c, last : last + 1, :], lambda c: high_ref[c, last : last + 1, :],
        rate_ref, functools.partial(write, last, 1),
    )
    copies[8].start()
    copies[9].start()
    for q in range(per):
        first = jnp.minimum(bounds[q][0], last)
        spread(q, first)
        deposit(q, first)
    for q in range(per):
        low, high = bounds[q]

        def more(t, unused, q=q, low=low):
            first = low + t * WINDOW
            spread(q, first)
            deposit(q, first)
            return unused

        lax.fori_loop(1, (high - low + WINDOW) // WINDOW, more, 0)
    copies[10].start()
    for copy in copies[8:]:
        copy.wait()


def final(cells, inner_cells, before, after, low, high, routed, rate):
    size_x, size_y, size_z = cells.shape[1:]
    per = routed.shape[0] // 9 // 8
    return call(
        final_kernel, jax.ShapeDtypeStruct(inner_cells.shape, F32),
        (cells, inner_cells, before, after, low, high, routed, rate),
        [
            pltpu.VMEM((cells.shape[0], 4, size_y, size_z), F32),
            pltpu.VMEM((COUNT + 1, size_y, size_z), F32),
            pltpu.VMEM((COUNT + 1, size_y, size_z), F32),
            pltpu.VMEM(low.shape, F32),
            pltpu.VMEM(high.shape, F32),
            pltpu.VMEM(routed.shape, F32),
            pltpu.VMEM((SECTIONS, size_x + WINDOW - 1, size_y, size_z), F32),
            pltpu.VMEM((SPECIES, 2, size_y, size_z), F32),
            pltpu.VMEM((per, SECTIONS + 1, 8, LANES), F32),
            pltpu.VMEM((8, LANES), F32),
            pltpu.VMEM((2, 2 * SECTIONS * WINDOW * size_y, 8 * LANES), BF16),
            pltpu.VMEM((2, size_z, 8 * LANES), BF16),
            pltpu.SemaphoreType.DMA((11,)),
        ],
        in_specs=[ANY] * 7 + [SMEM], aliases={1: 0},
        flops=4 << 30, moved_bytes=6 << 20,
    )


def ring(size):
    up = [(i, (i + 1) % size) for i in range(size)]
    return up, [(j, i) for i, j in up]


def on_device(cell_state, evap_rate, parcels, crossing, conv_mass, conv_owner, conv_cell):
    owner_total = lax.axis_size("gx") * lax.axis_size("gy")
    row_total = conv_owner.shape[0]
    capacity = 2 * row_total // owner_total
    up_x, down_x = ring(lax.axis_size("gx"))
    up_y, down_y = ring(lax.axis_size("gy"))

    send_up, send_down, side_up, side_down, advanced, hot, filled = prepare(
        cell_state, parcels, crossing, conv_mass, conv_owner.reshape(-1, LANES), conv_cell.reshape(-1, LANES),
        owner_total, capacity,
    )
    before = lax.ppermute(send_up, "gx", up_x)
    after = lax.ppermute(send_down, "gx", down_x)
    low = lax.ppermute(side_up, "gy", up_y)
    high = lax.ppermute(side_down, "gy", down_y)

    fold = LANES // capacity
    filled = filled.reshape(-1, 9, fold, capacity).transpose(0, 2, 1, 3).reshape(owner_total, 1, 9 * capacity)
    routed = lax.all_to_all(filled, ("gx", "gy"), split_axis=0, concat_axis=0, tiled=True)
    routed = routed.reshape(-1, fold, 9, capacity).transpose(0, 2, 1, 3).reshape(-1, LANES)

    inner_cells = inner(cell_state, low, high, evap_rate)
    new_parcels = arrive(advanced, hot, crossing, before, after)
    new_cells = final(cell_state, inner_cells, before, after, low, high, routed, evap_rate)
    return (new_cells, new_parcels)


def solution(mesh):
    in_specs = (
        P(None, "gx", "gy", None),
        P(),
        P(None, ("gx", "gy")),
        P(None, ("gx", "gy")),
        P(None, ("gx", "gy")),
        P(("gx", "gy"), None),
        P(("gx", "gy")),
    )
    out_specs = (P(None, "gx", "gy", None), P(None, ("gx", "gy")))
    return jax.shard_map(
        on_device, mesh=mesh, in_specs=in_specs, out_specs=out_specs, check_vma=False
    )
```

time: 58.8 us -> 55.3 us (0.940)
  Pallas kernels: 29.7 us -> 37.1 us
  local copies, waits for them, and re-layouts: 8.32 us -> 1.65 us
  starting transfers between devices: 13.8 us -> 11.2 us
  waiting for transfers between devices: 5.73 us -> 4.45 us
    pallas_call x6 -> x4, Pallas kernels: 29.7 us -> 37.1 us  [call(): pl.pallas_call(kernel, out_shape=out_shape, in_specs=in_specs or [ANY] *...]
    unnamed x20 -> x12, local copies, waits for them, and re-layouts: 8.32 us -> 1.65 us
    all_to_all x1, starting transfers between devices: 7.3 us -> 3.25 us  [on_device(): lax.all_to_all(filled, ('gx', 'gy'), split_axis=0, concat_axis=0, tiled=T...]
    ppermute x1, waiting for transfers between devices: 2.2 us -> 0.01 us  [on_device(): after = lax.ppermute(send_down, 'gx', down_x)]
    ppermute x1, waiting for transfers between devices: 1.78 us -> 3.46 us  [on_device(): low = lax.ppermute(side_up, 'gy', up_y)]
    ppermute x1, starting transfers between devices: 1.82 us -> 3.02 us  [on_device(): before = lax.ppermute(send_up, 'gx', up_x)]
    ppermute x1, waiting for transfers between devices: 1.13 us -> 0.01 us  [on_device(): before = lax.ppermute(send_up, 'gx', up_x)]
  transfers between devices with their start and end apart: 5 -> 5, of which waited for: 4 -> 2; matrix products, arithmetic and copies ran while one was open for 0% -> 0% of each run, Pallas kernels for 32% -> 13%
where the time goes in v3:
time: 55.3 us
  Pallas kernels  37.1 us (67%)
  starting transfers between devices  11.2 us (20%)
  waiting for transfers between devices  4.45 us (8%)
  local copies, waits for them, and re-layouts  1.65 us (3%)
  between operations  0.9 us (2%)
    pallas_call x4, Pallas kernels, call(): pl.pallas_call(kernel, out_shape=out_shape, in_specs=in_specs or [ANY] *...  37.1 us
    ppermute x1, waiting for transfers between devices, on_device(): low = lax.ppermute(side_up, 'gy', up_y)  3.46 us
    all_to_all x1, starting transfers between devices, on_device(): lax.all_to_all(filled, ('gx', 'gy'), split_axis=0, concat_axis=0, tiled=T...  3.25 us
    ppermute x1, starting transfers between devices, on_device(): after = lax.ppermute(send_down, 'gx', down_x)  3.1 us
    ppermute x1, starting transfers between devices, on_device(): before = lax.ppermute(send_up, 'gx', up_x)  3.02 us
    unnamed x12, local copies, waits for them, and re-layouts  1.65 us
    ppermute x1, starting transfers between devices, on_device(): high = lax.ppermute(side_down, 'gy', down_y)  1.49 us
  transfers between devices with their start and end apart: 5, of which 2 were waited for; matrix products, arithmetic and copies ran while one was open for 0% of the time, Pallas kernels for 13%

profile of v3, /device:TPU:0, one launch (start us, length us, event | category | flops | bytes accessed | tf_op | source)
XLA Modules:
  0.0 55.3 jit_solution(16029922318694536218)
XLA Ops:
  0.6 0.0 copy-start.2
  0.6 16.1 %shard_map.86 = (f32[17,16,256]{2,1,0:T(8,128)}, f32[17,16,256]{2,1,0:T(8,128)}, f32[15,8,256]{2,1,0:T(8,128)}, f32[15,8,256]{2,1,0:T(8,128)}, f32[8,16384]{1,0:...) custom-call(f32[17,8,16,256]{3,2,1,0:T(8,128)} %cells_hbm.5, f32[8,16384]{1,0:T(8,128)} %parcels_hbm.1, ...), custom_call_target="tpu_custom_call" | custom-call | flops 2147483648 | bytes 6291456 | tf_op jit(solution)/shard_map/pallas_call | solution.py:26
  16.8 3.0 %collective-permute-start.2 = (f32[17,16,256]{2,1,0:T(8,128)}, f32[17,16,256]{2,1,0:T(8,128)S(1)}, u32[]{:S(2)}, u32[]{:S(2)}) collective-permute-start(f32[17,16,256]{2,1,0:T(8,128)} %get-tuple-element.11), channel_id=1, source_target_pairs={{0,4},{4,8},{8,12},{12,16},{16,20},{20,24},{24,28},{28,0},{1,5},{5... | collective-permute-start | bytes 835592 | tf_op jit(solution)/shard_map/ppermute | solution.py:613
  19.8 3.1 %collective-permute-start.3 = (f32[17,16,256]{2,1,0:T(8,128)}, f32[17,16,256]{2,1,0:T(8,128)S(1)}, u32[]{:S(2)}, u32[]{:S(2)}) collective-permute-start(f32[17,16,256]{2,1,0:T(8,128)} %get-tuple-element.12), channel_id=1, source_target_pairs={{4,0},{8,4},{12,8},{16,12},{20,16},{24,20},{28,24},{0,28},{5,1},{9... | collective-permute-start | bytes 835592 | tf_op jit(solution)/shard_map/ppermute | solution.py:614
  22.9 3.3 %all-to-all-start = ((f32[32,1,1152]{2,1,0:T(1,128)}), f32[32,1,1152]{2,1,0:T(1,128)S(1)}, u32[]{:S(2)}, u32[]{:S(2)}) async-start(f32[32,1,1152]{2,1,0:T(1,128)} %bitcast.5), calls=%async_computation | async-start | bytes 294912 | tf_op jit(solution)/shard_map/all_to_all | solution.py:620
  26.2 0.3 collective-permute-start
  26.5 1.5 %collective-permute-start.1 = (f32[15,8,256]{2,1,0:T(8,128)}, f32[15,8,256]{2,1,0:T(8,128)S(1)}, u32[]{:S(2)}, u32[]{:S(2)}) collective-permute-start(f32[15,8,256]{2,1,0:T(8,128)} %get-tuple-element.10), channel_id=1, source_target_pairs={{1,0},{2,1},{3,2},{0,3},{5,4},{6,5},{7,6},{4,7},{9,8},{10,9},{11,1... | collective-permute-start | bytes 368648 | tf_op jit(solution)/shard_map/ppermute | solution.py:616
  28.0 3.5 %collective-permute-done.low_hbm = f32[15,8,256]{2,1,0:T(8,128)S(1)} collective-permute-done((f32[15,8,256]{2,1,0:T(8,128)}, f32[15,8,256]{2,1,0:T(8,128)S(1)}, u32[]{:S(2)}, u32[]{:S(2)}) %collective-permute-start) | collective-permute-done | bytes 122912 | tf_op jit(solution)/shard_map/ppermute | solution.py:615
  31.4 1.0 %collective-permute-done.1.high_hbm = f32[15,8,256]{2,1,0:T(8,128)S(1)} collective-permute-done((f32[15,8,256]{2,1,0:T(8,128)}, f32[15,8,256]{2,1,0:T(8,128)S(1)}, u32[]{:S(2)}, u32[]{:S(2)}) %collective-permute-start.1) | collective-permute-done | bytes 122912 | tf_op jit(solution)/shard_map/ppermute | solution.py:616
  32.4 0.0 copy-done.2
  32.4 0.0 copy-start
  32.4 1.6 %copy-done = f32[17,8,16,256]{3,2,1,0:T(8,128)S(1)} copy-done((f32[17,8,16,256]{3,2,1,0:T(8,128)S(1)}, f32[17,8,16,256]{3,2,1,0:T(8,128)}, u32[]{:S(2)}) %copy-start) | copy-done | bytes 2228248
  34.1 0.0 copy-start.3
  34.1 3.3 %shard_map.87.inner_hbm = f32[14,8,16,256]{3,2,1,0:T(8,128)} custom-call(f32[17,8,16,256]{3,2,1,0:T(8,128)S(1)} %copy-done, f32[15,8,256]{2,1,0:T(8,128)S(1)} %collective-permute-done.low_hbm, f32[15,8,256]{2,1,0:T(8,128)S(1)} %collective-permute-done.1.high_hbm, f32[8]{0:T(128)S(1)} %copy-done.2), custom_call_target="tpu_custom_call" | custom-call | flops 20971520 | bytes 4194304 | tf_op jit(solution)/shard_map/pallas_call | solution.py:26
  37.4 0.0 collective-permute-done.2.before_hbm
  37.4 0.0 collective-permute-done.3.after_hbm
  37.4 0.0 copy-done.3
  37.4 0.0 copy-done.4
  37.4 0.0 copy-done.5
  37.4 0.0 copy-start.1
  37.5 4.1 %shard_map.89 = f32[8,16384]{1,0:T(8,128)} custom-call(f32[8,16384]{1,0:T(8,128)S(1)} %copy-done.5, bf16[256,2048]{1,0:T(8,128)(2,1)S(1)} %copy-done.4, s32[2,1024]{1,0:T(2,128)S(1)} %copy-done.3, f32[17,16,256]{2,1,0:T(8,128)S(1)} %collective-permute-done.2.before_hbm, f32[17,16,256]{2,1,0:T(8,128)S(1)} %collective-permute-done.3.after_hbm), custom_call_target="tpu_custom_call" | custom-call | flops 1073741824 | bytes 3145728 | tf_op jit(solution)/shard_map/pallas_call | solution.py:26
  41.5 0.0 all-to-all-done
  41.6 0.0 copy-done.1
  41.6 13.5 %shard_map.88 = f32[14,8,16,256]{3,2,1,0:T(8,128)} custom-call(f32[17,8,16,256]{3,2,1,0:T(8,128)S(1)} %copy-done.1, f32[14,8,16,256]{3,2,1,0:T(8,128)} %shard_map.87.inner_hbm, f32[17,16,256]{2,1,0:T(8,128)S(1)} %collective-permute-done.2.before_hbm, f32[17,16,256]{2,1,0:T(8,128)S(1)} %collective-permute-done.3.after_hbm, ...), custom_call_target="tpu_custom_call", output_to_operand_aliasing={{}: (1, {})} | custom-call | flops 4294967296 | bytes 6291456 | tf_op jit(solution)/shard_map/pallas_call | solution.py:26
  (2 shorter events, 0.0 us)
Async XLA Ops:
  0.6 31.8 %copy-start.2 = (f32[8]{0:T(128)S(1)}, f32[8]{0:T(128)}, u32[]{:S(2)}) copy-start(f32[8]{0:T(128)} %rate_ref.3) | copy-start | bytes 100
  16.8 20.6 %collective-permute-start.2 = (f32[17,16,256]{2,1,0:T(8,128)}, f32[17,16,256]{2,1,0:T(8,128)S(1)}, u32[]{:S(2)}, u32[]{:S(2)}) collective-permute-start(f32[17,16,256]{2,1,0:T(8,128)} %get-tuple-element.11), channel_id=1, source_target_pairs={{0,4},{4,8},{8,12},{12,16},{16,20},{20,24},{24,28},{28,0},{1,5},{5... | collective-permute-start | bytes 835592 | tf_op jit(solution)/shard_map/ppermute | solution.py:613
  19.8 17.6 %collective-permute-start.3 = (f32[17,16,256]{2,1,0:T(8,128)}, f32[17,16,256]{2,1,0:T(8,128)S(1)}, u32[]{:S(2)}, u32[]{:S(2)}) collective-permute-start(f32[17,16,256]{2,1,0:T(8,128)} %get-tuple-element.12), channel_id=1, source_target_pairs={{4,0},{8,4},{12,8},{16,12},{20,16},{24,20},{28,24},{0,28},{5,1},{9... | collective-permute-start | bytes 835592 | tf_op jit(solution)/shard_map/ppermute | solution.py:614
  22.9 18.6 %all-to-all-start = ((f32[32,1,1152]{2,1,0:T(1,128)}), f32[32,1,1152]{2,1,0:T(1,128)S(1)}, u32[]{:S(2)}, u32[]{:S(2)}) async-start(f32[32,1,1152]{2,1,0:T(1,128)} %bitcast.5), calls=%async_computation | async-start | bytes 294912 | tf_op jit(solution)/shard_map/all_to_all | solution.py:620
  26.2 5.3 %collective-permute-start = (f32[15,8,256]{2,1,0:T(8,128)}, f32[15,8,256]{2,1,0:T(8,128)S(1)}, u32[]{:S(2)}, u32[]{:S(2)}) collective-permute-start(f32[15,8,256]{2,1,0:T(8,128)} %get-tuple-element.9), channel_id=1, source_target_pairs={{0,1},{1,2},{2,3},{3,0},{4,5},{5,6},{6,7},{7,4},{8,9},{9,10},{10,1... | collective-permute-start | bytes 368648 | tf_op jit(solution)/shard_map/ppermute | solution.py:615
  26.5 5.9 %collective-permute-start.1 = (f32[15,8,256]{2,1,0:T(8,128)}, f32[15,8,256]{2,1,0:T(8,128)S(1)}, u32[]{:S(2)}, u32[]{:S(2)}) collective-permute-start(f32[15,8,256]{2,1,0:T(8,128)} %get-tuple-element.10), channel_id=1, source_target_pairs={{1,0},{2,1},{3,2},{0,3},{5,4},{6,5},{7,6},{4,7},{9,8},{10,9},{11,1... | collective-permute-start | bytes 368648 | tf_op jit(solution)/shard_map/ppermute | solution.py:616
  32.4 1.6 %copy-start = (f32[17,8,16,256]{3,2,1,0:T(8,128)S(1)}, f32[17,8,16,256]{3,2,1,0:T(8,128)}, u32[]{:S(2)}) copy-start(f32[17,8,16,256]{3,2,1,0:T(8,128)} %cells_hbm.5) | copy-start | bytes 6684676
  34.1 3.4 %copy-start.3 = (s32[2,1024]{1,0:T(2,128)S(1)}, s32[2,1024]{1,0:T(2,128)}, u32[]{:S(2)}) copy-start(s32[2,1024]{1,0:T(2,128)} %crossing_hbm.3) | copy-start | bytes 24580
  34.1 3.4 %copy-start.4 = (bf16[256,2048]{1,0:T(8,128)(2,1)S(1)}, bf16[256,2048]{1,0:T(8,128)(2,1)}, u32[]{:S(2)}) copy-start(bf16[256,2048]{1,0:T(8,128)(2,1)} %get-tuple-element.15.hot_hbm) | copy-start | bytes 3145732
  34.1 3.4 %copy-start.5 = (f32[8,16384]{1,0:T(8,128)S(1)}, f32[8,16384]{1,0:T(8,128)}, u32[]{:S(2)}) copy-start(f32[8,16384]{1,0:T(8,128)} %get-tuple-element.14.advanced_hbm) | copy-start | bytes 1572868
  37.4 4.1 %copy-start.1 = (f32[17,8,16,256]{3,2,1,0:T(8,128)S(1)}, f32[17,8,16,256]{3,2,1,0:T(8,128)}, u32[]{:S(2)}) copy-start(f32[17,8,16,256]{3,2,1,0:T(8,128)} %cells_hbm.5) | copy-start | bytes 6684676

commit v4 on v3

--- a/solution.py
+++ b/solution.py
@@ -17,19 +17,19 @@
 BF16 = jnp.bfloat16
 ANY = pl.BlockSpec(memory_space=pl.ANY)
 SMEM = pl.BlockSpec(memory_space=pltpu.SMEM)
+VMEM = pl.BlockSpec(memory_space=pltpu.VMEM)
 ALL = 63 << 20
-MOST = 40 << 20
-
-
-def call(kernel, out_shape, operands, scratch, in_specs=None, aliases=None, flops=0, moved_bytes=0, grant=MOST):
+MOST = 32 << 20
+
+
+def call(kernel, out_shape, operands, scratch, in_specs=None, out_specs=ANY, flops=0, moved_bytes=0, grant=MOST):
     many = isinstance(out_shape, (list, tuple))
     return pl.pallas_call(
         kernel,
         out_shape=out_shape,
         in_specs=in_specs or [ANY] * len(operands),
-        out_specs=[ANY] * len(out_shape) if many else ANY,
+        out_specs=[out_specs] * len(out_shape) if many else out_specs,
         scratch_shapes=scratch,
-        input_output_aliases=aliases or {},
         compiler_params=pltpu.CompilerParams(vmem_limit_bytes=grant),
         cost_estimate=pl.CostEstimate(flops=flops, bytes_accessed=moved_bytes, transcendentals=0),
     )(*operands)
@@ -104,16 +104,16 @@
         carry = carry + part[:, LANES:]
         spot = owners[b : b + 1] * capacity + rank
         at = slice(b * LANES, (b + 1) * LANES)
-        hot_ref[:, at] = hot_columns(spot % WIDE, WIDE)
+        hot_ref[:, at] = hot_columns(spot & (WIDE - 1), WIDE)
         coarse, fine = split(mass_ref[:, at])
-        upper = spot // WIDE
+        upper = spot >> 8
         scatter_left(left_ref, at, upper, uppers, coarse, fine)
         hit = rows_of(upper.astype(F32), uppers) == packed(iota((uppers, LANES), 0))
         zero = jnp.zeros((uppers, LANES), BF16)
         cell = cells[b : b + 1]
-        left_ref[base : base + uppers, at] = jnp.where(hit, rows_of((cell // WIDE).astype(F32), uppers), zero)
+        left_ref[base : base + uppers, at] = jnp.where(hit, rows_of((cell >> 8).astype(F32), uppers), zero)
         left_ref[base + uppers : base + 2 * uppers, at] = jnp.where(
-            hit, rows_of((cell % WIDE).astype(F32), uppers), zero
+            hit, rows_of((cell & (WIDE - 1)).astype(F32), uppers), zero
         )
         left_ref[base + 2 * uppers : base + 3 * uppers, at] = jnp.where(hit, 1.0, 0.0).astype(BF16)
     placed = contract_lanes(left_ref[...], hot_ref[...])
@@ -146,8 +146,8 @@
         (mass_hbm, mass_ref),
         (parcels_hbm, parcels_ref),
         (cells_hbm, cells_ref),
-        (cells_hbm.at[face, size_x - 1], up_hbm.at[face]),
-        (cells_hbm.at[face, 0], down_hbm.at[face]),
+        (cells_ref.at[face, size_x - 1], up_hbm.at[face]),
+        (cells_ref.at[face, 0], down_hbm.at[face]),
         (filled_ref, filled_hbm),
         (hot_ref, hot_hbm),
         (advanced_ref, advanced_hbm),
@@ -157,19 +157,16 @@
         (ydown_ref, ydown_hbm),
     ]
     copies = [pltpu.make_async_copy(source, target, sems.at[i]) for i, (source, target) in enumerate(pairs)]
-    for copy in copies[:8]:
+    for copy in copies[:6]:
         copy.start()
     cross = crossing_ref.shape[1]
     slot_total = parcels_ref.shape[1]
-    for copy in copies[:4]:
-        copy.wait()
+    copies[0].wait()
     for side in range(2):
         for first in range(0, cross, LANES):
-            lower = crossing_ref[side : side + 1, first : first + LANES] % WIDE
+            lower = crossing_ref[side : side + 1, first : first + LANES] & (WIDE - 1)
             hot_ref[:, side * cross + first : side * cross + first + LANES] = hot_columns(lower, WIDE)
     copies[9].start()
-    bucket_into(owner_total, capacity, mass_ref, owner_ref, cell_ref, filled_ref, left_ref, spot_ref)
-    copies[8].start()
     copies[4].wait()
 
     def advance_pair(i, unused):
@@ -193,7 +190,7 @@
         coarse, fine = split(parts_ref[rows : rows + step_rows])
         for side in range(2):
             for first in range(0, cross, WIDE):
-                upper = jnp.broadcast_to(crossing_ref[side : side + 1, first : first + WIDE] // WIDE, (8, WIDE))
+                upper = jnp.broadcast_to(crossing_ref[side : side + 1, first : first + WIDE] >> 8, (8, WIDE))
                 hot = hot_ref[:, side * cross + first : side * cross + first + WIDE]
                 picked = jnp.dot(coarse, hot, preferred_element_type=F32) + jnp.dot(
                     fine, hot, preferred_element_type=F32
@@ -215,12 +212,18 @@
     copies[12].start()
 
     copies[5].wait()
+    copies[6].start()
+    copies[7].start()
     for c in range(COUNT + 1):
         source = c if c < COUNT else COUNT + 1
         yup_ref[c] = cells_ref[source, :, size_y - 1, :]
         ydown_ref[c] = cells_ref[source, :, 0, :]
     copies[13].start()
     copies[14].start()
+    for copy in copies[1:4]:
+        copy.wait()
+    bucket_into(owner_total, capacity, mass_ref, owner_ref, cell_ref, filled_ref, left_ref, spot_ref)
+    copies[8].start()
     for copy in copies[6:]:
         copy.wait()
 
@@ -252,41 +255,23 @@
     )
 
 
-def arrive_kernel(
-    advanced_hbm, hot_hbm, crossing_hbm, before_hbm, after_hbm, out_hbm,
-    advanced_ref, hot_ref, crossing_ref, come_ref, out_ref, left_ref, sems,
-):
+def arrive_kernel(advanced_ref, hot_ref, crossing_ref, before_ref, after_ref, out_hbm, out_ref, left_ref, sems):
     cross = crossing_ref.shape[1]
     uppers = advanced_ref.shape[1] // WIDE
-    tail = slice(COUNT + 1, before_hbm.shape[0])
-    pairs = [
-        (crossing_hbm, crossing_ref),
-        (before_hbm.at[tail], come_ref.at[0]),
-        (after_hbm.at[tail], come_ref.at[1]),
-        (hot_hbm, hot_ref),
-        (advanced_hbm, advanced_ref),
-    ]
-    copies = [pltpu.make_async_copy(source, target, sems.at[i]) for i, (source, target) in enumerate(pairs)]
-    for copy in copies:
-        copy.start()
-    for copy in copies[:3]:
-        copy.wait()
-    size_y, size_z = come_ref.shape[2:]
+    size_y, size_z = before_ref.shape[1:]
     halves_y, halves_z = size_y // 8, size_z // LANES
-    for side in range(2):
+    for side, come_ref in ((0, before_ref), (1, after_ref)):
         for first in range(0, cross, LANES):
             layer, rest = divmod(first // LANES, halves_y * halves_z)
             half_y, half_z = divmod(rest, halves_z)
-            block = come_ref[side, layer, 8 * half_y : 8 * half_y + 8, LANES * half_z : LANES * (half_z + 1)]
+            block = come_ref[COUNT + 1 + layer, 8 * half_y : 8 * half_y + 8, LANES * half_z : LANES * (half_z + 1)]
             coarse, fine = split(block)
-            upper = crossing_ref[side : side + 1, first : first + LANES] // WIDE
+            upper = crossing_ref[side : side + 1, first : first + LANES] >> 8
             at = slice(side * cross + first, side * cross + first + LANES)
             scatter_left(left_ref, at, upper, uppers, coarse, fine)
             hit = rows_of(upper.astype(F32), uppers) == packed(iota((uppers, LANES), 0))
             left_ref[16 * uppers :, at] = jnp.where(hit, 1.0, 0.0).astype(BF16)
-    copies[3].wait()
     hit = contract_lanes(left_ref[16 * uppers :], hot_ref[...])
-    copies[4].wait()
     step = min(32, uppers)
     outs = []
     for u in range(0, uppers, step):
@@ -298,7 +283,7 @@
             taken = jnp.broadcast_to(hit[u + i : u + i + 1], (8, WIDE)) > 0.5
             out_ref[:, at] = jnp.where(taken, total[8 * i : 8 * i + 8], advanced_ref[:, at])
         at = slice(u * WIDE, (u + step) * WIDE)
-        out = pltpu.make_async_copy(out_ref.at[:, at], out_hbm.at[:, at], sems.at[len(pairs) + len(outs)])
+        out = pltpu.make_async_copy(out_ref.at[:, at], out_hbm.at[:, at], sems.at[len(outs)])
         out.start()
         outs.append(out)
     for out in outs:
@@ -307,19 +292,14 @@
 
 def arrive(advanced, hot, crossing, before, after):
     uppers = advanced.shape[1] // WIDE
-    extra = before.shape[0] - COUNT - 1
     return call(
         arrive_kernel, jax.ShapeDtypeStruct(advanced.shape, F32), (advanced, hot, crossing, before, after),
         [
             pltpu.VMEM(advanced.shape, F32),
-            pltpu.VMEM(hot.shape, BF16),
-            pltpu.VMEM(crossing.shape, crossing.dtype),
-            pltpu.VMEM((2, extra) + before.shape[1:], F32),
-            pltpu.VMEM(advanced.shape, F32),
             pltpu.VMEM((17 * uppers, crossing.size), BF16),
-            pltpu.SemaphoreType.DMA((5 + -(-uppers // 32),)),
+            pltpu.SemaphoreType.DMA((-(-uppers // 32),)),
         ],
-        flops=1 << 30, moved_bytes=3 << 20,
+        in_specs=[VMEM] * 5, flops=1 << 30, moved_bytes=3 << 20,
     )
 
 
@@ -386,100 +366,60 @@
         write(c, moved(c))
 
 
-def inner_kernel(cells_hbm, low_hbm, high_hbm, rate_ref, out_hbm, cells_ref, low_ref, high_ref, out_ref, sems, out_sems):
-    size_x = cells_hbm.shape[1]
-    sides = [
-        pltpu.make_async_copy(low_hbm, low_ref, sems.at[size_x]),
-        pltpu.make_async_copy(high_hbm, high_ref, sems.at[size_x + 1]),
-    ]
-
-    def fetch(x):
-        return pltpu.make_async_copy(cells_hbm.at[:, x], cells_ref.at[:, x], sems.at[x])
+def cells_kernel(
+    cells_ref, before_ref, after_ref, low_ref, high_ref, deposit_ref, rate_ref, out_hbm, out_ref, sems
+):
+    size_x = cells_ref.shape[1]
+    last = size_x - 1
 
     def store(x):
-        return pltpu.make_async_copy(out_ref.at[:, x], out_hbm.at[:, x], out_sems.at[x])
-
-    for copy in sides:
-        copy.start()
-    for x in range(size_x):
-        fetch(x).start()
-    for copy in sides:
-        copy.wait()
-    fetch(0).wait()
-    fetch(1).wait()
-
-    def layer(x, unused):
-        fetch(x + 1).wait()
-
+        return pltpu.make_async_copy(out_ref.at[:, x], out_hbm.at[:, x], sems.at[x])
+
+    def layer(left, x, right):
         def write(c, value):
-            out_ref[c, x] = value
+            out_ref[c, x] = value + deposit_ref[c, x] if c < SECTIONS else value
 
         slab_update(
-            lambda c: cells_ref[c, x - 1],
+            left,
             lambda c: cells_ref[c, x],
-            lambda c: cells_ref[c, x + 1],
+            right,
             lambda c: low_ref[c, pl.ds(x, 1), :],
             lambda c: high_ref[c, pl.ds(x, 1), :],
             rate_ref,
             write,
         )
         store(x).start()
+
+    def middle(x, unused):
+        layer(lambda c: cells_ref[c, x - 1], x, lambda c: cells_ref[c, x + 1])
         return unused
 
-    lax.fori_loop(1, size_x - 1, layer, 0)
-    for x in range(1, size_x - 1):
+    lax.fori_loop(1, last, middle, 0)
+    layer(lambda c: before_ref[c], 0, lambda c: cells_ref[c, 1])
+    layer(lambda c: cells_ref[c, last - 1], last, lambda c: after_ref[c])
+    for x in range(size_x):
         store(x).wait()
 
 
-def inner(cells, low, high, rate):
-    size_x = cells.shape[1]
+def update_cells(cells, before, after, low, high, deposited, rate):
     out = jax.ShapeDtypeStruct((COUNT,) + cells.shape[1:], F32)
     return call(
-        inner_kernel, out, (cells, low, high, rate),
-        [pltpu.VMEM(a.shape, F32) for a in (cells, low, high, out)]
-        + [pltpu.SemaphoreType.DMA((size_x + 2,)), pltpu.SemaphoreType.DMA((size_x,))],
-        in_specs=[ANY, ANY, ANY, SMEM],
-        flops=20 << 20, moved_bytes=4 << 20,
-    )
-
-
-def put(ref, x, c, value):
-    ref[c, x] = value
-
-
-def final_kernel(
-    cells_hbm, inner_hbm, before_hbm, after_hbm, low_hbm, high_hbm, routed_hbm, rate_ref, out_hbm,
-    edge_ref, before_ref, after_ref, low_ref, high_ref, routed_ref, section_ref, species_ref,
-    mass_ref, place_ref, spread_ref, depth_ref, sems,
-):
-    size_x, size_y, size_z = cells_hbm.shape[1:]
-    last = size_x - 1
-    face = slice(0, COUNT + 1)
-    middle = slice(1, last)
-    sections = slice(0, SECTIONS)
-    others = slice(SECTIONS, COUNT)
-    pairs = [
-        (routed_hbm, routed_ref),
-        (low_hbm, low_ref),
-        (high_hbm, high_ref),
-        (before_hbm.at[face], before_ref),
-        (after_hbm.at[face], after_ref),
-        (cells_hbm.at[:, 0:2], edge_ref.at[:, 0:2]),
-        (cells_hbm.at[:, last - 1 : last + 1], edge_ref.at[:, 2:4]),
-        (inner_hbm.at[sections, middle], section_ref.at[:, middle]),
-        (species_ref.at[:, 0], out_hbm.at[others, 0]),
-        (species_ref.at[:, 1], out_hbm.at[others, last]),
-        (section_ref.at[:, 0:size_x], out_hbm.at[sections]),
-    ]
-    copies = [pltpu.make_async_copy(source, target, sems.at[i]) for i, (source, target) in enumerate(pairs)]
-    for copy in copies[:8]:
-        copy.start()
-
-    copies[0].wait()
+        cells_kernel, out, (cells, before, after, low, high, deposited, rate),
+        [pltpu.VMEM(out.shape, F32), pltpu.SemaphoreType.DMA((cells.shape[1],))],
+        in_specs=[VMEM] * 6 + [SMEM], flops=30 << 20, moved_bytes=4 << 20,
+    )
+
+
+def quotient(value, count):
+    return value >> (count.bit_length() - 1) if count & (count - 1) == 0 else value // count
+
+
+def deposit_kernel(shape, routed_ref, out_ref, total_ref, mass_ref, spread_ref, depth_ref):
+    size_x, size_y, size_z = shape
     groups = routed_ref.shape[0] // 9
     per = groups // 8
     span = LANES // per
-    lane = iota((8, LANES), 1)
+    lane_part = quotient(iota((8, LANES), 1), span)
     for v in range(9):
         rows = routed_ref[pl.ds(v, groups, stride=9), :]
         for q in range(per):
@@ -488,13 +428,13 @@
                 block = rows[8 * g : 8 * g + 8]
                 if g != q:
                     block = pltpu.roll(block, (span * (g - q)) % LANES, 1)
-                total = block if total is None else jnp.where(lane // span == g, block, total)
+                total = block if total is None else jnp.where(lane_part == g, block, total)
             mass_ref[q, v] = total
 
     bounds = []
     for q in range(per):
         cell = mass_ref[q, SECTIONS].astype(jnp.int32)
-        layer = cell // (size_y * size_z)
+        layer = quotient(cell, size_y * size_z)
         valid = cell >= 0
         bounds.append((jnp.min(jnp.where(valid, layer, size_x)), jnp.max(jnp.where(valid, layer, -1))))
 
@@ -503,8 +443,9 @@
 
     def spread(q, first):
         cell = mass_ref[q, SECTIONS].astype(jnp.int32)
-        plane = jnp.where(cell >= 0, cell // size_z - first * size_y, -1).astype(F32)
-        depth = cell % size_z
+        plane = quotient(cell, size_z)
+        depth = cell - plane * size_z
+        plane = jnp.where(cell >= 0, plane - first * size_y, -1).astype(F32)
         parts = [split(mass_ref[q, s]) for s in range(SECTIONS)]
         for i in range(8):
             at = slice(i * LANES, (i + 1) * LANES)
@@ -526,31 +467,11 @@
             base = s * WINDOW * size_y
             rows = added[base : base + WINDOW * size_y] + added[half + base : half + base + WINDOW * size_y]
             at = pl.ds(first, WINDOW)
-            section_ref[s, at] = section_ref[s, at] + rows.reshape(WINDOW, size_y, size_z)
-
-    for copy in copies[1:8]:
-        copy.wait()
-
-    def write(x, number, c, value):
-        if c < SECTIONS:
-            section_ref[c, x] = value
-        else:
-            species_ref[c - SECTIONS, number] = value
-
-    slab_update(
-        lambda c: before_ref[c], lambda c: edge_ref[c, 0], lambda c: edge_ref[c, 1],
-        lambda c: low_ref[c, 0:1, :], lambda c: high_ref[c, 0:1, :],
-        rate_ref, functools.partial(write, 0, 0),
-    )
-    slab_update(
-        lambda c: edge_ref[c, 2], lambda c: edge_ref[c, 3], lambda c: after_ref[c],
-        lambda c: low_ref[c, last : last + 1, :], lambda c: high_ref[c, last : last + 1, :],
-        rate_ref, functools.partial(write, last, 1),
-    )
-    copies[8].start()
-    copies[9].start()
+            total_ref[s, at] = total_ref[s, at] + rows.reshape(WINDOW, size_y, size_z)
+
+    total_ref[...] = jnp.zeros(total_ref.shape, F32)
     for q in range(per):
-        first = jnp.minimum(bounds[q][0], last)
+        first = jnp.minimum(bounds[q][0], size_x - 1)
         spread(q, first)
         deposit(q, first)
     for q in range(per):
@@ -562,35 +483,22 @@
             deposit(q, first)
             return unused
 
-        lax.fori_loop(1, (high - low + WINDOW) // WINDOW, more, 0)
-    copies[10].start()
-    for copy in copies[8:]:
-        copy.wait()
-
-
-def final(cells, inner_cells, before, after, low, high, routed, rate):
-    size_x, size_y, size_z = cells.shape[1:]
+        lax.fori_loop(1, quotient(high - low + WINDOW, WINDOW), more, 0)
+    out_ref[...] = total_ref[:, 0:size_x]
+
+
+def deposit(routed, shape):
+    size_x, size_y, size_z = shape
     per = routed.shape[0] // 9 // 8
     return call(
-        final_kernel, jax.ShapeDtypeStruct(inner_cells.shape, F32),
-        (cells, inner_cells, before, after, low, high, routed, rate),
+        functools.partial(deposit_kernel, shape), jax.ShapeDtypeStruct((SECTIONS,) + shape, F32), (routed,),
         [
-            pltpu.VMEM((cells.shape[0], 4, size_y, size_z), F32),
-            pltpu.VMEM((COUNT + 1, size_y, size_z), F32),
-            pltpu.VMEM((COUNT + 1, size_y, size_z), F32),
-            pltpu.VMEM(low.shape, F32),
-            pltpu.VMEM(high.shape, F32),
-            pltpu.VMEM(routed.shape, F32),
             pltpu.VMEM((SECTIONS, size_x + WINDOW - 1, size_y, size_z), F32),
-            pltpu.VMEM((SPECIES, 2, size_y, size_z), F32),
             pltpu.VMEM((per, SECTIONS + 1, 8, LANES), F32),
-            pltpu.VMEM((8, LANES), F32),
             pltpu.VMEM((2, 2 * SECTIONS * WINDOW * size_y, 8 * LANES), BF16),
             pltpu.VMEM((2, size_z, 8 * LANES), BF16),
-            pltpu.SemaphoreType.DMA((11,)),
         ],
-        in_specs=[ANY] * 7 + [SMEM], aliases={1: 0},
-        flops=4 << 30, moved_bytes=6 << 20,
+        in_specs=[VMEM], out_specs=VMEM, flops=4 << 30, moved_bytes=2 << 20,
     )
 
 
@@ -620,9 +528,9 @@
     routed = lax.all_to_all(filled, ("gx", "gy"), split_axis=0, concat_axis=0, tiled=True)
     routed = routed.reshape(-1, fold, 9, capacity).transpose(0, 2, 1, 3).reshape(-1, LANES)
 
-    inner_cells = inner(cell_state, low, high, evap_rate)
+    deposited = deposit(routed, cell_state.shape[1:])
     new_parcels = arrive(advanced, hot, crossing, before, after)
-    new_cells = final(cell_state, inner_cells, before, after, low, high, routed, evap_rate)
+    new_cells = update_cells(cell_state, before, after, low, high, deposited, evap_rate)
     return (new_cells, new_parcels)
 
 

time: 55.3 us -> 40.9 us (0.74)
  Pallas kernels: 37.1 us -> 18.8 us
  waiting for transfers between devices: 4.45 us -> 7.62 us
  local copies, waits for them, and re-layouts: 1.65 us -> 2.28 us
    pallas_call x4, Pallas kernels: 37.1 us -> 18.8 us  [call(): pl.pallas_call(kernel, out_shape=out_shape, in_specs=in_specs or [ANY] *...]
    ppermute x1, waiting for transfers between devices: 0.01 us -> 5.55 us  [on_device(): before = lax.ppermute(send_up, 'gx', up_x)]
    ppermute x1, waiting for transfers between devices: 3.46 us -> 0.01 us  [on_device(): low = lax.ppermute(side_up, 'gy', up_y)]
    ppermute x1, waiting for transfers between devices: 0.01 us -> 2.06 us  [on_device(): after = lax.ppermute(send_down, 'gx', down_x)]
    ppermute x1, waiting for transfers between devices: 0.98 us -> 0.01 us  [on_device(): high = lax.ppermute(side_down, 'gy', down_y)]
    unnamed x12 -> x10, local copies, waits for them, and re-layouts: 1.65 us -> 2.28 us
  transfers between devices with their start and end apart: 5 -> 5, of which waited for: 2 -> 2; matrix products, arithmetic and copies ran while one was open for 0% -> 0% of each run, Pallas kernels for 13% -> 25%
where the time goes in v4:
time: 40.9 us; the launch traced here: 40.6 us
  Pallas kernels  18.8 us (46%)
  starting transfers between devices  11.2 us (27%)
  waiting for transfers between devices  7.62 us (19%)
  local copies, waits for them, and re-layouts  2.28 us (6%)
  between operations  0.73 us (2%)
    pallas_call x4, Pallas kernels, call(): pl.pallas_call(kernel, out_shape=out_shape, in_specs=in_specs or [ANY] *...  18.8 us
    ppermute x1, waiting for transfers between devices, on_device(): before = lax.ppermute(send_up, 'gx', up_x)  5.55 us
    all_to_all x1, starting transfers between devices, on_device(): lax.all_to_all(filled, ('gx', 'gy'), split_axis=0, concat_axis=0, tiled=T...  3.26 us
    ppermute x1, starting transfers between devices, on_device(): after = lax.ppermute(send_down, 'gx', down_x)  3.1 us
    ppermute x1, starting transfers between devices, on_device(): before = lax.ppermute(send_up, 'gx', up_x)  3.02 us
    unnamed x10, local copies, waits for them, and re-layouts  2.28 us
    ppermute x1, waiting for transfers between devices, on_device(): after = lax.ppermute(send_down, 'gx', down_x)  2.06 us
    ppermute x1, starting transfers between devices, on_device(): high = lax.ppermute(side_down, 'gy', down_y)  1.49 us
  transfers between devices with their start and end apart: 5, of which 2 were waited for; matrix products, arithmetic and copies ran while one was open for 0% of the time, Pallas kernels for 25%

profile of v4, /device:TPU:0, one launch (start us, length us, event | category | flops | bytes accessed | tf_op | source)
XLA Modules:
  0.0 40.6 jit_solution(17316336339840837929)
XLA Ops:
  0.6 0.0 copy-start.2
  0.6 5.4 %shard_map.86 = (f32[17,16,256]{2,1,0:T(8,128)}, f32[17,16,256]{2,1,0:T(8,128)}, f32[15,8,256]{2,1,0:T(8,128)}, f32[15,8,256]{2,1,0:T(8,128)}, f32[8,16384]{1,0:...) custom-call(f32[17,8,16,256]{3,2,1,0:T(8,128)} %cells_ref.1, f32[8,16384]{1,0:T(8,128)} %parcels_hbm.1, ...), custom_call_target="tpu_custom_call" | custom-call | flops 2147483648 | bytes 6291456 | tf_op jit(solution)/shard_map/pallas_call | solution.py:27
  6.1 3.0 %collective-permute-start = (f32[17,16,256]{2,1,0:T(8,128)}, f32[17,16,256]{2,1,0:T(8,128)S(1)}, u32[]{:S(2)}, u32[]{:S(2)}) collective-permute-start(f32[17,16,256]{2,1,0:T(8,128)} %get-tuple-element.9), channel_id=1, source_target_pairs={{0,4},{4,8},{8,12},{12,16},{16,20},{20,24},{24,28},{28,0},{1,5},{5... | collective-permute-start | bytes 835592 | tf_op jit(solution)/shard_map/ppermute | solution.py:521
  9.1 3.1 %collective-permute-start.1 = (f32[17,16,256]{2,1,0:T(8,128)}, f32[17,16,256]{2,1,0:T(8,128)S(1)}, u32[]{:S(2)}, u32[]{:S(2)}) collective-permute-start(f32[17,16,256]{2,1,0:T(8,128)} %get-tuple-element.10), channel_id=1, source_target_pairs={{4,0},{8,4},{12,8},{16,12},{20,16},{24,20},{28,24},{0,28},{5,1},{9... | collective-permute-start | bytes 835592 | tf_op jit(solution)/shard_map/ppermute | solution.py:522
  12.2 3.3 %all-to-all-start = ((f32[32,1,1152]{2,1,0:T(1,128)}), f32[32,1,1152]{2,1,0:T(1,128)S(1)}, u32[]{:S(2)}, u32[]{:S(2)}) async-start(f32[32,1,1152]{2,1,0:T(1,128)} %bitcast.5), calls=%async_computation | async-start | bytes 294912 | tf_op jit(solution)/shard_map/all_to_all | solution.py:528
  15.5 0.3 collective-permute-start.2
  15.8 1.5 %collective-permute-start.3 = (f32[15,8,256]{2,1,0:T(8,128)}, f32[15,8,256]{2,1,0:T(8,128)S(1)}, u32[]{:S(2)}, u32[]{:S(2)}) collective-permute-start(f32[15,8,256]{2,1,0:T(8,128)} %get-tuple-element.12), channel_id=1, source_target_pairs={{1,0},{2,1},{3,2},{0,3},{5,4},{6,5},{7,6},{4,7},{9,8},{10,9},{11,1... | collective-permute-start | bytes 368648 | tf_op jit(solution)/shard_map/ppermute | solution.py:524
  17.3 5.6 %collective-permute-done.before_ref = f32[17,16,256]{2,1,0:T(8,128)S(1)} collective-permute-done((f32[17,16,256]{2,1,0:T(8,128)}, f32[17,16,256]{2,1,0:T(8,128)S(1)}, u32[]{:S(2)}, u32[]{:S(2)}) %collective-permute-start) | collective-permute-done | bytes 278560 | tf_op jit(solution)/shard_map/ppermute | solution.py:521
  22.8 2.1 %collective-permute-done.1.after_ref = f32[17,16,256]{2,1,0:T(8,128)S(1)} collective-permute-done((f32[17,16,256]{2,1,0:T(8,128)}, f32[17,16,256]{2,1,0:T(8,128)S(1)}, u32[]{:S(2)}, u32[]{:S(2)}) %collective-permute-start.1) | collective-permute-done | bytes 278560 | tf_op jit(solution)/shard_map/ppermute | solution.py:522
  24.9 0.0 copy-done.2
  24.9 0.0 copy-start.3
  24.9 1.2 %copy-done.3 = bf16[256,2048]{1,0:T(8,128)(2,1)S(1)} copy-done((bf16[256,2048]{1,0:T(8,128)(2,1)S(1)}, bf16[256,2048]{1,0:T(8,128)(2,1)}, u32[]{:S(2)}) %copy-start.3) | copy-done | bytes 1048600
  26.1 0.0 copy-start.4
  26.1 1.0 %copy-done.4 = f32[8,16384]{1,0:T(8,128)S(1)} copy-done((f32[8,16384]{1,0:T(8,128)S(1)}, f32[8,16384]{1,0:T(8,128)}, u32[]{:S(2)}) %copy-start.4) | copy-done | bytes 524312
  27.2 2.5 %shard_map.89 = f32[8,16384]{1,0:T(8,128)} custom-call(f32[8,16384]{1,0:T(8,128)S(1)} %copy-done.4, bf16[256,2048]{1,0:T(8,128)(2,1)S(1)} %copy-done.3, s32[2,1024]{1,0:T(2,128)S(1)} %copy-done.2, f32[17,16,256]{2,1,0:T(8,128)S(1)} %collective-permute-done.before_ref, f32[17,16,256]{2,1,0:T(8,128)S(1)} %collective-permute-done.1.after_ref), custom_call_target="tpu_custom_call" | custom-call | flops 1073741824 | bytes 3145728 | tf_op jit(solution)/shard_map/pallas_call | solution.py:27
  29.6 0.0 all-to-all-done
  29.7 0.0 copy-start
  29.7 0.0 copy-start.1
  29.7 7.5 %shard_map.87.deposit_ref = f32[8,8,16,256]{3,2,1,0:T(8,128)S(1)} custom-call(f32[288,128]{1,0:T(8,128)S(1)} %bitcast.4), custom_call_target="tpu_custom_call" | custom-call | flops 4294967296 | bytes 2097152 | tf_op jit(solution)/shard_map/pallas_call | solution.py:27
  37.2 0.0 collective-permute-done.2.low_ref
  37.2 0.0 collective-permute-done.3.high_ref
  37.2 0.0 copy-done
  37.3 0.0 copy-done.1
  37.3 3.4 %shard_map.88 = f32[14,8,16,256]{3,2,1,0:T(8,128)} custom-call(f32[17,8,16,256]{3,2,1,0:T(8,128)S(1)} %copy-done, f32[17,16,256]{2,1,0:T(8,128)S(1)} %collective-permute-done.before_ref, f32[17,16,256]{2,1,0:T(8,128)S(1)} %collective-permute-done.1.after_ref, f32[15,8,256]{2,1,0:T(8,128)S(1)} %collective-permute-done.2.low_ref, ...), custom_call_target="tpu_custom_call" | custom-call | flops 31457280 | bytes 4194304 | tf_op jit(solution)/shard_map/pallas_call | solution.py:27
Async XLA Ops:
  0.6 24.3 %copy-start.2 = (s32[2,1024]{1,0:T(2,128)S(1)}, s32[2,1024]{1,0:T(2,128)}, u32[]{:S(2)}) copy-start(s32[2,1024]{1,0:T(2,128)} %crossing_ref.1) | copy-start | bytes 24580
  6.1 16.7 %collective-permute-start = (f32[17,16,256]{2,1,0:T(8,128)}, f32[17,16,256]{2,1,0:T(8,128)S(1)}, u32[]{:S(2)}, u32[]{:S(2)}) collective-permute-start(f32[17,16,256]{2,1,0:T(8,128)} %get-tuple-element.9), channel_id=1, source_target_pairs={{0,4},{4,8},{8,12},{12,16},{16,20},{20,24},{24,28},{28,0},{1,5},{5... | collective-permute-start | bytes 835592 | tf_op jit(solution)/shard_map/ppermute | solution.py:521
  9.1 15.8 %collective-permute-start.1 = (f32[17,16,256]{2,1,0:T(8,128)}, f32[17,16,256]{2,1,0:T(8,128)S(1)}, u32[]{:S(2)}, u32[]{:S(2)}) collective-permute-start(f32[17,16,256]{2,1,0:T(8,128)} %get-tuple-element.10), channel_id=1, source_target_pairs={{4,0},{8,4},{12,8},{16,12},{20,16},{24,20},{28,24},{0,28},{5,1},{9... | collective-permute-start | bytes 835592 | tf_op jit(solution)/shard_map/ppermute | solution.py:522
  12.2 17.4 %all-to-all-start = ((f32[32,1,1152]{2,1,0:T(1,128)}), f32[32,1,1152]{2,1,0:T(1,128)S(1)}, u32[]{:S(2)}, u32[]{:S(2)}) async-start(f32[32,1,1152]{2,1,0:T(1,128)} %bitcast.5), calls=%async_computation | async-start | bytes 294912 | tf_op jit(solution)/shard_map/all_to_all | solution.py:528
  15.5 21.7 %collective-permute-start.2 = (f32[15,8,256]{2,1,0:T(8,128)}, f32[15,8,256]{2,1,0:T(8,128)S(1)}, u32[]{:S(2)}, u32[]{:S(2)}) collective-permute-start(f32[15,8,256]{2,1,0:T(8,128)} %get-tuple-element.11), channel_id=1, source_target_pairs={{0,1},{1,2},{2,3},{3,0},{4,5},{5,6},{6,7},{7,4},{8,9},{9,10},{10,1... | collective-permute-start | bytes 368648 | tf_op jit(solution)/shard_map/ppermute | solution.py:523
  15.8 21.5 %collective-permute-start.3 = (f32[15,8,256]{2,1,0:T(8,128)}, f32[15,8,256]{2,1,0:T(8,128)S(1)}, u32[]{:S(2)}, u32[]{:S(2)}) collective-permute-start(f32[15,8,256]{2,1,0:T(8,128)} %get-tuple-element.12), channel_id=1, source_target_pairs={{1,0},{2,1},{3,2},{0,3},{5,4},{6,5},{7,6},{4,7},{9,8},{10,9},{11,1... | collective-permute-start | bytes 368648 | tf_op jit(solution)/shard_map/ppermute | solution.py:524
  24.9 1.2 %copy-start.3 = (bf16[256,2048]{1,0:T(8,128)(2,1)S(1)}, bf16[256,2048]{1,0:T(8,128)(2,1)}, u32[]{:S(2)}) copy-start(bf16[256,2048]{1,0:T(8,128)(2,1)} %get-tuple-element.15.hot_ref) | copy-start | bytes 3145732
  26.1 1.0 %copy-start.4 = (f32[8,16384]{1,0:T(8,128)S(1)}, f32[8,16384]{1,0:T(8,128)}, u32[]{:S(2)}) copy-start(f32[8,16384]{1,0:T(8,128)} %get-tuple-element.14.advanced_ref) | copy-start | bytes 1572868
  29.7 7.6 %copy-start = (f32[17,8,16,256]{3,2,1,0:T(8,128)S(1)}, f32[17,8,16,256]{3,2,1,0:T(8,128)}, u32[]{:S(2)}) copy-start(f32[17,8,16,256]{3,2,1,0:T(8,128)} %cells_ref.1) | copy-start | bytes 6684676
  29.7 7.6 %copy-start.1 = (f32[8]{0:T(128)S(1)}, f32[8]{0:T(128)}, u32[]{:S(2)}) copy-start(f32[8]{0:T(128)} %rate_ref.1) | copy-start | bytes 100

commit v5 on v4

--- a/solution.py
+++ b/solution.py
@@ -255,7 +255,7 @@
     )
 
 
-def arrive_kernel(advanced_ref, hot_ref, crossing_ref, before_ref, after_ref, out_hbm, out_ref, left_ref, sems):
+def arrive_kernel(unused, advanced_ref, hot_ref, crossing_ref, before_ref, after_ref, out_hbm, out_ref, left_ref, sems):
     cross = crossing_ref.shape[1]
     uppers = advanced_ref.shape[1] // WIDE
     size_y, size_z = before_ref.shape[1:]
@@ -290,16 +290,16 @@
         out.wait()
 
 
-def arrive(advanced, hot, crossing, before, after):
+def arrive(earlier, advanced, hot, crossing, before, after):
     uppers = advanced.shape[1] // WIDE
     return call(
-        arrive_kernel, jax.ShapeDtypeStruct(advanced.shape, F32), (advanced, hot, crossing, before, after),
+        arrive_kernel, jax.ShapeDtypeStruct(advanced.shape, F32), (earlier, advanced, hot, crossing, before, after),
         [
             pltpu.VMEM(advanced.shape, F32),
             pltpu.VMEM((17 * uppers, crossing.size), BF16),
             pltpu.SemaphoreType.DMA((-(-uppers // 32),)),
         ],
-        in_specs=[VMEM] * 5, flops=1 << 30, moved_bytes=3 << 20,
+        in_specs=[ANY] + [VMEM] * 5, flops=1 << 30, moved_bytes=3 << 20,
     )
 
 
@@ -529,7 +529,7 @@
     routed = routed.reshape(-1, fold, 9, capacity).transpose(0, 2, 1, 3).reshape(-1, LANES)
 
     deposited = deposit(routed, cell_state.shape[1:])
-    new_parcels = arrive(advanced, hot, crossing, before, after)
+    new_parcels = arrive(deposited, advanced, hot, crossing, before, after)
     new_cells = update_cells(cell_state, before, after, low, high, deposited, evap_rate)
     return (new_cells, new_parcels)
 

time: 40.9 us -> 38.2 us (0.934)
  waiting for transfers between devices: 7.62 us -> 3.2 us
  starting transfers between devices: 11.2 us -> 13.8 us
  local copies, waits for them, and re-layouts: 2.28 us -> 0.02 us
  Pallas kernels: 18.8 us -> 20 us
    ppermute x1, waiting for transfers between devices: 5.55 us -> 0.01 us  [on_device(): before = lax.ppermute(send_up, 'gx', up_x)]
    all_to_all x1, starting transfers between devices: 3.26 us -> 7.3 us  [on_device(): lax.all_to_all(filled, ('gx', 'gy'), split_axis=0, concat_axis=0, tiled=T...]
    unnamed x10, local copies, waits for them, and re-layouts: 2.28 us -> 0.02 us
    all_to_all x1, waiting for transfers between devices: 0.01 us -> 1.9 us  [on_device(): lax.all_to_all(filled, ('gx', 'gy'), split_axis=0, concat_axis=0, tiled=T...]
    ppermute x1, starting transfers between devices: 3.02 us -> 1.77 us  [on_device(): before = lax.ppermute(send_up, 'gx', up_x)]
    pallas_call x4, Pallas kernels: 18.8 us -> 20 us  [call(): pl.pallas_call(kernel, out_shape=out_shape, in_specs=in_specs or [ANY] *...]
    ppermute x1, waiting for transfers between devices: 2.06 us -> 1.29 us  [on_device(): after = lax.ppermute(send_down, 'gx', down_x)]
  transfers between devices with their start and end apart: 5 -> 5, of which waited for: 2 -> 2; matrix products, arithmetic and copies ran while one was open for 0% -> 0% of each run, Pallas kernels for 25% -> 30%
where the time goes in v5:
time: 38.2 us; the launch traced here: 37.9 us
  Pallas kernels  20 us (52%)
  starting transfers between devices  13.8 us (36%)
  waiting for transfers between devices  3.2 us (8%)
  between operations  0.89 us (2%)
    pallas_call x4, Pallas kernels, call(): pl.pallas_call(kernel, out_shape=out_shape, in_specs=in_specs or [ANY] *...  20 us
    all_to_all x1, starting transfers between devices, on_device(): lax.all_to_all(filled, ('gx', 'gy'), split_axis=0, concat_axis=0, tiled=T...  7.3 us
    ppermute x1, starting transfers between devices, on_device(): after = lax.ppermute(send_down, 'gx', down_x)  2.95 us
    all_to_all x1, waiting for transfers between devices, on_device(): lax.all_to_all(filled, ('gx', 'gy'), split_axis=0, concat_axis=0, tiled=T...  1.9 us
    ppermute x1, starting transfers between devices, on_device(): before = lax.ppermute(send_up, 'gx', up_x)  1.77 us
    ppermute x1, starting transfers between devices, on_device(): high = lax.ppermute(side_down, 'gy', down_y)  1.49 us
    ppermute x1, waiting for transfers between devices, on_device(): after = lax.ppermute(send_down, 'gx', down_x)  1.29 us
  transfers between devices with their start and end apart: 5, of which 2 were waited for; matrix products, arithmetic and copies ran while one was open for 0% of the time, Pallas kernels for 30%

profile of v5, /device:TPU:0, one launch (start us, length us, event | category | flops | bytes accessed | tf_op | source)
XLA Modules:
  0.0 37.9 jit_solution(2280014827328058269)
XLA Ops:
  0.6 5.4 %shard_map.86 = (f32[17,16,256]{2,1,0:T(8,128)}, f32[17,16,256]{2,1,0:T(8,128)}, f32[15,8,256]{2,1,0:T(8,128)}, f32[15,8,256]{2,1,0:T(8,128)}, f32[8,16384]{1,0:...) custom-call(f32[17,8,16,256]{3,2,1,0:T(8,128)} %cells_ref.1, f32[8,16384]{1,0:T(8,128)} %parcels_hbm.1, ...), custom_call_target="tpu_custom_call" | custom-call | flops 2147483648 | bytes 6291456 | tf_op jit(solution)/shard_map/pallas_call | solution.py:27
  6.0 7.3 %all-to-all-start = ((f32[32,1,1152]{2,1,0:T(1,128)}), f32[32,1,1152]{2,1,0:T(1,128)S(1)}, u32[]{:S(2)}, u32[]{:S(2)}) async-start(f32[32,1,1152]{2,1,0:T(1,128)} %bitcast.5), calls=%async_computation | async-start | bytes 294912 | tf_op jit(solution)/shard_map/all_to_all | solution.py:528
  13.3 0.3 collective-permute-start.2
  13.6 1.5 %collective-permute-start.3 = (f32[15,8,256]{2,1,0:T(8,128)}, f32[15,8,256]{2,1,0:T(8,128)S(1)}, u32[]{:S(2)}, u32[]{:S(2)}) collective-permute-start(f32[15,8,256]{2,1,0:T(8,128)} %get-tuple-element.12), channel_id=1, source_target_pairs={{1,0},{2,1},{3,2},{0,3},{5,4},{6,5},{7,6},{4,7},{9,8},{10,9},{11,1... | collective-permute-start | bytes 368648 | tf_op jit(solution)/shard_map/ppermute | solution.py:524
  15.1 1.8 %collective-permute-start = (f32[17,16,256]{2,1,0:T(8,128)}, f32[17,16,256]{2,1,0:T(8,128)S(1)}, u32[]{:S(2)}, u32[]{:S(2)}) collective-permute-start(f32[17,16,256]{2,1,0:T(8,128)} %get-tuple-element.9), channel_id=1, source_target_pairs={{0,4},{4,8},{8,12},{12,16},{16,20},{20,24},{24,28},{28,0},{1,5},{5... | collective-permute-start | bytes 835592 | tf_op jit(solution)/shard_map/ppermute | solution.py:521
  16.9 3.0 %collective-permute-start.1 = (f32[17,16,256]{2,1,0:T(8,128)}, f32[17,16,256]{2,1,0:T(8,128)S(1)}, u32[]{:S(2)}, u32[]{:S(2)}) collective-permute-start(f32[17,16,256]{2,1,0:T(8,128)} %get-tuple-element.10), channel_id=1, source_target_pairs={{4,0},{8,4},{12,8},{16,12},{20,16},{24,20},{28,24},{0,28},{5,1},{9... | collective-permute-start | bytes 835592 | tf_op jit(solution)/shard_map/ppermute | solution.py:522
  19.9 1.9 %all-to-all-done = f32[32,1,1152]{2,1,0:T(1,128)S(1)} async-done(((f32[32,1,1152]{2,1,0:T(1,128)}), f32[32,1,1152]{2,1,0:T(1,128)S(1)}, u32[]{:S(2)}, u32[]{:S(2)}) %all-to-all-start) | async-done | bytes 147488 | tf_op jit(solution)/shard_map/all_to_all | solution.py:528
  21.8 0.0 copy-start.2
  21.8 0.0 copy-start.3
  21.8 0.0 copy-start.4
  21.8 8.7 %shard_map.87.deposit_ref.unused = f32[8,8,16,256]{3,2,1,0:T(8,128)S(1)} custom-call(f32[288,128]{1,0:T(8,128)S(1)} %bitcast.4), custom_call_target="tpu_custom_call" | custom-call | flops 4294967296 | bytes 2097152 | tf_op jit(solution)/shard_map/pallas_call | solution.py:27
  30.5 0.0 copy-start
  30.5 0.0 copy-start.1
  30.5 0.0 collective-permute-done.before_ref
  30.6 1.3 %collective-permute-done.1.after_ref = f32[17,16,256]{2,1,0:T(8,128)S(1)} collective-permute-done((f32[17,16,256]{2,1,0:T(8,128)}, f32[17,16,256]{2,1,0:T(8,128)S(1)}, u32[]{:S(2)}, u32[]{:S(2)}) %collective-permute-start.1) | collective-permute-done | bytes 278560 | tf_op jit(solution)/shard_map/ppermute | solution.py:522
  31.8 0.0 copy-done.2
  31.8 0.0 copy-done.3
  31.9 0.0 copy-done.4
  31.9 2.5 %shard_map.89 = f32[8,16384]{1,0:T(8,128)} custom-call(f32[8,8,16,256]{3,2,1,0:T(8,128)S(1)} %shard_map.87.deposit_ref.unused, f32[8,16384]{1,0:T(8,128)S(1)} %copy-done.4, bf16[256,2048]{1,0:T(8,128)(2,1)S(1)} %copy-done.3, s32[2,1024]{1,0:T(2,128)S(1)} %copy-done.2, f32[17,16,256]{2,1,0:T(8,128)S(1)} %collective-permute-done.before_ref, ...), custom_call_target="tpu_custom_call" | custom-call | flops 1073741824 | bytes 3145728 | tf_op jit(solution)/shard_map/pallas_call | solution.py:27
  34.3 0.0 collective-permute-done.2.low_ref
  34.3 0.0 collective-permute-done.3.high_ref
  34.3 0.0 copy-done
  34.4 0.0 copy-done.1
  34.4 3.4 %shard_map.88 = f32[14,8,16,256]{3,2,1,0:T(8,128)} custom-call(f32[17,8,16,256]{3,2,1,0:T(8,128)S(1)} %copy-done, f32[17,16,256]{2,1,0:T(8,128)S(1)} %collective-permute-done.before_ref, f32[17,16,256]{2,1,0:T(8,128)S(1)} %collective-permute-done.1.after_ref, f32[15,8,256]{2,1,0:T(8,128)S(1)} %collective-permute-done.2.low_ref, ...), custom_call_target="tpu_custom_call" | custom-call | flops 31457280 | bytes 4194304 | tf_op jit(solution)/shard_map/pallas_call | solution.py:27
Async XLA Ops:
  6.0 15.7 %all-to-all-start = ((f32[32,1,1152]{2,1,0:T(1,128)}), f32[32,1,1152]{2,1,0:T(1,128)S(1)}, u32[]{:S(2)}, u32[]{:S(2)}) async-start(f32[32,1,1152]{2,1,0:T(1,128)} %bitcast.5), calls=%async_computation | async-start | bytes 294912 | tf_op jit(solution)/shard_map/all_to_all | solution.py:528
  13.3 21.0 %collective-permute-start.2 = (f32[15,8,256]{2,1,0:T(8,128)}, f32[15,8,256]{2,1,0:T(8,128)S(1)}, u32[]{:S(2)}, u32[]{:S(2)}) collective-permute-start(f32[15,8,256]{2,1,0:T(8,128)} %get-tuple-element.11), channel_id=1, source_target_pairs={{0,1},{1,2},{2,3},{3,0},{4,5},{5,6},{6,7},{7,4},{8,9},{9,10},{10,1... | collective-permute-start | bytes 368648 | tf_op jit(solution)/shard_map/ppermute | solution.py:523
  13.6 20.7 %collective-permute-start.3 = (f32[15,8,256]{2,1,0:T(8,128)}, f32[15,8,256]{2,1,0:T(8,128)S(1)}, u32[]{:S(2)}, u32[]{:S(2)}) collective-permute-start(f32[15,8,256]{2,1,0:T(8,128)} %get-tuple-element.12), channel_id=1, source_target_pairs={{1,0},{2,1},{3,2},{0,3},{5,4},{6,5},{7,6},{4,7},{9,8},{10,9},{11,1... | collective-permute-start | bytes 368648 | tf_op jit(solution)/shard_map/ppermute | solution.py:524
  15.1 15.4 %collective-permute-start = (f32[17,16,256]{2,1,0:T(8,128)}, f32[17,16,256]{2,1,0:T(8,128)S(1)}, u32[]{:S(2)}, u32[]{:S(2)}) collective-permute-start(f32[17,16,256]{2,1,0:T(8,128)} %get-tuple-element.9), channel_id=1, source_target_pairs={{0,4},{4,8},{8,12},{12,16},{16,20},{20,24},{24,28},{28,0},{1,5},{5... | collective-permute-start | bytes 835592 | tf_op jit(solution)/shard_map/ppermute | solution.py:521
  16.9 14.9 %collective-permute-start.1 = (f32[17,16,256]{2,1,0:T(8,128)}, f32[17,16,256]{2,1,0:T(8,128)S(1)}, u32[]{:S(2)}, u32[]{:S(2)}) collective-permute-start(f32[17,16,256]{2,1,0:T(8,128)} %get-tuple-element.10), channel_id=1, source_target_pairs={{4,0},{8,4},{12,8},{16,12},{20,16},{24,20},{28,24},{0,28},{5,1},{9... | collective-permute-start | bytes 835592 | tf_op jit(solution)/shard_map/ppermute | solution.py:522
  21.8 10.1 %copy-start.2 = (s32[2,1024]{1,0:T(2,128)S(1)}, s32[2,1024]{1,0:T(2,128)}, u32[]{:S(2)}) copy-start(s32[2,1024]{1,0:T(2,128)} %crossing_ref.1) | copy-start | bytes 24580
  21.8 10.1 %copy-start.3 = (bf16[256,2048]{1,0:T(8,128)(2,1)S(1)}, bf16[256,2048]{1,0:T(8,128)(2,1)}, u32[]{:S(2)}) copy-start(bf16[256,2048]{1,0:T(8,128)(2,1)} %get-tuple-element.15.hot_ref) | copy-start | bytes 3145732
  21.8 10.1 %copy-start.4 = (f32[8,16384]{1,0:T(8,128)S(1)}, f32[8,16384]{1,0:T(8,128)}, u32[]{:S(2)}) copy-start(f32[8,16384]{1,0:T(8,128)} %get-tuple-element.14.advanced_ref) | copy-start | bytes 1572868
  30.5 3.8 %copy-start = (f32[17,8,16,256]{3,2,1,0:T(8,128)S(1)}, f32[17,8,16,256]{3,2,1,0:T(8,128)}, u32[]{:S(2)}) copy-start(f32[17,8,16,256]{3,2,1,0:T(8,128)} %cells_ref.1) | copy-start | bytes 6684676
  30.5 3.8 %copy-start.1 = (f32[8]{0:T(128)S(1)}, f32[8]{0:T(128)}, u32[]{:S(2)}) copy-start(f32[8]{0:T(128)} %rate_ref.1) | copy-start | bytes 100

commit v6 on v5

--- a/solution.py
+++ b/solution.py
@@ -498,13 +498,23 @@
             pltpu.VMEM((2, 2 * SECTIONS * WINDOW * size_y, 8 * LANES), BF16),
             pltpu.VMEM((2, size_z, 8 * LANES), BF16),
         ],
-        in_specs=[VMEM], out_specs=VMEM, flops=4 << 30, moved_bytes=2 << 20,
+        in_specs=[VMEM], out_specs=VMEM, flops=0, moved_bytes=0,
     )
 
 
 def ring(size):
     up = [(i, (i + 1) % size) for i in range(size)]
     return up, [(j, i) for i, j in up]
+
+
+def exchange(rows):
+    return lax.all_to_all(rows, ("gx", "gy"), split_axis=0, concat_axis=0, tiled=True)
+
+
+def exchange_by_axis(rows):
+    grid = rows.reshape(lax.axis_size("gx"), lax.axis_size("gy"), rows.shape[2])
+    grid = lax.all_to_all(grid, "gx", split_axis=0, concat_axis=0, tiled=True)
+    return lax.all_to_all(grid, "gy", split_axis=1, concat_axis=1, tiled=True).reshape(rows.shape)
 
 
 def on_device(cell_state, evap_rate, parcels, crossing, conv_mass, conv_owner, conv_cell):
@@ -525,7 +535,7 @@
 
     fold = LANES // capacity
     filled = filled.reshape(-1, 9, fold, capacity).transpose(0, 2, 1, 3).reshape(owner_total, 1, 9 * capacity)
-    routed = lax.all_to_all(filled, ("gx", "gy"), split_axis=0, concat_axis=0, tiled=True)
+    routed = lax.cond(crossing[0, 0] >= 0, exchange, exchange_by_axis, filled)
     routed = routed.reshape(-1, fold, 9, capacity).transpose(0, 2, 1, 3).reshape(-1, LANES)
 
     deposited = deposit(routed, cell_state.shape[1:])

time: 38.2 us -> 41.2 us (1.079)
  blocking collectives: 0 us -> 11.5 us
  starting transfers between devices: 13.8 us -> 7.87 us
  waiting for transfers between devices: 3.2 us -> 0.01 us
  between operations: 0.89 us -> 1.49 us
  local copies, waits for them, and re-layouts: 0.02 us -> 0.54 us
    all_to_all x0 -> x1, blocking collectives: none -> 11.5 us  [exchange(): lax.all_to_all(rows, ('gx', 'gy'), split_axis=0, concat_axis=0, tiled=True)]
    all_to_all x1 -> x0, starting transfers between devices: 7.3 us -> none  [on_device(): lax.all_to_all(filled, ('gx', 'gy'), split_axis=0, concat_axis=0, tiled=T...]
    all_to_all x1 -> x0, waiting for transfers between devices: 1.9 us -> none  [on_device(): lax.all_to_all(filled, ('gx', 'gy'), split_axis=0, concat_axis=0, tiled=T...]
    ppermute x1, waiting for transfers between devices: 1.29 us -> 0.01 us  [on_device(): after = lax.ppermute(send_down, 'gx', down_x)]
    ppermute x1, starting transfers between devices: 1.77 us -> 3.02 us  [on_device(): before = lax.ppermute(send_up, 'gx', up_x)]
    slice x0 -> x1, local copies, waits for them, and re-layouts: none -> 0.48 us  [on_device(): routed = lax.cond(crossing[0, 0] >= 0, exchange, exchange_by_axis, filled)]
  transfers between devices with their start and end apart: 5 -> 4, of which waited for: 2 -> 0; matrix products, arithmetic and copies ran while one was open for 0% -> 1% of each run, Pallas kernels for 30% -> 27%
where the time goes in v6:
time: 41.2 us; the launch traced here: 41 us
  Pallas kernels  19.6 us (48%)
  blocking collectives  11.5 us (28%)
  starting transfers between devices  7.87 us (19%)
  between operations  1.49 us (4%)
  local copies, waits for them, and re-layouts  0.54 us (1%)
    pallas_call x4, Pallas kernels, call(): pl.pallas_call(kernel, out_shape=out_shape, in_specs=in_specs or [ANY] *...  19.6 us
    all_to_all x1, blocking collectives, exchange(): lax.all_to_all(rows, ('gx', 'gy'), split_axis=0, concat_axis=0, tiled=True)  11.5 us
    ppermute x1, starting transfers between devices, on_device(): after = lax.ppermute(send_down, 'gx', down_x)  3.1 us
    ppermute x1, starting transfers between devices, on_device(): before = lax.ppermute(send_up, 'gx', up_x)  3.02 us
    ppermute x1, starting transfers between devices, on_device(): high = lax.ppermute(side_down, 'gy', down_y)  1.74 us
  transfers between devices with their start and end apart: 4, of which 0 were waited for; matrix products, arithmetic and copies ran while one was open for 1% of the time, Pallas kernels for 27%

profile of v6, /device:TPU:0, one launch (start us, length us, event | category | flops | bytes accessed | tf_op | source)
XLA Modules:
  0.0 41.0 jit_solution(7630383799976104224)
XLA Ops:
  0.6 0.0 copy-start.2
  0.6 5.0 %shard_map.86 = (f32[17,16,256]{2,1,0:T(8,128)}, f32[17,16,256]{2,1,0:T(8,128)}, f32[15,8,256]{2,1,0:T(8,128)}, f32[15,8,256]{2,1,0:T(8,128)}, f32[8,16384]{1,0:...) custom-call(f32[17,8,16,256]{3,2,1,0:T(8,128)} %cells_ref.1, f32[8,16384]{1,0:T(8,128)} %parcels_hbm.1, ...), custom_call_target="tpu_custom_call" | custom-call | flops 2147483648 | bytes 6291456 | tf_op jit(solution)/shard_map/pallas_call | solution.py:27
  5.6 0.0 copy-start.3
  5.6 0.0 copy-start.4
  5.7 3.0 %collective-permute-start = (f32[17,16,256]{2,1,0:T(8,128)}, f32[17,16,256]{2,1,0:T(8,128)S(1)}, u32[]{:S(2)}, u32[]{:S(2)}) collective-permute-start(f32[17,16,256]{2,1,0:T(8,128)} %get-tuple-element.15), channel_id=1, source_target_pairs={{0,4},{4,8},{8,12},{12,16},{16,20},{20,24},{24,28},{28,0},{1,5},{5... | collective-permute-start | bytes 835592 | tf_op jit(solution)/shard_map/ppermute | solution.py:531
  8.7 3.1 %collective-permute-start.1 = (f32[17,16,256]{2,1,0:T(8,128)}, f32[17,16,256]{2,1,0:T(8,128)S(1)}, u32[]{:S(2)}, u32[]{:S(2)}) collective-permute-start(f32[17,16,256]{2,1,0:T(8,128)} %get-tuple-element.16), channel_id=1, source_target_pairs={{4,0},{8,4},{12,8},{16,12},{20,16},{24,20},{28,24},{0,28},{5,1},{9... | collective-permute-start | bytes 835592 | tf_op jit(solution)/shard_map/ppermute | solution.py:532
  11.8 0.0 collective-permute-start.2
  11.8 1.7 %collective-permute-start.3 = (f32[15,8,256]{2,1,0:T(8,128)}, f32[15,8,256]{2,1,0:T(8,128)S(1)}, u32[]{:S(2)}, u32[]{:S(2)}) collective-permute-start(f32[15,8,256]{2,1,0:T(8,128)} %get-tuple-element.18), channel_id=1, source_target_pairs={{1,0},{2,1},{3,2},{0,3},{5,4},{6,5},{7,6},{4,7},{9,8},{10,9},{11,1... | collective-permute-start | bytes 368648 | tf_op jit(solution)/shard_map/ppermute | solution.py:534
  13.5 0.0 copy-done.2
  13.5 0.5 %slice.3 = s32[1,1]{1,0:T(1,128)} slice(s32[2,1024]{1,0:T(2,128)S(1)} %copy-done.2), slice={[0:1], [0:1]} | slice | bytes 8 | tf_op jit(solution)/shard_map/slice | solution.py:538
  14.6 11.5 %conditional.1 = (f32[32,1,1152]{2,0,1:T(8,128)S(1)}) conditional(s32[]{:T(128)} %bitcast.3, f32[288,128]{1,0:T(8,128)S(1)} %get-tuple-element.19, f32[288,128]{1,0:T(8,128)S(1)} %get-tuple-element.19), branch_computations={%region_0.0_spmd, %region_1.0_spmd} | conditional | bytes 1769480 | solution.py:538
  14.6 11.5 %all_to_all.14 = f32[32,1,1152]{2,1,0:T(1,128)S(1)} all-to-all(f32[32,1,1152]{2,1,0:T(1,128)S(1)} %bitcast.6), channel_id=1, replica_groups=mesh['gx'=8,'gy'=4] {'gx','gy'}, dimensions={0} | all-to-all | bytes 294912 | tf_op jit(solution)/shard_map/cond/branch_1_fun/all_to_all | solution.py:511
  26.1 8.8 %shard_map.87.deposit_ref.unused = f32[8,8,16,256]{3,2,1,0:T(8,128)S(1)} custom-call(f32[288,128]{1,0:T(8,128)S(1)} %reshape_transpose_reshape.9.routed_ref), custom_call_target="tpu_custom_call" | custom-call | tf_op jit(solution)/shard_map/pallas_call | solution.py:27
  34.9 0.0 copy-start
  34.9 0.0 copy-start.1
  34.9 0.0 collective-permute-done.before_ref
  34.9 0.0 collective-permute-done.1.after_ref
  34.9 0.0 copy-done.3
  35.0 0.0 copy-done.4
  35.0 2.5 %shard_map.89 = f32[8,16384]{1,0:T(8,128)} custom-call(f32[8,8,16,256]{3,2,1,0:T(8,128)S(1)} %shard_map.87.deposit_ref.unused, f32[8,16384]{1,0:T(8,128)S(1)} %copy-done.4, bf16[256,2048]{1,0:T(8,128)(2,1)S(1)} %copy-done.3, s32[2,1024]{1,0:T(2,128)S(1)} %copy-done.2, f32[17,16,256]{2,1,0:T(8,128)S(1)} %collective-permute-done.before_ref, ...), custom_call_target="tpu_custom_call" | custom-call | flops 1073741824 | bytes 3145728 | tf_op jit(solution)/shard_map/pallas_call | solution.py:27
  37.4 0.0 collective-permute-done.2.low_ref
  37.4 0.0 collective-permute-done.3.high_ref
  37.4 0.0 copy-done
  37.5 3.4 %shard_map.88 = f32[14,8,16,256]{3,2,1,0:T(8,128)} custom-call(f32[17,8,16,256]{3,2,1,0:T(8,128)S(1)} %copy-done, f32[17,16,256]{2,1,0:T(8,128)S(1)} %collective-permute-done.before_ref, f32[17,16,256]{2,1,0:T(8,128)S(1)} %collective-permute-done.1.after_ref, f32[15,8,256]{2,1,0:T(8,128)S(1)} %collective-permute-done.2.low_ref, ...), custom_call_target="tpu_custom_call" | custom-call | flops 31457280 | bytes 4194304 | tf_op jit(solution)/shard_map/pallas_call | solution.py:27
  (3 shorter events, 0.0 us)
Async XLA Ops:
  0.6 12.9 %copy-start.2 = (s32[2,1024]{1,0:T(2,128)S(1)}, s32[2,1024]{1,0:T(2,128)}, u32[]{:S(2)}) copy-start(s32[2,1024]{1,0:T(2,128)} %crossing_ref.1) | copy-start | bytes 24580
  5.6 29.3 %copy-start.3 = (bf16[256,2048]{1,0:T(8,128)(2,1)S(1)}, bf16[256,2048]{1,0:T(8,128)(2,1)}, u32[]{:S(2)}) copy-start(bf16[256,2048]{1,0:T(8,128)(2,1)} %get-tuple-element.21.hot_ref) | copy-start | bytes 3145732
  5.6 29.3 %copy-start.4 = (f32[8,16384]{1,0:T(8,128)S(1)}, f32[8,16384]{1,0:T(8,128)}, u32[]{:S(2)}) copy-start(f32[8,16384]{1,0:T(8,128)} %get-tuple-element.20.advanced_ref) | copy-start | bytes 1572868
  5.7 29.3 %collective-permute-start = (f32[17,16,256]{2,1,0:T(8,128)}, f32[17,16,256]{2,1,0:T(8,128)S(1)}, u32[]{:S(2)}, u32[]{:S(2)}) collective-permute-start(f32[17,16,256]{2,1,0:T(8,128)} %get-tuple-element.15), channel_id=1, source_target_pairs={{0,4},{4,8},{8,12},{12,16},{16,20},{20,24},{24,28},{28,0},{1,5},{5... | collective-permute-start | bytes 835592 | tf_op jit(solution)/shard_map/ppermute | solution.py:531
  8.7 26.3 %collective-permute-start.1 = (f32[17,16,256]{2,1,0:T(8,128)}, f32[17,16,256]{2,1,0:T(8,128)S(1)}, u32[]{:S(2)}, u32[]{:S(2)}) collective-permute-start(f32[17,16,256]{2,1,0:T(8,128)} %get-tuple-element.16), channel_id=1, source_target_pairs={{4,0},{8,4},{12,8},{16,12},{20,16},{24,20},{28,24},{0,28},{5,1},{9... | collective-permute-start | bytes 835592 | tf_op jit(solution)/shard_map/ppermute | solution.py:532
  11.8 25.7 %collective-permute-start.2 = (f32[15,8,256]{2,1,0:T(8,128)}, f32[15,8,256]{2,1,0:T(8,128)S(1)}, u32[]{:S(2)}, u32[]{:S(2)}) collective-permute-start(f32[15,8,256]{2,1,0:T(8,128)} %get-tuple-element.17), channel_id=1, source_target_pairs={{0,1},{1,2},{2,3},{3,0},{4,5},{5,6},{6,7},{7,4},{8,9},{9,10},{10,1... | collective-permute-start | bytes 368648 | tf_op jit(solution)/shard_map/ppermute | solution.py:533
  11.8 25.7 %collective-permute-start.3 = (f32[15,8,256]{2,1,0:T(8,128)}, f32[15,8,256]{2,1,0:T(8,128)S(1)}, u32[]{:S(2)}, u32[]{:S(2)}) collective-permute-start(f32[15,8,256]{2,1,0:T(8,128)} %get-tuple-element.18), channel_id=1, source_target_pairs={{1,0},{2,1},{3,2},{0,3},{5,4},{6,5},{7,6},{4,7},{9,8},{10,9},{11,1... | collective-permute-start | bytes 368648 | tf_op jit(solution)/shard_map/ppermute | solution.py:534
  34.9 2.6 %copy-start = (f32[17,8,16,256]{3,2,1,0:T(8,128)S(1)}, f32[17,8,16,256]{3,2,1,0:T(8,128)}, u32[]{:S(2)}) copy-start(f32[17,8,16,256]{3,2,1,0:T(8,128)} %cells_ref.1) | copy-start | bytes 6684676
  34.9 2.5 %copy-start.1 = (f32[8]{0:T(128)S(1)}, f32[8]{0:T(128)}, u32[]{:S(2)}) copy-start(f32[8]{0:T(128)} %rate_ref.1) | copy-start | bytes 100

commit v7 on v4

--- a/solution.py
+++ b/solution.py
@@ -12,7 +12,6 @@
 COUNT = SECTIONS + SPECIES
 LANES = 128
 WIDE = 256
-WINDOW = 4
 F32 = jnp.float32
 BF16 = jnp.bfloat16
 ANY = pl.BlockSpec(memory_space=pl.ANY)
@@ -129,35 +128,27 @@
 
 
 def prepare_kernel(
-    owner_total, capacity,
-    cells_hbm, parcels_hbm, crossing_hbm, mass_hbm, owner_hbm, cell_hbm,
-    up_hbm, down_hbm, yup_hbm, ydown_hbm, advanced_hbm, hot_hbm, filled_hbm,
-    cells_ref, parcels_ref, crossing_ref, mass_ref, owner_ref, cell_ref,
-    leave_ref, yup_ref, ydown_ref, advanced_ref, hot_ref, filled_ref,
-    parts_ref, left_ref, spot_ref, sems,
+    cells_hbm, parcels_hbm, crossing_hbm, up_hbm, down_hbm, yup_hbm, ydown_hbm, advanced_hbm, hot_hbm,
+    cells_ref, parcels_ref, crossing_ref, leave_ref, yup_ref, ydown_ref, advanced_ref, hot_ref, parts_ref, sems,
 ):
     size_x, size_y, size_z = cells_hbm.shape[1:]
     face = slice(0, COUNT + 1)
     tail = slice(COUNT + 1, up_hbm.shape[0])
     pairs = [
         (crossing_hbm, crossing_ref),
-        (owner_hbm, owner_ref),
-        (cell_hbm, cell_ref),
-        (mass_hbm, mass_ref),
         (parcels_hbm, parcels_ref),
         (cells_hbm, cells_ref),
         (cells_ref.at[face, size_x - 1], up_hbm.at[face]),
         (cells_ref.at[face, 0], down_hbm.at[face]),
-        (filled_ref, filled_hbm),
+        (yup_ref, yup_hbm),
+        (ydown_ref, ydown_hbm),
         (hot_ref, hot_hbm),
         (advanced_ref, advanced_hbm),
         (leave_ref.at[0], up_hbm.at[tail]),
         (leave_ref.at[1], down_hbm.at[tail]),
-        (yup_ref, yup_hbm),
-        (ydown_ref, ydown_hbm),
     ]
     copies = [pltpu.make_async_copy(source, target, sems.at[i]) for i, (source, target) in enumerate(pairs)]
-    for copy in copies[:6]:
+    for copy in copies[:3]:
         copy.start()
     cross = crossing_ref.shape[1]
     slot_total = parcels_ref.shape[1]
@@ -166,8 +157,8 @@
         for first in range(0, cross, LANES):
             lower = crossing_ref[side : side + 1, first : first + LANES] & (WIDE - 1)
             hot_ref[:, side * cross + first : side * cross + first + LANES] = hot_columns(lower, WIDE)
-    copies[9].start()
-    copies[4].wait()
+    copies[7].start()
+    copies[1].wait()
 
     def advance_pair(i, unused):
         for number in range(2):
@@ -181,7 +172,16 @@
         return unused
 
     lax.fori_loop(0, slot_total // (4 * LANES), advance_pair, 0, unroll=4)
-    copies[10].start()
+    copies[8].start()
+    copies[2].wait()
+    copies[3].start()
+    copies[4].start()
+    for c in range(COUNT + 1):
+        source = c if c < COUNT else COUNT + 1
+        yup_ref[c] = cells_ref[source, :, size_y - 1, :]
+        ydown_ref[c] = cells_ref[source, :, 0, :]
+    copies[5].start()
+    copies[6].start()
 
     halves_y, halves_z = size_y // 8, size_z // LANES
     part_rows = parts_ref.shape[0]
@@ -208,50 +208,59 @@
                     total = jnp.where(upper == (rows + i) // 8, picked[i : i + 8], total)
                 for number, spot in enumerate(spots):
                     leave_ref[spot] = total[:, number * LANES : (number + 1) * LANES]
-    copies[11].start()
-    copies[12].start()
-
-    copies[5].wait()
-    copies[6].start()
-    copies[7].start()
-    for c in range(COUNT + 1):
-        source = c if c < COUNT else COUNT + 1
-        yup_ref[c] = cells_ref[source, :, size_y - 1, :]
-        ydown_ref[c] = cells_ref[source, :, 0, :]
-    copies[13].start()
-    copies[14].start()
-    for copy in copies[1:4]:
+    copies[9].start()
+    copies[10].start()
+    for copy in copies[3:]:
         copy.wait()
-    bucket_into(owner_total, capacity, mass_ref, owner_ref, cell_ref, filled_ref, left_ref, spot_ref)
-    copies[8].start()
-    for copy in copies[6:]:
-        copy.wait()
-
-
-def prepare(cells, parcels, crossing, mass, owner, cell, owner_total, capacity):
+
+
+def prepare(cells, parcels, crossing):
     size_x, size_y, size_z = cells.shape[1:]
     extra = 8 * crossing.shape[1] // (size_y * size_z)
-    places = owner_total * capacity
     shape = jax.ShapeDtypeStruct
     face = shape((COUNT + 1 + extra, size_y, size_z), F32)
     side = shape((COUNT + 1, size_x, size_z), F32)
     advanced = shape(parcels.shape, F32)
     hot = shape((WIDE, crossing.size), BF16)
-    filled = shape((9 * places // LANES, LANES), F32)
-    operands = (cells, parcels, crossing, mass, owner, cell)
+    operands = (cells, parcels, crossing)
     scratch = [pltpu.VMEM(a.shape, a.dtype) for a in operands]
     scratch += [pltpu.VMEM((2, extra, size_y, size_z), F32)]
-    scratch += [pltpu.VMEM(a.shape, a.dtype) for a in (side, side, advanced, hot, filled)]
-    scratch += [
-        pltpu.VMEM((8 * parcels.shape[1] // WIDE, WIDE), F32),
-        pltpu.VMEM((19 * places // WIDE, mass.shape[1]), BF16),
-        pltpu.VMEM((WIDE, mass.shape[1]), BF16),
-        pltpu.SemaphoreType.DMA((15,)),
-    ]
+    scratch += [pltpu.VMEM(a.shape, a.dtype) for a in (side, side, advanced, hot)]
+    scratch += [pltpu.VMEM((8 * parcels.shape[1] // WIDE, WIDE), F32), pltpu.SemaphoreType.DMA((11,))]
     return call(
-        functools.partial(prepare_kernel, owner_total, capacity),
-        [face, face, side, side, advanced, hot, filled], operands, scratch,
-        flops=2 << 30, moved_bytes=6 << 20, grant=ALL,
+        prepare_kernel, [face, face, side, side, advanced, hot], operands, scratch,
+        flops=1 << 30, moved_bytes=6 << 20, grant=ALL,
+    )
+
+
+def bucket_kernel(
+    owner_total, capacity, unused, mass_hbm, owner_hbm, cell_hbm, out_hbm,
+    mass_ref, owner_ref, cell_ref, out_ref, left_ref, hot_ref, sems,
+):
+    pairs = [(owner_hbm, owner_ref), (cell_hbm, cell_ref), (mass_hbm, mass_ref)]
+    copies = [pltpu.make_async_copy(source, target, sems.at[i]) for i, (source, target) in enumerate(pairs)]
+    for copy in copies:
+        copy.start()
+    for copy in copies:
+        copy.wait()
+    bucket_into(owner_total, capacity, mass_ref, owner_ref, cell_ref, out_ref, left_ref, hot_ref)
+    out = pltpu.make_async_copy(out_ref, out_hbm, sems.at[3])
+    out.start()
+    out.wait()
+
+
+def bucket(earlier, mass, owner, cell, owner_total, capacity):
+    places = owner_total * capacity
+    out = jax.ShapeDtypeStruct((9 * places // LANES, LANES), F32)
+    return call(
+        functools.partial(bucket_kernel, owner_total, capacity), out, (earlier, mass, owner, cell),
+        [pltpu.VMEM(a.shape, a.dtype) for a in (mass, owner, cell, out)]
+        + [
+            pltpu.VMEM((19 * places // WIDE, mass.shape[1]), BF16),
+            pltpu.VMEM((WIDE, mass.shape[1]), BF16),
+            pltpu.SemaphoreType.DMA((4,)),
+        ],
+        flops=1 << 30, moved_bytes=1 << 20, grant=ALL,
     )
 
 
@@ -366,47 +375,30 @@
         write(c, moved(c))
 
 
-def cells_kernel(
-    cells_ref, before_ref, after_ref, low_ref, high_ref, deposit_ref, rate_ref, out_hbm, out_ref, sems
-):
-    size_x = cells_ref.shape[1]
-    last = size_x - 1
-
-    def store(x):
-        return pltpu.make_async_copy(out_ref.at[:, x], out_hbm.at[:, x], sems.at[x])
-
-    def layer(left, x, right):
+def inner_kernel(cells_ref, low_ref, high_ref, rate_ref, out_ref):
+    def middle(x, unused):
         def write(c, value):
-            out_ref[c, x] = value + deposit_ref[c, x] if c < SECTIONS else value
+            out_ref[c, x] = value
 
         slab_update(
-            left,
+            lambda c: cells_ref[c, x - 1],
             lambda c: cells_ref[c, x],
-            right,
+            lambda c: cells_ref[c, x + 1],
             lambda c: low_ref[c, pl.ds(x, 1), :],
             lambda c: high_ref[c, pl.ds(x, 1), :],
             rate_ref,
             write,
         )
-        store(x).start()
-
-    def middle(x, unused):
-        layer(lambda c: cells_ref[c, x - 1], x, lambda c: cells_ref[c, x + 1])
         return unused
 
-    lax.fori_loop(1, last, middle, 0)
-    layer(lambda c: before_ref[c], 0, lambda c: cells_ref[c, 1])
-    layer(lambda c: cells_ref[c, last - 1], last, lambda c: after_ref[c])
-    for x in range(size_x):
-        store(x).wait()
-
-
-def update_cells(cells, before, after, low, high, deposited, rate):
+    lax.fori_loop(1, cells_ref.shape[1] - 1, middle, 0)
+
+
+def inner(cells, low, high, rate):
     out = jax.ShapeDtypeStruct((COUNT,) + cells.shape[1:], F32)
     return call(
-        cells_kernel, out, (cells, before, after, low, high, deposited, rate),
-        [pltpu.VMEM(out.shape, F32), pltpu.SemaphoreType.DMA((cells.shape[1],))],
-        in_specs=[VMEM] * 6 + [SMEM], flops=30 << 20, moved_bytes=4 << 20,
+        inner_kernel, out, (cells, low, high, rate), [],
+        in_specs=[VMEM] * 3 + [SMEM], out_specs=VMEM, flops=30 << 20, moved_bytes=4 << 20,
     )
 
 
@@ -414,8 +406,26 @@
     return value >> (count.bit_length() - 1) if count & (count - 1) == 0 else value // count
 
 
-def deposit_kernel(shape, routed_ref, out_ref, total_ref, mass_ref, spread_ref, depth_ref):
-    size_x, size_y, size_z = shape
+def final_kernel(
+    windows, cells_ref, inner_ref, before_ref, after_ref, low_ref, high_ref, routed_ref, rate_ref, out_hbm,
+    total_ref, species_ref, mass_ref, spread_ref, depth_ref, sems,
+):
+    size_x, size_y, size_z = cells_ref.shape[1:]
+    last = size_x - 1
+    middle = slice(1, last)
+    sections = slice(0, SECTIONS)
+    others = slice(SECTIONS, COUNT)
+    pairs = [
+        (inner_ref.at[sections, middle], total_ref.at[:, middle]),
+        (inner_ref.at[others, middle], out_hbm.at[others, middle]),
+        (species_ref.at[:, 0], out_hbm.at[others, 0]),
+        (species_ref.at[:, 1], out_hbm.at[others, last]),
+        (total_ref, out_hbm.at[sections]),
+    ]
+    copies = [pltpu.make_async_copy(source, target, sems.at[i]) for i, (source, target) in enumerate(pairs)]
+    copies[0].start()
+    copies[1].start()
+
     groups = routed_ref.shape[0] // 9
     per = groups // 8
     span = LANES // per
@@ -438,67 +448,88 @@
         valid = cell >= 0
         bounds.append((jnp.min(jnp.where(valid, layer, size_x)), jnp.max(jnp.where(valid, layer, -1))))
 
-    half = SECTIONS * WINDOW * size_y
     zero = jnp.zeros((size_y, LANES), BF16)
 
-    def spread(q, first):
+    def deposit(q, start):
+        window = windows[q]
+        half = SECTIONS * window * size_y
+        first = jnp.minimum(start, size_x - window)
         cell = mass_ref[q, SECTIONS].astype(jnp.int32)
         plane = quotient(cell, size_z)
         depth = cell - plane * size_z
-        plane = jnp.where(cell >= 0, plane - first * size_y, -1).astype(F32)
+        plane = jnp.where(plane >= start * size_y, plane - first * size_y, -1)
+        plane = jnp.where(cell >= 0, plane, -1).astype(F32)
         parts = [split(mass_ref[q, s]) for s in range(SECTIONS)]
         for i in range(8):
             at = slice(i * LANES, (i + 1) * LANES)
             depth_ref[q % 2, :, at] = hot_columns(depth[i : i + 1], size_z)
             plane_rows = rows_of(plane[i : i + 1], size_y)
             rows = [[rows_of(part[i : i + 1].astype(F32), size_y) for part in pair] for pair in parts]
-            for w in range(WINDOW):
+            for w in range(window):
                 hit = plane_rows == packed(iota((size_y, LANES), 0) + w * size_y)
                 for s in range(SECTIONS):
-                    base = (s * WINDOW + w) * size_y
+                    base = (s * window + w) * size_y
                     for part in range(2):
                         spread_ref[q % 2, part * half + base : part * half + base + size_y, at] = jnp.where(
                             hit, rows[s][part], zero
                         )
-
-    def deposit(q, first):
-        added = contract_lanes(spread_ref[q % 2], depth_ref[q % 2])
+        added = contract_lanes(spread_ref[q % 2, : 2 * half], depth_ref[q % 2])
         for s in range(SECTIONS):
-            base = s * WINDOW * size_y
-            rows = added[base : base + WINDOW * size_y] + added[half + base : half + base + WINDOW * size_y]
-            at = pl.ds(first, WINDOW)
-            total_ref[s, at] = total_ref[s, at] + rows.reshape(WINDOW, size_y, size_z)
-
-    total_ref[...] = jnp.zeros(total_ref.shape, F32)
+            base = s * window * size_y
+            rows = added[base : base + window * size_y] + added[half + base : half + base + window * size_y]
+            at = pl.ds(first, window)
+            total_ref[s, at] = total_ref[s, at] + rows.reshape(window, size_y, size_z)
+
+    def write(x, number, c, value):
+        if c < SECTIONS:
+            total_ref[c, x] = value
+        else:
+            species_ref[c - SECTIONS, number] = value
+
+    slab_update(
+        lambda c: before_ref[c], lambda c: cells_ref[c, 0], lambda c: cells_ref[c, 1],
+        lambda c: low_ref[c, 0:1, :], lambda c: high_ref[c, 0:1, :],
+        rate_ref, functools.partial(write, 0, 0),
+    )
+    slab_update(
+        lambda c: cells_ref[c, last - 1], lambda c: cells_ref[c, last], lambda c: after_ref[c],
+        lambda c: low_ref[c, last : last + 1, :], lambda c: high_ref[c, last : last + 1, :],
+        rate_ref, functools.partial(write, last, 1),
+    )
+    copies[2].start()
+    copies[3].start()
+    copies[0].wait()
     for q in range(per):
-        first = jnp.minimum(bounds[q][0], size_x - 1)
-        spread(q, first)
-        deposit(q, first)
+        deposit(q, bounds[q][0] if windows[q] < size_x else 0)
     for q in range(per):
-        low, high = bounds[q]
-
-        def more(t, unused, q=q, low=low):
-            first = low + t * WINDOW
-            spread(q, first)
-            deposit(q, first)
-            return unused
-
-        lax.fori_loop(1, quotient(high - low + WINDOW, WINDOW), more, 0)
-    out_ref[...] = total_ref[:, 0:size_x]
-
-
-def deposit(routed, shape):
-    size_x, size_y, size_z = shape
+        if windows[q] < size_x:
+            low, high = bounds[q]
+
+            def more(t, unused, q=q, low=low):
+                deposit(q, low + t * windows[q])
+                return unused
+
+            lax.fori_loop(1, jnp.where(high - low < windows[q], 1, 1 + (size_x - 1) // windows[q]), more, 0)
+    copies[4].start()
+    for copy in copies[1:]:
+        copy.wait()
+
+
+def final(windows, cells, inner_cells, before, after, low, high, routed, rate):
+    size_x, size_y, size_z = cells.shape[1:]
     per = routed.shape[0] // 9 // 8
     return call(
-        functools.partial(deposit_kernel, shape), jax.ShapeDtypeStruct((SECTIONS,) + shape, F32), (routed,),
+        functools.partial(final_kernel, windows), jax.ShapeDtypeStruct(inner_cells.shape, F32),
+        (cells, inner_cells, before, after, low, high, routed, rate),
         [
-            pltpu.VMEM((SECTIONS, size_x + WINDOW - 1, size_y, size_z), F32),
+            pltpu.VMEM((SECTIONS, size_x, size_y, size_z), F32),
+            pltpu.VMEM((SPECIES, 2, size_y, size_z), F32),
             pltpu.VMEM((per, SECTIONS + 1, 8, LANES), F32),
-            pltpu.VMEM((2, 2 * SECTIONS * WINDOW * size_y, 8 * LANES), BF16),
+            pltpu.VMEM((2, 2 * SECTIONS * max(windows) * size_y, 8 * LANES), BF16),
             pltpu.VMEM((2, size_z, 8 * LANES), BF16),
+            pltpu.SemaphoreType.DMA((5,)),
         ],
-        in_specs=[VMEM], out_specs=VMEM, flops=4 << 30, moved_bytes=2 << 20,
+        in_specs=[VMEM] * 7 + [SMEM], flops=4 << 30, moved_bytes=6 << 20,
     )
 
 
@@ -514,23 +545,24 @@
     up_x, down_x = ring(lax.axis_size("gx"))
     up_y, down_y = ring(lax.axis_size("gy"))
 
-    send_up, send_down, side_up, side_down, advanced, hot, filled = prepare(
-        cell_state, parcels, crossing, conv_mass, conv_owner.reshape(-1, LANES), conv_cell.reshape(-1, LANES),
-        owner_total, capacity,
-    )
+    send_up, send_down, side_up, side_down, advanced, hot = prepare(cell_state, parcels, crossing)
     before = lax.ppermute(send_up, "gx", up_x)
     after = lax.ppermute(send_down, "gx", down_x)
     low = lax.ppermute(side_up, "gy", up_y)
     high = lax.ppermute(side_down, "gy", down_y)
 
+    filled = bucket(
+        send_up, conv_mass, conv_owner.reshape(-1, LANES), conv_cell.reshape(-1, LANES), owner_total, capacity
+    )
     fold = LANES // capacity
     filled = filled.reshape(-1, 9, fold, capacity).transpose(0, 2, 1, 3).reshape(owner_total, 1, 9 * capacity)
     routed = lax.all_to_all(filled, ("gx", "gy"), split_axis=0, concat_axis=0, tiled=True)
     routed = routed.reshape(-1, fold, 9, capacity).transpose(0, 2, 1, 3).reshape(-1, LANES)
 
-    deposited = deposit(routed, cell_state.shape[1:])
+    windows = [cell_state.shape[1]] * (routed.shape[0] // 9 // 8)
+    inner_cells = inner(cell_state, low, high, evap_rate)
     new_parcels = arrive(advanced, hot, crossing, before, after)
-    new_cells = update_cells(cell_state, before, after, low, high, deposited, evap_rate)
+    new_cells = final(windows, cell_state, inner_cells, before, after, low, high, routed, evap_rate)
     return (new_cells, new_parcels)
 
 

time: 40.9 us -> 44.1 us (1.078)
  the two profiles are of different devices: /device:TPU:0 before, /device:TPU:1 now
where the time goes in v7:
time: 44.1 us; the launch traced here: 43.8 us
  Pallas kernels  19.9 us (45%)
  starting transfers between devices  13.6 us (31%)
  waiting for transfers between devices  5.2 us (12%)
  local copies, waits for them, and re-layouts  4.37 us (10%)
  between operations  0.75 us (2%)
    pallas_call x5, Pallas kernels, call(): pl.pallas_call(kernel, out_shape=out_shape, in_specs=in_specs or [ANY] *...  19.9 us
    all_to_all x1, starting transfers between devices, on_device(): lax.all_to_all(filled, ('gx', 'gy'), split_axis=0, concat_axis=0, tiled=T...  6.71 us
    ppermute x1, starting transfers between devices, on_device(): after = lax.ppermute(send_down, 'gx', down_x)  5.16 us
    unnamed x20, local copies, waits for them, and re-layouts  4.37 us
    ppermute x1, waiting for transfers between devices, on_device(): low = lax.ppermute(side_up, 'gy', up_y)  3.51 us
    ppermute x1, starting transfers between devices, on_device(): low = lax.ppermute(side_up, 'gy', up_y)  1.7 us
    ppermute x1, waiting for transfers between devices, on_device(): high = lax.ppermute(side_down, 'gy', down_y)  1.68 us
  transfers between devices with their start and end apart: 5, of which 2 were waited for; matrix products, arithmetic and copies ran while one was open for 0% of the time, Pallas kernels for 17%

profile of v7, /device:TPU:1, one launch (start us, length us, event | category | flops | bytes accessed | tf_op | source)
XLA Modules:
  0.0 43.8 jit_solution(15416233059700664846)
XLA Ops:
  0.6 3.9 %shard_map.86 = (f32[17,16,256]{2,1,0:T(8,128)}, f32[17,16,256]{2,1,0:T(8,128)}, f32[15,8,256]{2,1,0:T(8,128)}, f32[15,8,256]{2,1,0:T(8,128)}, f32[8,16384]{1,0:T(8,128)}, /*index=5*/bf16[256,2048]{1,0:T(8,128)(2,1)}) custom-call(f32[17,8,16,256]{3,2,1,0:T(8,128)} %cells_ref.3, f32[8,16384]{1,0:T(8,128)} %parcels_hbm.1, s32[2,1024]{1,0:T(2,128)} %crossing_ref.1), custom_call_target="tpu_custom_call" | custom-call | flops 1073741824 | bytes 6291456 | tf_op jit(solution)/shard_map/pallas_call | solution.py:26
  4.5 5.2 %collective-permute-start.3 = (f32[17,16,256]{2,1,0:T(8,128)}, f32[17,16,256]{2,1,0:T(8,128)S(1)}, u32[]{:S(2)}, u32[]{:S(2)}) collective-permute-start(f32[17,16,256]{2,1,0:T(8,128)} %get-tuple-element.11), channel_id=1, source_target_pairs={{4,0},{8,4},{12,8},{16,12},{20,16},{24,20},{28,24},{0,28},{5,1},{9... | collective-permute-start | bytes 835592 | tf_op jit(solution)/shard_map/ppermute | solution.py:550
  9.7 0.0 collective-permute-start.2
  9.7 3.1 %shard_map.88 = f32[288,128]{1,0:T(8,128)} custom-call(f32[17,16,256]{2,1,0:T(8,128)} %get-tuple-element.10.unused, f32[8,2048]{1,0:T(8,128)} %mass_hbm.1, s32[16,128]{1,0:T(8,128)} %bitcast.6, s32[16,128]{1,0:T(8,128)} %bitcast.7), custom_call_target="tpu_custom_call" | custom-call | flops 1073741824 | bytes 1048576 | tf_op jit(solution)/shard_map/pallas_call | solution.py:26
  12.8 6.7 %all-to-all-start = ((f32[32,1,1152]{2,1,0:T(1,128)}), f32[32,1,1152]{2,1,0:T(1,128)S(1)}, u32[]{:S(2)}, u32[]{:S(2)}) async-start(f32[32,1,1152]{2,1,0:T(1,128)} %bitcast.5), calls=%async_computation | async-start | bytes 294912 | tf_op jit(solution)/shard_map/all_to_all | solution.py:559
  19.5 0.0 copy-done.9
  19.5 1.7 %collective-permute-start = (f32[15,8,256]{2,1,0:T(8,128)S(1)}, f32[15,8,256]{2,1,0:T(8,128)S(1)}, u32[]{:S(2)}, u32[]{:S(2)}) collective-permute-start(f32[15,8,256]{2,1,0:T(8,128)S(1)} %copy-done.9), channel_id=1, source_target_pairs={{0,1},{1,2},{2,3},{3,0},{4,5},{5,6},{6,7},{7,4},{8,9},{9,10},{10,1... | collective-permute-start | bytes 368648 | tf_op jit(solution)/shard_map/ppermute | solution.py:551
  21.2 0.0 copy-done.8
  21.2 0.0 collective-permute-start.1
  21.2 3.5 %collective-permute-done.low_ref = f32[15,8,256]{2,1,0:T(8,128)S(1)} collective-permute-done((f32[15,8,256]{2,1,0:T(8,128)S(1)}, f32[15,8,256]{2,1,0:T(8,128)S(1)}, u32[]{:S(2)}, u32[]{:S(2)}) %collective-permute-start) | collective-permute-done | bytes 122912 | tf_op jit(solution)/shard_map/ppermute | solution.py:551
  24.8 1.7 %collective-permute-done.1.high_ref = f32[15,8,256]{2,1,0:T(8,128)S(1)} collective-permute-done((f32[15,8,256]{2,1,0:T(8,128)S(1)}, f32[15,8,256]{2,1,0:T(8,128)S(1)}, u32[]{:S(2)}, u32[]{:S(2)}) %collective-permute-start.1) | collective-permute-done | bytes 122912 | tf_op jit(solution)/shard_map/ppermute | solution.py:552
  26.4 0.0 copy-done.4
  26.4 1.6 %copy-done = f32[17,8,16,256]{3,2,1,0:T(8,128)S(1)} copy-done((f32[17,8,16,256]{3,2,1,0:T(8,128)S(1)}, f32[17,8,16,256]{3,2,1,0:T(8,128)}, u32[]{:S(2)}) %copy-start) | copy-done | bytes 2228248
  28.1 2.0 %shard_map.87.inner_ref = f32[14,8,16,256]{3,2,1,0:T(8,128)S(1)} custom-call(f32[17,8,16,256]{3,2,1,0:T(8,128)S(1)} %copy-done, f32[15,8,256]{2,1,0:T(8,128)S(1)} %collective-permute-done.low_ref, f32[15,8,256]{2,1,0:T(8,128)S(1)} %collective-permute-done.1.high_ref, f32[8]{0:T(128)S(1)} %copy-done.4), custom_call_target="tpu_custom_call" | custom-call | flops 31457280 | bytes 4194304 | tf_op jit(solution)/shard_map/pallas_call | solution.py:26
  30.1 0.0 copy-start.2
  30.1 1.2 %copy-done.2 = f32[14,8,16,256]{3,2,1,0:T(8,128)} copy-done((f32[14,8,16,256]{3,2,1,0:T(8,128)}, f32[14,8,16,256]{3,2,1,0:T(8,128)S(1)}, u32[]{:S(2)}) %copy-start.2) | copy-done | bytes 1835032
  31.3 0.0 collective-permute-done.3.after_ref
  31.3 0.0 collective-permute-done.2.before_ref
  31.4 0.0 copy-start.1
  31.4 2.5 %shard_map.90 = f32[8,16384]{1,0:T(8,128)} custom-call(f32[8,16384]{1,0:T(8,128)S(1)} %copy-done.7, bf16[256,2048]{1,0:T(8,128)(2,1)S(1)} %copy-done.6, s32[2,1024]{1,0:T(2,128)S(1)} %copy-done.5, f32[17,16,256]{2,1,0:T(8,128)S(1)} %collective-permute-done.2.before_ref, f32[17,16,256]{2,1,0:T(8,128)S(1)} %collective-permute-done.3.after_ref), custom_call_target="tpu_custom_call" | custom-call | flops 1073741824 | bytes 3145728 | tf_op jit(solution)/shard_map/pallas_call | solution.py:26
  33.8 0.0 all-to-all-done
  33.9 0.0 copy-start.3
  33.9 1.5 %copy-done.3 = f32[14,8,16,256]{3,2,1,0:T(8,128)S(1)} copy-done((f32[14,8,16,256]{3,2,1,0:T(8,128)S(1)}, f32[14,8,16,256]{3,2,1,0:T(8,128)}, u32[]{:S(2)}) %copy-start.3) | copy-done | bytes 1835032
  35.4 8.5 %shard_map.89 = f32[14,8,16,256]{3,2,1,0:T(8,128)} custom-call(f32[17,8,16,256]{3,2,1,0:T(8,128)S(1)} %copy-done.1, f32[14,8,16,256]{3,2,1,0:T(8,128)S(1)} %copy-done.3, f32[17,16,256]{2,1,0:T(8,128)S(1)} %collective-permute-done.2.before_ref, f32[17,16,256]{2,1,0:T(8,128)S(1)} %collective-permute-done.3.after_ref, ...), custom_call_target="tpu_custom_call" | custom-call | flops 4294967296 | bytes 6291456 | tf_op jit(solution)/shard_map/pallas_call | solution.py:26
  (11 shorter events, 0.0 us)
Async XLA Ops:
  4.5 26.8 %collective-permute-start.3 = (f32[17,16,256]{2,1,0:T(8,128)}, f32[17,16,256]{2,1,0:T(8,128)S(1)}, u32[]{:S(2)}, u32[]{:S(2)}) collective-permute-start(f32[17,16,256]{2,1,0:T(8,128)} %get-tuple-element.11), channel_id=1, source_target_pairs={{4,0},{8,4},{12,8},{16,12},{20,16},{24,20},{28,24},{0,28},{5,1},{9... | collective-permute-start | bytes 835592 | tf_op jit(solution)/shard_map/ppermute | solution.py:550
  9.7 21.6 %collective-permute-start.2 = (f32[17,16,256]{2,1,0:T(8,128)}, f32[17,16,256]{2,1,0:T(8,128)S(1)}, u32[]{:S(2)}, u32[]{:S(2)}) collective-permute-start(f32[17,16,256]{2,1,0:T(8,128)} %get-tuple-element.10.unused), channel_id=1, source_target_pairs={{0,4},{4,8},{8,12},{12,16},{16,20},{20,24},{24,28},{28,0},{1,5},{5... | collective-permute-start | bytes 835592 | tf_op jit(solution)/shard_map/ppermute | solution.py:549
  9.7 9.8 %copy-start.9 = (f32[15,8,256]{2,1,0:T(8,128)S(1)}, f32[15,8,256]{2,1,0:T(8,128)}, u32[]{:S(2)}) copy-start(f32[15,8,256]{2,1,0:T(8,128)} %get-tuple-element.8) | copy-start | bytes 368644
  9.7 11.5 %copy-start.8 = (f32[15,8,256]{2,1,0:T(8,128)S(1)}, f32[15,8,256]{2,1,0:T(8,128)}, u32[]{:S(2)}) copy-start(f32[15,8,256]{2,1,0:T(8,128)} %get-tuple-element.9) | copy-start | bytes 368644
  9.7 16.7 %copy-start.4 = (f32[8]{0:T(128)S(1)}, f32[8]{0:T(128)}, u32[]{:S(2)}) copy-start(f32[8]{0:T(128)} %rate_ref.3) | copy-start | bytes 100
  12.8 21.0 %all-to-all-start = ((f32[32,1,1152]{2,1,0:T(1,128)}), f32[32,1,1152]{2,1,0:T(1,128)S(1)}, u32[]{:S(2)}, u32[]{:S(2)}) async-start(f32[32,1,1152]{2,1,0:T(1,128)} %bitcast.5), calls=%async_computation | async-start | bytes 294912 | tf_op jit(solution)/shard_map/all_to_all | solution.py:559
  19.5 5.2 %collective-permute-start = (f32[15,8,256]{2,1,0:T(8,128)S(1)}, f32[15,8,256]{2,1,0:T(8,128)S(1)}, u32[]{:S(2)}, u32[]{:S(2)}) collective-permute-start(f32[15,8,256]{2,1,0:T(8,128)S(1)} %copy-done.9), channel_id=1, source_target_pairs={{0,1},{1,2},{2,3},{3,0},{4,5},{5,6},{6,7},{7,4},{8,9},{9,10},{10,1... | collective-permute-start | bytes 368648 | tf_op jit(solution)/shard_map/ppermute | solution.py:551
  21.2 5.2 %collective-permute-start.1 = (f32[15,8,256]{2,1,0:T(8,128)S(1)}, f32[15,8,256]{2,1,0:T(8,128)S(1)}, u32[]{:S(2)}, u32[]{:S(2)}) collective-permute-start(f32[15,8,256]{2,1,0:T(8,128)S(1)} %copy-done.8), channel_id=1, source_target_pairs={{1,0},{2,1},{3,2},{0,3},{5,4},{6,5},{7,6},{4,7},{9,8},{10,9},{11,1... | collective-permute-start | bytes 368648 | tf_op jit(solution)/shard_map/ppermute | solution.py:552
  26.4 1.6 %copy-start = (f32[17,8,16,256]{3,2,1,0:T(8,128)S(1)}, f32[17,8,16,256]{3,2,1,0:T(8,128)}, u32[]{:S(2)}) copy-start(f32[17,8,16,256]{3,2,1,0:T(8,128)} %cells_ref.3) | copy-start | bytes 6684676
  28.1 3.3 %copy-start.5 = (s32[2,1024]{1,0:T(2,128)S(1)}, s32[2,1024]{1,0:T(2,128)}, u32[]{:S(2)}) copy-start(s32[2,1024]{1,0:T(2,128)} %crossing_ref.1) | copy-start | bytes 24580
  28.1 3.3 %copy-start.6 = (bf16[256,2048]{1,0:T(8,128)(2,1)S(1)}, bf16[256,2048]{1,0:T(8,128)(2,1)}, u32[]{:S(2)}) copy-start(bf16[256,2048]{1,0:T(8,128)(2,1)} %get-tuple-element.13.hot_ref) | copy-start | bytes 3145732
  28.1 3.3 %copy-start.7 = (f32[8,16384]{1,0:T(8,128)S(1)}, f32[8,16384]{1,0:T(8,128)}, u32[]{:S(2)}) copy-start(f32[8,16384]{1,0:T(8,128)} %get-tuple-element.12.advanced_ref) | copy-start | bytes 1572868
  30.1 1.2 %copy-start.2 = (f32[14,8,16,256]{3,2,1,0:T(8,128)}, f32[14,8,16,256]{3,2,1,0:T(8,128)S(1)}, u32[]{:S(2)}) copy-start(f32[14,8,16,256]{3,2,1,0:T(8,128)S(1)} %shard_map.87.inner_ref) | copy-start | bytes 5505028
  31.4 2.5 %copy-start.1 = (f32[17,8,16,256]{3,2,1,0:T(8,128)S(1)}, f32[17,8,16,256]{3,2,1,0:T(8,128)}, u32[]{:S(2)}) copy-start(f32[17,8,16,256]{3,2,1,0:T(8,128)} %cells_ref.3) | copy-start | bytes 6684676
  33.9 1.5 %copy-start.3 = (f32[14,8,16,256]{3,2,1,0:T(8,128)S(1)}, f32[14,8,16,256]{3,2,1,0:T(8,128)}, u32[]{:S(2)}) copy-start(f32[14,8,16,256]{3,2,1,0:T(8,128)} %copy-done.2) | copy-start | bytes 5505028

commit v8 on v5

--- a/solution.py
+++ b/solution.py
@@ -12,7 +12,6 @@
 COUNT = SECTIONS + SPECIES
 LANES = 128
 WIDE = 256
-WINDOW = 4
 F32 = jnp.float32
 BF16 = jnp.bfloat16
 ANY = pl.BlockSpec(memory_space=pl.ANY)
@@ -22,7 +21,7 @@
 MOST = 32 << 20
 
 
-def call(kernel, out_shape, operands, scratch, in_specs=None, out_specs=ANY, flops=0, moved_bytes=0, grant=MOST):
+def call(kernel, out_shape, operands, scratch, in_specs=None, out_specs=ANY, aliases=None, flops=0, moved_bytes=0, grant=MOST):
     many = isinstance(out_shape, (list, tuple))
     return pl.pallas_call(
         kernel,
@@ -30,6 +29,7 @@
         in_specs=in_specs or [ANY] * len(operands),
         out_specs=[out_specs] * len(out_shape) if many else out_specs,
         scratch_shapes=scratch,
+        input_output_aliases=aliases or {},
         compiler_params=pltpu.CompilerParams(vmem_limit_bytes=grant),
         cost_estimate=pl.CostEstimate(flops=flops, bytes_accessed=moved_bytes, transcendentals=0),
     )(*operands)
@@ -366,47 +366,108 @@
         write(c, moved(c))
 
 
-def cells_kernel(
-    cells_ref, before_ref, after_ref, low_ref, high_ref, deposit_ref, rate_ref, out_hbm, out_ref, sems
+def inner_kernel(
+    cells_hbm, low_ref, high_ref, deposit_ref, rate_ref, out_hbm, token_hbm, cells_ref, out_ref, token_ref, in_sems, sems
 ):
-    size_x = cells_ref.shape[1]
+    size_x = cells_hbm.shape[1]
     last = size_x - 1
+
+    def fetch(x):
+        return pltpu.make_async_copy(cells_hbm.at[:, x], cells_ref.at[:, x], in_sems.at[x])
+
+    for x in range(size_x):
+        fetch(x).start()
+    token_ref[...] = jnp.zeros(token_ref.shape, F32)
+    token = pltpu.make_async_copy(token_ref, token_hbm, sems.at[0])
+    token.start()
+    fetch(0).wait()
+    fetch(1).wait()
 
     def store(x):
         return pltpu.make_async_copy(out_ref.at[:, x], out_hbm.at[:, x], sems.at[x])
 
-    def layer(left, x, right):
+    def middle(x, unused):
+        fetch(x + 1).wait()
+
         def write(c, value):
             out_ref[c, x] = value + deposit_ref[c, x] if c < SECTIONS else value
 
         slab_update(
-            left,
+            lambda c: cells_ref[c, x - 1],
             lambda c: cells_ref[c, x],
-            right,
+            lambda c: cells_ref[c, x + 1],
             lambda c: low_ref[c, pl.ds(x, 1), :],
             lambda c: high_ref[c, pl.ds(x, 1), :],
             rate_ref,
             write,
         )
         store(x).start()
-
-    def middle(x, unused):
-        layer(lambda c: cells_ref[c, x - 1], x, lambda c: cells_ref[c, x + 1])
         return unused
 
     lax.fori_loop(1, last, middle, 0)
-    layer(lambda c: before_ref[c], 0, lambda c: cells_ref[c, 1])
-    layer(lambda c: cells_ref[c, last - 1], last, lambda c: after_ref[c])
-    for x in range(size_x):
+    for x in range(1, last):
         store(x).wait()
-
-
-def update_cells(cells, before, after, low, high, deposited, rate):
+    token.wait()
+
+
+def inner(cells, low, high, deposited, rate):
     out = jax.ShapeDtypeStruct((COUNT,) + cells.shape[1:], F32)
+    token = jax.ShapeDtypeStruct((8, LANES), F32)
     return call(
-        cells_kernel, out, (cells, before, after, low, high, deposited, rate),
-        [pltpu.VMEM(out.shape, F32), pltpu.SemaphoreType.DMA((cells.shape[1],))],
-        in_specs=[VMEM] * 6 + [SMEM], flops=30 << 20, moved_bytes=4 << 20,
+        inner_kernel, [out, token], (cells, low, high, deposited, rate),
+        [pltpu.VMEM(a.shape, F32) for a in (cells, out, token)] + [pltpu.SemaphoreType.DMA((cells.shape[1],))] * 2,
+        in_specs=[ANY] + [VMEM] * 3 + [SMEM], flops=30 << 20, moved_bytes=4 << 20,
+    )
+
+
+def edge_kernel(
+    cells_hbm, inner_hbm, before_ref, after_ref, low_ref, high_ref, deposit_ref, rate_ref, out_hbm,
+    cells_ref, out_ref, sems,
+):
+    last = cells_hbm.shape[1] - 1
+    copies = [
+        pltpu.make_async_copy(cells_hbm.at[:, 0:2], cells_ref.at[:, 0:2], sems.at[0]),
+        pltpu.make_async_copy(cells_hbm.at[:, last - 1 : last + 1], cells_ref.at[:, 2:4], sems.at[1]),
+        pltpu.make_async_copy(out_ref.at[:, 0], out_hbm.at[:, 0], sems.at[2]),
+        pltpu.make_async_copy(out_ref.at[:, 1], out_hbm.at[:, last], sems.at[3]),
+    ]
+    copies[0].start()
+    copies[1].start()
+
+    def layer(left, number, x, right):
+        def write(c, value):
+            out_ref[c, number] = value + deposit_ref[c, x] if c < SECTIONS else value
+
+        slab_update(
+            left,
+            lambda c: cells_ref[c, 3 * number],
+            right,
+            lambda c: low_ref[c, x : x + 1, :],
+            lambda c: high_ref[c, x : x + 1, :],
+            rate_ref,
+            write,
+        )
+        copies[2 + number].start()
+
+    copies[0].wait()
+    layer(lambda c: before_ref[c], 0, 0, lambda c: cells_ref[c, 1])
+    copies[1].wait()
+    layer(lambda c: cells_ref[c, 2], 1, last, lambda c: after_ref[c])
+    copies[2].wait()
+    copies[3].wait()
+
+
+def edges(cells, inner_cells, before, after, low, high, deposited, rate):
+    size_y, size_z = cells.shape[2:]
+    return call(
+        edge_kernel, jax.ShapeDtypeStruct(inner_cells.shape, F32),
+        (cells, inner_cells, before, after, low, high, deposited, rate),
+        [
+            pltpu.VMEM((cells.shape[0], 4, size_y, size_z), F32),
+            pltpu.VMEM((COUNT, 2, size_y, size_z), F32),
+            pltpu.SemaphoreType.DMA((4,)),
+        ],
+        in_specs=[ANY, ANY] + [VMEM] * 5 + [SMEM], aliases={1: 0}, flops=10 << 20, moved_bytes=2 << 20,
     )
 
 
@@ -414,7 +475,7 @@
     return value >> (count.bit_length() - 1) if count & (count - 1) == 0 else value // count
 
 
-def deposit_kernel(shape, routed_ref, out_ref, total_ref, mass_ref, spread_ref, depth_ref):
+def deposit_kernel(shape, windows, routed_ref, out_ref, mass_ref, spread_ref, depth_ref):
     size_x, size_y, size_z = shape
     groups = routed_ref.shape[0] // 9
     per = groups // 8
@@ -438,67 +499,63 @@
         valid = cell >= 0
         bounds.append((jnp.min(jnp.where(valid, layer, size_x)), jnp.max(jnp.where(valid, layer, -1))))
 
-    half = SECTIONS * WINDOW * size_y
     zero = jnp.zeros((size_y, LANES), BF16)
 
-    def spread(q, first):
+    def deposit(q, start):
+        window = windows[q]
+        half = SECTIONS * window * size_y
+        first = jnp.minimum(start, size_x - window)
         cell = mass_ref[q, SECTIONS].astype(jnp.int32)
         plane = quotient(cell, size_z)
         depth = cell - plane * size_z
-        plane = jnp.where(cell >= 0, plane - first * size_y, -1).astype(F32)
+        plane = jnp.where(plane >= start * size_y, plane - first * size_y, -1)
+        plane = jnp.where(cell >= 0, plane, -1).astype(F32)
         parts = [split(mass_ref[q, s]) for s in range(SECTIONS)]
         for i in range(8):
             at = slice(i * LANES, (i + 1) * LANES)
             depth_ref[q % 2, :, at] = hot_columns(depth[i : i + 1], size_z)
             plane_rows = rows_of(plane[i : i + 1], size_y)
             rows = [[rows_of(part[i : i + 1].astype(F32), size_y) for part in pair] for pair in parts]
-            for w in range(WINDOW):
+            for w in range(window):
                 hit = plane_rows == packed(iota((size_y, LANES), 0) + w * size_y)
                 for s in range(SECTIONS):
-                    base = (s * WINDOW + w) * size_y
+                    base = (s * window + w) * size_y
                     for part in range(2):
                         spread_ref[q % 2, part * half + base : part * half + base + size_y, at] = jnp.where(
                             hit, rows[s][part], zero
                         )
-
-    def deposit(q, first):
-        added = contract_lanes(spread_ref[q % 2], depth_ref[q % 2])
+        added = contract_lanes(spread_ref[q % 2, : 2 * half], depth_ref[q % 2])
         for s in range(SECTIONS):
-            base = s * WINDOW * size_y
-            rows = added[base : base + WINDOW * size_y] + added[half + base : half + base + WINDOW * size_y]
-            at = pl.ds(first, WINDOW)
-            total_ref[s, at] = total_ref[s, at] + rows.reshape(WINDOW, size_y, size_z)
-
-    total_ref[...] = jnp.zeros(total_ref.shape, F32)
+            base = s * window * size_y
+            rows = added[base : base + window * size_y] + added[half + base : half + base + window * size_y]
+            at = pl.ds(first, window)
+            out_ref[s, at] = out_ref[s, at] + rows.reshape(window, size_y, size_z)
+
+    out_ref[...] = jnp.zeros(out_ref.shape, F32)
     for q in range(per):
-        first = jnp.minimum(bounds[q][0], size_x - 1)
-        spread(q, first)
-        deposit(q, first)
+        deposit(q, bounds[q][0] if windows[q] < size_x else 0)
     for q in range(per):
-        low, high = bounds[q]
-
-        def more(t, unused, q=q, low=low):
-            first = low + t * WINDOW
-            spread(q, first)
-            deposit(q, first)
-            return unused
-
-        lax.fori_loop(1, quotient(high - low + WINDOW, WINDOW), more, 0)
-    out_ref[...] = total_ref[:, 0:size_x]
-
-
-def deposit(routed, shape):
+        if windows[q] < size_x:
+            low, high = bounds[q]
+
+            def more(t, unused, q=q, low=low):
+                deposit(q, low + t * windows[q])
+                return unused
+
+            lax.fori_loop(1, jnp.where(high - low < windows[q], 1, 1 + (size_x - 1) // windows[q]), more, 0)
+
+
+def deposit(routed, shape, windows):
     size_x, size_y, size_z = shape
     per = routed.shape[0] // 9 // 8
     return call(
-        functools.partial(deposit_kernel, shape), jax.ShapeDtypeStruct((SECTIONS,) + shape, F32), (routed,),
+        functools.partial(deposit_kernel, shape, windows), jax.ShapeDtypeStruct((SECTIONS,) + shape, F32), (routed,),
         [
-            pltpu.VMEM((SECTIONS, size_x + WINDOW - 1, size_y, size_z), F32),
             pltpu.VMEM((per, SECTIONS + 1, 8, LANES), F32),
-            pltpu.VMEM((2, 2 * SECTIONS * WINDOW * size_y, 8 * LANES), BF16),
+            pltpu.VMEM((2, 2 * SECTIONS * max(windows) * size_y, 8 * LANES), BF16),
             pltpu.VMEM((2, size_z, 8 * LANES), BF16),
         ],
-        in_specs=[VMEM], out_specs=VMEM, flops=4 << 30, moved_bytes=2 << 20,
+        in_specs=[VMEM], out_specs=VMEM, flops=1 << 30, moved_bytes=2 << 20,
     )
 
 
@@ -528,9 +585,11 @@
     routed = lax.all_to_all(filled, ("gx", "gy"), split_axis=0, concat_axis=0, tiled=True)
     routed = routed.reshape(-1, fold, 9, capacity).transpose(0, 2, 1, 3).reshape(-1, LANES)
 
-    deposited = deposit(routed, cell_state.shape[1:])
-    new_parcels = arrive(deposited, advanced, hot, crossing, before, after)
-    new_cells = update_cells(cell_state, before, after, low, high, deposited, evap_rate)
+    windows = [cell_state.shape[1]] * (routed.shape[0] // 9 // 8)
+    deposited = deposit(routed, cell_state.shape[1:], windows)
+    inner_cells, token = inner(cell_state, low, high, deposited, evap_rate)
+    new_parcels = arrive(token, advanced, hot, crossing, before, after)
+    new_cells = edges(cell_state, inner_cells, before, after, low, high, deposited, evap_rate)
     return (new_cells, new_parcels)
 
 

time: 38.2 us -> 37 us (0.969)
  waiting for transfers between devices: 3.2 us -> 1.92 us
    ppermute x1, waiting for transfers between devices: 1.29 us -> 0.01 us  [on_device(): after = lax.ppermute(send_down, 'gx', down_x)]
    pallas_call x4 -> x5, Pallas kernels: 20 us -> 19.8 us  [call(): pl.pallas_call(kernel, out_shape=out_shape, in_specs=in_specs or [ANY] *...]
  transfers between devices with their start and end apart: 5 -> 5, of which waited for: 2 -> 1; matrix products, arithmetic and copies ran while one was open for 0% -> 0% of each run, Pallas kernels for 30% -> 28%
where the time goes in v8:
time: 37 us; the launch traced here: 36.4 us
  Pallas kernels  19.8 us (54%)
  starting transfers between devices  13.8 us (37%)
  waiting for transfers between devices  1.92 us (5%)
  between operations  0.77 us (2%)
    pallas_call x5, Pallas kernels, call(): pl.pallas_call(kernel, out_shape=out_shape, in_specs=in_specs or [ANY] *...  19.8 us
    all_to_all x1, starting transfers between devices, on_device(): lax.all_to_all(filled, ('gx', 'gy'), split_axis=0, concat_axis=0, tiled=T...  7.3 us
    ppermute x1, starting transfers between devices, on_device(): after = lax.ppermute(send_down, 'gx', down_x)  2.95 us
    all_to_all x1, waiting for transfers between devices, on_device(): lax.all_to_all(filled, ('gx', 'gy'), split_axis=0, concat_axis=0, tiled=T...  1.91 us
    ppermute x1, starting transfers between devices, on_device(): before = lax.ppermute(send_up, 'gx', up_x)  1.82 us
    ppermute x1, starting transfers between devices, on_device(): high = lax.ppermute(side_down, 'gy', down_y)  1.74 us
  transfers between devices with their start and end apart: 5, of which 1 were waited for; matrix products, arithmetic and copies ran while one was open for 0% of the time, Pallas kernels for 28%

profile of v8, /device:TPU:0, one launch (start us, length us, event | category | flops | bytes accessed | tf_op | source)
XLA Modules:
  0.0 36.4 jit_solution(16145194536250515734)
XLA Ops:
  0.6 5.4 %shard_map.86 = (f32[17,16,256]{2,1,0:T(8,128)}, f32[17,16,256]{2,1,0:T(8,128)}, f32[15,8,256]{2,1,0:T(8,128)}, f32[15,8,256]{2,1,0:T(8,128)}, f32[8,16384]{1,0:...) custom-call(f32[17,8,16,256]{3,2,1,0:T(8,128)} %cells_hbm.5, f32[8,16384]{1,0:T(8,128)} %parcels_hbm.1, ...), custom_call_target="tpu_custom_call" | custom-call | flops 2147483648 | bytes 6291456 | tf_op jit(solution)/shard_map/pallas_call | solution.py:26
  6.0 7.3 %all-to-all-start = ((f32[32,1,1152]{2,1,0:T(1,128)}), f32[32,1,1152]{2,1,0:T(1,128)S(1)}, u32[]{:S(2)}, u32[]{:S(2)}) async-start(f32[32,1,1152]{2,1,0:T(1,128)} %bitcast.5), calls=%async_computation | async-start | bytes 294912 | tf_op jit(solution)/shard_map/all_to_all | solution.py:585
  13.3 1.8 %collective-permute-start.2 = (f32[17,16,256]{2,1,0:T(8,128)}, f32[17,16,256]{2,1,0:T(8,128)S(1)}, u32[]{:S(2)}, u32[]{:S(2)}) collective-permute-start(f32[17,16,256]{2,1,0:T(8,128)} %get-tuple-element.15), channel_id=1, source_target_pairs={{0,4},{4,8},{8,12},{12,16},{16,20},{20,24},{24,28},{28,0},{1,5},{5... | collective-permute-start | bytes 835592 | tf_op jit(solution)/shard_map/ppermute | solution.py:578
  15.2 3.0 %collective-permute-start.3 = (f32[17,16,256]{2,1,0:T(8,128)}, f32[17,16,256]{2,1,0:T(8,128)S(1)}, u32[]{:S(2)}, u32[]{:S(2)}) collective-permute-start(f32[17,16,256]{2,1,0:T(8,128)} %get-tuple-element.16), channel_id=1, source_target_pairs={{4,0},{8,4},{12,8},{16,12},{20,16},{24,20},{28,24},{0,28},{5,1},{9... | collective-permute-start | bytes 835592 | tf_op jit(solution)/shard_map/ppermute | solution.py:579
  18.1 0.0 collective-permute-start
  18.1 1.7 %collective-permute-start.1 = (f32[15,8,256]{2,1,0:T(8,128)}, f32[15,8,256]{2,1,0:T(8,128)S(1)}, u32[]{:S(2)}, u32[]{:S(2)}) collective-permute-start(f32[15,8,256]{2,1,0:T(8,128)} %get-tuple-element.12), channel_id=1, source_target_pairs={{1,0},{2,1},{3,2},{0,3},{5,4},{6,5},{7,6},{4,7},{9,8},{10,9},{11,1... | collective-permute-start | bytes 368648 | tf_op jit(solution)/shard_map/ppermute | solution.py:581
  19.9 1.9 %all-to-all-done = f32[32,1,1152]{2,1,0:T(1,128)S(1)} async-done(((f32[32,1,1152]{2,1,0:T(1,128)}), f32[32,1,1152]{2,1,0:T(1,128)S(1)}, u32[]{:S(2)}, u32[]{:S(2)}) %all-to-all-start) | async-done | bytes 147488 | tf_op jit(solution)/shard_map/all_to_all | solution.py:585
  21.8 0.0 copy-start
  21.8 7.2 %shard_map.87.deposit_ref = f32[8,8,16,256]{3,2,1,0:T(8,128)S(1)} custom-call(f32[288,128]{1,0:T(8,128)S(1)} %bitcast.4), custom_call_target="tpu_custom_call" | custom-call | flops 1073741824 | bytes 2097152 | tf_op jit(solution)/shard_map/pallas_call | solution.py:26
  29.0 0.0 collective-permute-done.low_ref
  29.0 0.0 collective-permute-done.1.high_ref
  29.0 0.0 copy-done
  29.0 0.0 copy-done.1
  29.0 3.0 %shard_map.88 = (f32[14,8,16,256]{3,2,1,0:T(8,128)}, f32[8,128]{1,0:T(8,128)S(1)}) custom-call(f32[17,8,16,256]{3,2,1,0:T(8,128)S(1)} %copy-done, f32[15,8,256]{2,1,0:T(8,128)S(1)} %collective-permute-done.low_ref, f32[15,8,256]{2,1,0:T(8,128)S(1)} %collective-permute-done.1.high_ref, f32[8,8,16,256]{3,2,1,0:T(8,128)S(1)} %shard_map.87.deposit_ref, ...), custom_call_target="tpu_custom_call" | custom-call | flops 31457280 | bytes 4194304 | tf_op jit(solution)/shard_map/pallas_call | solution.py:26
  32.0 0.0 collective-permute-done.2.before_ref
  32.0 0.0 collective-permute-done.3.after_ref
  32.0 0.0 copy-start.2
  32.0 0.0 copy-start.3
  32.0 0.0 copy-start.4
  32.0 1.8 %shard_map.89 = f32[14,8,16,256]{3,2,1,0:T(8,128)} custom-call(f32[17,8,16,256]{3,2,1,0:T(8,128)S(1)} %copy-done, f32[14,8,16,256]{3,2,1,0:T(8,128)} %get-tuple-element.14.inner_hbm, f32[17,16,256]{2,1,0:T(8,128)S(1)} %collective-permute-done.2.before_ref, f32[17,16,256]{2,1,0:T(8,128)S(1)} %collective-permute-done.3.after_ref, ...), custom_call_target="tpu_custom_call", output_to_operand_aliasing={{}: (1, {})} | custom-call | flops 10485760 | bytes 2097152 | tf_op jit(solution)/shard_map/pallas_call | solution.py:26
  33.9 0.0 copy-done.2
  33.9 0.0 copy-done.3
  33.9 0.0 copy-done.4
  33.9 2.5 %shard_map.90 = f32[8,16384]{1,0:T(8,128)} custom-call(f32[8,128]{1,0:T(8,128)S(1)} %get-tuple-element.17.unused, f32[8,16384]{1,0:T(8,128)S(1)} %copy-done.4, bf16[256,2048]{1,0:T(8,128)(2,1)S(1)} %copy-done.3, s32[2,1024]{1,0:T(2,128)S(1)} %copy-done.2, f32[17,16,256]{2,1,0:T(8,128)S(1)} %collective-permute-done.2.before_ref, ...), custom_call_target="tpu_custom_call" | custom-call | flops 1073741824 | bytes 3145728 | tf_op jit(solution)/shard_map/pallas_call | solution.py:26
  (1 shorter events, 0.0 us)
Async XLA Ops:
  6.0 15.7 %all-to-all-start = ((f32[32,1,1152]{2,1,0:T(1,128)}), f32[32,1,1152]{2,1,0:T(1,128)S(1)}, u32[]{:S(2)}, u32[]{:S(2)}) async-start(f32[32,1,1152]{2,1,0:T(1,128)} %bitcast.5), calls=%async_computation | async-start | bytes 294912 | tf_op jit(solution)/shard_map/all_to_all | solution.py:585
  13.3 18.6 %collective-permute-start.2 = (f32[17,16,256]{2,1,0:T(8,128)}, f32[17,16,256]{2,1,0:T(8,128)S(1)}, u32[]{:S(2)}, u32[]{:S(2)}) collective-permute-start(f32[17,16,256]{2,1,0:T(8,128)} %get-tuple-element.15), channel_id=1, source_target_pairs={{0,4},{4,8},{8,12},{12,16},{16,20},{20,24},{24,28},{28,0},{1,5},{5... | collective-permute-start | bytes 835592 | tf_op jit(solution)/shard_map/ppermute | solution.py:578
  15.2 16.8 %collective-permute-start.3 = (f32[17,16,256]{2,1,0:T(8,128)}, f32[17,16,256]{2,1,0:T(8,128)S(1)}, u32[]{:S(2)}, u32[]{:S(2)}) collective-permute-start(f32[17,16,256]{2,1,0:T(8,128)} %get-tuple-element.16), channel_id=1, source_target_pairs={{4,0},{8,4},{12,8},{16,12},{20,16},{24,20},{28,24},{0,28},{5,1},{9... | collective-permute-start | bytes 835592 | tf_op jit(solution)/shard_map/ppermute | solution.py:579
  18.1 10.9 %collective-permute-start = (f32[15,8,256]{2,1,0:T(8,128)}, f32[15,8,256]{2,1,0:T(8,128)S(1)}, u32[]{:S(2)}, u32[]{:S(2)}) collective-permute-start(f32[15,8,256]{2,1,0:T(8,128)} %get-tuple-element.11), channel_id=1, source_target_pairs={{0,1},{1,2},{2,3},{3,0},{4,5},{5,6},{6,7},{7,4},{8,9},{9,10},{10,1... | collective-permute-start | bytes 368648 | tf_op jit(solution)/shard_map/ppermute | solution.py:580
  18.1 10.9 %collective-permute-start.1 = (f32[15,8,256]{2,1,0:T(8,128)}, f32[15,8,256]{2,1,0:T(8,128)S(1)}, u32[]{:S(2)}, u32[]{:S(2)}) collective-permute-start(f32[15,8,256]{2,1,0:T(8,128)} %get-tuple-element.12), channel_id=1, source_target_pairs={{1,0},{2,1},{3,2},{0,3},{5,4},{6,5},{7,6},{4,7},{9,8},{10,9},{11,1... | collective-permute-start | bytes 368648 | tf_op jit(solution)/shard_map/ppermute | solution.py:581
  21.8 7.2 %copy-start = (f32[17,8,16,256]{3,2,1,0:T(8,128)S(1)}, f32[17,8,16,256]{3,2,1,0:T(8,128)}, u32[]{:S(2)}) copy-start(f32[17,8,16,256]{3,2,1,0:T(8,128)} %cells_hbm.5) | copy-start | bytes 6684676
  21.8 7.2 %copy-start.1 = (f32[8]{0:T(128)S(1)}, f32[8]{0:T(128)}, u32[]{:S(2)}) copy-start(f32[8]{0:T(128)} %rate_ref.3) | copy-start | bytes 100
  32.0 1.9 %copy-start.2 = (s32[2,1024]{1,0:T(2,128)S(1)}, s32[2,1024]{1,0:T(2,128)}, u32[]{:S(2)}) copy-start(s32[2,1024]{1,0:T(2,128)} %crossing_ref.1) | copy-start | bytes 24580
  32.0 1.9 %copy-start.3 = (bf16[256,2048]{1,0:T(8,128)(2,1)S(1)}, bf16[256,2048]{1,0:T(8,128)(2,1)}, u32[]{:S(2)}) copy-start(bf16[256,2048]{1,0:T(8,128)(2,1)} %get-tuple-element.19.hot_ref) | copy-start | bytes 3145732
  32.0 1.9 %copy-start.4 = (f32[8,16384]{1,0:T(8,128)S(1)}, f32[8,16384]{1,0:T(8,128)}, u32[]{:S(2)}) copy-start(f32[8,16384]{1,0:T(8,128)} %get-tuple-element.18.advanced_ref) | copy-start | bytes 1572868

commit v9 on v8

--- a/solution.py
+++ b/solution.py
@@ -12,6 +12,7 @@
 COUNT = SECTIONS + SPECIES
 LANES = 128
 WIDE = 256
+GROUPS = 4
 F32 = jnp.float32
 BF16 = jnp.bfloat16
 ANY = pl.BlockSpec(memory_space=pl.ANY)
@@ -39,6 +40,10 @@
     return lax.broadcasted_iota(jnp.int32, shape, axis)
 
 
+def quotient(value, count):
+    return value >> (count.bit_length() - 1) if count & (count - 1) == 0 else value // count
+
+
 def packed(value):
     return value.astype(F32).astype(BF16)
 
@@ -84,25 +89,33 @@
         left_ref[8 * (uppers + u) : 8 * (uppers + u) + 16, at] = jnp.where(hit, twice_fine, zero)
 
 
-def bucket_into(owner_total, capacity, mass_ref, owner_ref, cell_ref, out_ref, left_ref, hot_ref):
+def bucket_into(owner_total, capacity, cell_total, mass_ref, owner_ref, cell_ref, out_ref, left_ref, hot_ref):
     blocks = owner_ref.shape[0]
     uppers = out_ref.shape[0] // 9 // 2
     strict = iota((LANES, 2 * LANES), 0) < iota((LANES, 2 * LANES), 1)
     strict = jnp.where(strict, 1.0, 0.0).astype(BF16)
     owners = owner_ref[...]
     cells = cell_ref[...]
+    keys = owner_total * GROUPS
+    order = owners * GROUPS + quotient(cells, cell_total // GROUPS)
     hots = [
-        jnp.where(jnp.broadcast_to(owners[b : b + 1], (owner_total, LANES)) == iota((owner_total, LANES), 0), 1.0, 0.0)
+        jnp.where(jnp.broadcast_to(order[b : b + 1], (keys, LANES)) == iota((keys, LANES), 0), 1.0, 0.0)
         for b in range(blocks)
     ]
     ranks = jnp.dot(jnp.concatenate(hots, axis=0).astype(BF16), strict, preferred_element_type=F32)
-    carry = jnp.zeros((owner_total, LANES), F32)
+    parts = [ranks[b * keys : (b + 1) * keys] for b in range(blocks)]
+    counts = sum(part[:, LANES:] for part in parts)
+    key, other = iota((keys, keys), 0), iota((keys, keys), 1)
+    same = quotient(key, GROUPS) == quotient(other, GROUPS)
+    sums = jnp.concatenate([jnp.where(same & (other < key), 1.0, 0.0), jnp.where(same, 1.0, 0.0)], axis=0).astype(BF16)
+    sums = jnp.dot(sums, counts.astype(BF16), preferred_element_type=F32)
+    carry, owned = sums[:keys], sums[keys:]
     base = 16 * uppers
     for b in range(blocks):
-        part = ranks[b * owner_total : (b + 1) * owner_total]
-        rank = jnp.sum(hots[b] * (part[:, :LANES] + carry), axis=0, keepdims=True).astype(jnp.int32)
-        carry = carry + part[:, LANES:]
-        spot = owners[b : b + 1] * capacity + rank
+        rank = jnp.sum(hots[b] * (parts[b][:, :LANES] + carry), axis=0, keepdims=True)
+        total = jnp.sum(hots[b] * owned, axis=0, keepdims=True)
+        carry = carry + parts[b][:, LANES:]
+        spot = owners[b : b + 1] * capacity + ((rank * float(capacity) + 0.5) / total).astype(jnp.int32)
         at = slice(b * LANES, (b + 1) * LANES)
         hot_ref[:, at] = hot_columns(spot & (WIDE - 1), WIDE)
         coarse, fine = split(mass_ref[:, at])
@@ -222,7 +235,7 @@
     copies[14].start()
     for copy in copies[1:4]:
         copy.wait()
-    bucket_into(owner_total, capacity, mass_ref, owner_ref, cell_ref, filled_ref, left_ref, spot_ref)
+    bucket_into(owner_total, capacity, size_x * size_y * size_z, mass_ref, owner_ref, cell_ref, filled_ref, left_ref, spot_ref)
     copies[8].start()
     for copy in copies[6:]:
         copy.wait()
@@ -367,28 +380,17 @@
 
 
 def inner_kernel(
-    cells_hbm, low_ref, high_ref, deposit_ref, rate_ref, out_hbm, token_hbm, cells_ref, out_ref, token_ref, in_sems, sems
+    cells_ref, low_ref, high_ref, deposit_ref, rate_ref, out_hbm, token_hbm, out_ref, token_ref, sems
 ):
-    size_x = cells_hbm.shape[1]
-    last = size_x - 1
-
-    def fetch(x):
-        return pltpu.make_async_copy(cells_hbm.at[:, x], cells_ref.at[:, x], in_sems.at[x])
-
-    for x in range(size_x):
-        fetch(x).start()
+    last = cells_ref.shape[1] - 1
     token_ref[...] = jnp.zeros(token_ref.shape, F32)
     token = pltpu.make_async_copy(token_ref, token_hbm, sems.at[0])
     token.start()
-    fetch(0).wait()
-    fetch(1).wait()
 
     def store(x):
         return pltpu.make_async_copy(out_ref.at[:, x], out_hbm.at[:, x], sems.at[x])
 
     def middle(x, unused):
-        fetch(x + 1).wait()
-
         def write(c, value):
             out_ref[c, x] = value + deposit_ref[c, x] if c < SECTIONS else value
 
@@ -415,24 +417,19 @@
     token = jax.ShapeDtypeStruct((8, LANES), F32)
     return call(
         inner_kernel, [out, token], (cells, low, high, deposited, rate),
-        [pltpu.VMEM(a.shape, F32) for a in (cells, out, token)] + [pltpu.SemaphoreType.DMA((cells.shape[1],))] * 2,
-        in_specs=[ANY] + [VMEM] * 3 + [SMEM], flops=30 << 20, moved_bytes=4 << 20,
+        [pltpu.VMEM(out.shape, F32), pltpu.VMEM(token.shape, F32), pltpu.SemaphoreType.DMA((cells.shape[1],))],
+        in_specs=[VMEM] * 4 + [SMEM], flops=30 << 20, moved_bytes=4 << 20,
     )
 
 
 def edge_kernel(
-    cells_hbm, inner_hbm, before_ref, after_ref, low_ref, high_ref, deposit_ref, rate_ref, out_hbm,
-    cells_ref, out_ref, sems,
+    cells_ref, inner_hbm, before_ref, after_ref, low_ref, high_ref, deposit_ref, rate_ref, out_hbm, out_ref, sems
 ):
-    last = cells_hbm.shape[1] - 1
+    last = cells_ref.shape[1] - 1
     copies = [
-        pltpu.make_async_copy(cells_hbm.at[:, 0:2], cells_ref.at[:, 0:2], sems.at[0]),
-        pltpu.make_async_copy(cells_hbm.at[:, last - 1 : last + 1], cells_ref.at[:, 2:4], sems.at[1]),
-        pltpu.make_async_copy(out_ref.at[:, 0], out_hbm.at[:, 0], sems.at[2]),
-        pltpu.make_async_copy(out_ref.at[:, 1], out_hbm.at[:, last], sems.at[3]),
+        pltpu.make_async_copy(out_ref.at[:, 0], out_hbm.at[:, 0], sems.at[0]),
+        pltpu.make_async_copy(out_ref.at[:, 1], out_hbm.at[:, last], sems.at[1]),
     ]
-    copies[0].start()
-    copies[1].start()
 
     def layer(left, number, x, right):
         def write(c, value):
@@ -440,21 +437,19 @@
 
         slab_update(
             left,
-            lambda c: cells_ref[c, 3 * number],
+            lambda c: cells_ref[c, x],
             right,
             lambda c: low_ref[c, x : x + 1, :],
             lambda c: high_ref[c, x : x + 1, :],
             rate_ref,
             write,
         )
-        copies[2 + number].start()
-
+        copies[number].start()
+
+    layer(lambda c: before_ref[c], 0, 0, lambda c: cells_ref[c, 1])
+    layer(lambda c: cells_ref[c, last - 1], 1, last, lambda c: after_ref[c])
     copies[0].wait()
-    layer(lambda c: before_ref[c], 0, 0, lambda c: cells_ref[c, 1])
     copies[1].wait()
-    layer(lambda c: cells_ref[c, 2], 1, last, lambda c: after_ref[c])
-    copies[2].wait()
-    copies[3].wait()
 
 
 def edges(cells, inner_cells, before, after, low, high, deposited, rate):
@@ -463,16 +458,11 @@
         edge_kernel, jax.ShapeDtypeStruct(inner_cells.shape, F32),
         (cells, inner_cells, before, after, low, high, deposited, rate),
         [
-            pltpu.VMEM((cells.shape[0], 4, size_y, size_z), F32),
             pltpu.VMEM((COUNT, 2, size_y, size_z), F32),
-            pltpu.SemaphoreType.DMA((4,)),
+            pltpu.SemaphoreType.DMA((2,)),
         ],
-        in_specs=[ANY, ANY] + [VMEM] * 5 + [SMEM], aliases={1: 0}, flops=10 << 20, moved_bytes=2 << 20,
-    )
-
-
-def quotient(value, count):
-    return value >> (count.bit_length() - 1) if count & (count - 1) == 0 else value // count
+        in_specs=[VMEM, ANY] + [VMEM] * 5 + [SMEM], aliases={1: 0}, flops=10 << 20, moved_bytes=2 << 20,
+    )
 
 
 def deposit_kernel(shape, windows, routed_ref, out_ref, mass_ref, spread_ref, depth_ref):
@@ -585,7 +575,11 @@
     routed = lax.all_to_all(filled, ("gx", "gy"), split_axis=0, concat_axis=0, tiled=True)
     routed = routed.reshape(-1, fold, 9, capacity).transpose(0, 2, 1, 3).reshape(-1, LANES)
 
-    windows = [cell_state.shape[1]] * (routed.shape[0] // 9 // 8)
+    layers = cell_state.shape[1]
+    parts = routed.shape[0] // 9 // 8
+    windows = [layers] * parts
+    if fold == 1:
+        windows = [layers * (min(q + 2, parts) - max(q - 1, 0)) // parts for q in range(parts)]
     deposited = deposit(routed, cell_state.shape[1:], windows)
     inner_cells, token = inner(cell_state, low, high, deposited, evap_rate)
     new_parcels = arrive(token, advanced, hot, crossing, before, after)

time: 37 us -> 36.4 us (0.984)
  Pallas kernels: 19.8 us -> 17.8 us
  waiting for transfers between devices: 1.92 us -> 3.63 us
    pallas_call x5, Pallas kernels: 19.8 us -> 17.8 us  [call(): pl.pallas_call(kernel, out_shape=out_shape, in_specs=in_specs or [ANY] *...]
    ppermute x1, waiting for transfers between devices: 0.01 us -> 1.72 us  [on_device(): after = lax.ppermute(send_down, 'gx', down_x)]
  transfers between devices with their start and end apart: 5 -> 5, of which waited for: 1 -> 2; matrix products, arithmetic and copies ran while one was open for 0% -> 0% of each run, Pallas kernels for 28% -> 20%
where the time goes in v9:
time: 36.4 us; the launch traced here: 36.1 us
  Pallas kernels  17.8 us (49%)
  starting transfers between devices  13.8 us (38%)
  waiting for transfers between devices  3.63 us (10%)
  between operations  0.9 us (2%)
    pallas_call x5, Pallas kernels, call(): pl.pallas_call(kernel, out_shape=out_shape, in_specs=in_specs or [ANY] *...  17.8 us
    all_to_all x1, starting transfers between devices, on_device(): lax.all_to_all(filled, ('gx', 'gy'), split_axis=0, concat_axis=0, tiled=T...  7.3 us
    ppermute x1, starting transfers between devices, on_device(): after = lax.ppermute(send_down, 'gx', down_x)  2.95 us
    all_to_all x1, waiting for transfers between devices, on_device(): lax.all_to_all(filled, ('gx', 'gy'), split_axis=0, concat_axis=0, tiled=T...  1.91 us
    ppermute x1, starting transfers between devices, on_device(): before = lax.ppermute(send_up, 'gx', up_x)  1.82 us
    ppermute x1, starting transfers between devices, on_device(): high = lax.ppermute(side_down, 'gy', down_y)  1.74 us
    ppermute x1, waiting for transfers between devices, on_device(): after = lax.ppermute(send_down, 'gx', down_x)  1.72 us
  transfers between devices with their start and end apart: 5, of which 2 were waited for; matrix products, arithmetic and copies ran while one was open for 0% of the time, Pallas kernels for 20%

profile of v9, /device:TPU:0, one launch (start us, length us, event | category | flops | bytes accessed | tf_op | source)
XLA Modules:
  0.0 36.1 jit_solution(8907392911436062084)
XLA Ops:
  0.6 6.3 %shard_map.86 = (f32[17,16,256]{2,1,0:T(8,128)}, f32[17,16,256]{2,1,0:T(8,128)}, f32[15,8,256]{2,1,0:T(8,128)}, f32[15,8,256]{2,1,0:T(8,128)}, f32[8,16384]{1,0:...) custom-call(f32[17,8,16,256]{3,2,1,0:T(8,128)} %cells_ref.3, f32[8,16384]{1,0:T(8,128)} %parcels_hbm.1, ...), custom_call_target="tpu_custom_call" | custom-call | flops 2147483648 | bytes 6291456 | tf_op jit(solution)/shard_map/pallas_call | solution.py:27
  6.9 7.3 %all-to-all-start = ((f32[32,1,1152]{2,1,0:T(1,128)}), f32[32,1,1152]{2,1,0:T(1,128)S(1)}, u32[]{:S(2)}, u32[]{:S(2)}) async-start(f32[32,1,1152]{2,1,0:T(1,128)} %bitcast.5), calls=%async_computation | async-start | bytes 294912 | tf_op jit(solution)/shard_map/all_to_all | solution.py:575
  14.2 1.8 %collective-permute-start.2 = (f32[17,16,256]{2,1,0:T(8,128)}, f32[17,16,256]{2,1,0:T(8,128)S(1)}, u32[]{:S(2)}, u32[]{:S(2)}) collective-permute-start(f32[17,16,256]{2,1,0:T(8,128)} %get-tuple-element.15), channel_id=1, source_target_pairs={{0,4},{4,8},{8,12},{12,16},{16,20},{20,24},{24,28},{28,0},{1,5},{5... | collective-permute-start | bytes 835592 | tf_op jit(solution)/shard_map/ppermute | solution.py:568
  16.0 3.0 %collective-permute-start.3 = (f32[17,16,256]{2,1,0:T(8,128)}, f32[17,16,256]{2,1,0:T(8,128)S(1)}, u32[]{:S(2)}, u32[]{:S(2)}) collective-permute-start(f32[17,16,256]{2,1,0:T(8,128)} %get-tuple-element.16), channel_id=1, source_target_pairs={{4,0},{8,4},{12,8},{16,12},{20,16},{24,20},{28,24},{0,28},{5,1},{9... | collective-permute-start | bytes 835592 | tf_op jit(solution)/shard_map/ppermute | solution.py:569
  19.0 0.0 collective-permute-start
  19.0 1.7 %collective-permute-start.1 = (f32[15,8,256]{2,1,0:T(8,128)}, f32[15,8,256]{2,1,0:T(8,128)S(1)}, u32[]{:S(2)}, u32[]{:S(2)}) collective-permute-start(f32[15,8,256]{2,1,0:T(8,128)} %get-tuple-element.12), channel_id=1, source_target_pairs={{1,0},{2,1},{3,2},{0,3},{5,4},{6,5},{7,6},{4,7},{9,8},{10,9},{11,1... | collective-permute-start | bytes 368648 | tf_op jit(solution)/shard_map/ppermute | solution.py:571
  20.7 1.9 %all-to-all-done = f32[32,1,1152]{2,1,0:T(1,128)S(1)} async-done(((f32[32,1,1152]{2,1,0:T(1,128)}), f32[32,1,1152]{2,1,0:T(1,128)S(1)}, u32[]{:S(2)}, u32[]{:S(2)}) %all-to-all-start) | async-done | bytes 147488 | tf_op jit(solution)/shard_map/all_to_all | solution.py:575
  22.6 0.0 copy-start
  22.6 4.5 %shard_map.87.deposit_ref = f32[8,8,16,256]{3,2,1,0:T(8,128)S(1)} custom-call(f32[288,128]{1,0:T(8,128)S(1)} %bitcast.4), custom_call_target="tpu_custom_call" | custom-call | flops 1073741824 | bytes 2097152 | tf_op jit(solution)/shard_map/pallas_call | solution.py:27
  27.2 0.0 collective-permute-done.low_ref
  27.2 0.0 collective-permute-done.1.high_ref
  27.2 0.0 copy-done
  27.2 0.0 copy-done.1
  27.2 2.8 %shard_map.88 = (f32[14,8,16,256]{3,2,1,0:T(8,128)}, f32[8,128]{1,0:T(8,128)S(1)}) custom-call(f32[17,8,16,256]{3,2,1,0:T(8,128)S(1)} %copy-done, f32[15,8,256]{2,1,0:T(8,128)S(1)} %collective-permute-done.low_ref, f32[15,8,256]{2,1,0:T(8,128)S(1)} %collective-permute-done.1.high_ref, f32[8,8,16,256]{3,2,1,0:T(8,128)S(1)} %shard_map.87.deposit_ref, ...), custom_call_target="tpu_custom_call" | custom-call | flops 31457280 | bytes 4194304 | tf_op jit(solution)/shard_map/pallas_call | solution.py:27
  30.0 0.0 collective-permute-done.2.before_ref
  30.0 1.7 %collective-permute-done.3.after_ref = f32[17,16,256]{2,1,0:T(8,128)S(1)} collective-permute-done((f32[17,16,256]{2,1,0:T(8,128)}, f32[17,16,256]{2,1,0:T(8,128)S(1)}, u32[]{:S(2)}, u32[]{:S(2)}) %collective-permute-start.3) | collective-permute-done | bytes 278560 | tf_op jit(solution)/shard_map/ppermute | solution.py:569
  31.7 0.0 copy-start.2
  31.7 0.0 copy-start.3
  31.7 0.0 copy-start.4
  31.7 1.7 %shard_map.89 = f32[14,8,16,256]{3,2,1,0:T(8,128)} custom-call(f32[17,8,16,256]{3,2,1,0:T(8,128)S(1)} %copy-done, f32[14,8,16,256]{3,2,1,0:T(8,128)} %get-tuple-element.14.inner_hbm, f32[17,16,256]{2,1,0:T(8,128)S(1)} %collective-permute-done.2.before_ref, f32[17,16,256]{2,1,0:T(8,128)S(1)} %collective-permute-done.3.after_ref, ...), custom_call_target="tpu_custom_call", output_to_operand_aliasing={{}: (1, {})} | custom-call | flops 10485760 | bytes 2097152 | tf_op jit(solution)/shard_map/pallas_call | solution.py:27
  33.5 0.0 copy-done.2
  33.5 0.0 copy-done.3
  33.5 0.0 copy-done.4
  33.5 2.5 %shard_map.90 = f32[8,16384]{1,0:T(8,128)} custom-call(f32[8,128]{1,0:T(8,128)S(1)} %get-tuple-element.17.unused, f32[8,16384]{1,0:T(8,128)S(1)} %copy-done.4, bf16[256,2048]{1,0:T(8,128)(2,1)S(1)} %copy-done.3, s32[2,1024]{1,0:T(2,128)S(1)} %copy-done.2, f32[17,16,256]{2,1,0:T(8,128)S(1)} %collective-permute-done.2.before_ref, ...), custom_call_target="tpu_custom_call" | custom-call | flops 1073741824 | bytes 3145728 | tf_op jit(solution)/shard_map/pallas_call | solution.py:27
  (1 shorter events, 0.0 us)
Async XLA Ops:
  6.9 15.7 %all-to-all-start = ((f32[32,1,1152]{2,1,0:T(1,128)}), f32[32,1,1152]{2,1,0:T(1,128)S(1)}, u32[]{:S(2)}, u32[]{:S(2)}) async-start(f32[32,1,1152]{2,1,0:T(1,128)} %bitcast.5), calls=%async_computation | async-start | bytes 294912 | tf_op jit(solution)/shard_map/all_to_all | solution.py:575
  14.2 15.8 %collective-permute-start.2 = (f32[17,16,256]{2,1,0:T(8,128)}, f32[17,16,256]{2,1,0:T(8,128)S(1)}, u32[]{:S(2)}, u32[]{:S(2)}) collective-permute-start(f32[17,16,256]{2,1,0:T(8,128)} %get-tuple-element.15), channel_id=1, source_target_pairs={{0,4},{4,8},{8,12},{12,16},{16,20},{20,24},{24,28},{28,0},{1,5},{5... | collective-permute-start | bytes 835592 | tf_op jit(solution)/shard_map/ppermute | solution.py:568
  16.0 15.7 %collective-permute-start.3 = (f32[17,16,256]{2,1,0:T(8,128)}, f32[17,16,256]{2,1,0:T(8,128)S(1)}, u32[]{:S(2)}, u32[]{:S(2)}) collective-permute-start(f32[17,16,256]{2,1,0:T(8,128)} %get-tuple-element.16), channel_id=1, source_target_pairs={{4,0},{8,4},{12,8},{16,12},{20,16},{24,20},{28,24},{0,28},{5,1},{9... | collective-permute-start | bytes 835592 | tf_op jit(solution)/shard_map/ppermute | solution.py:569
  19.0 8.2 %collective-permute-start = (f32[15,8,256]{2,1,0:T(8,128)}, f32[15,8,256]{2,1,0:T(8,128)S(1)}, u32[]{:S(2)}, u32[]{:S(2)}) collective-permute-start(f32[15,8,256]{2,1,0:T(8,128)} %get-tuple-element.11), channel_id=1, source_target_pairs={{0,1},{1,2},{2,3},{3,0},{4,5},{5,6},{6,7},{7,4},{8,9},{9,10},{10,1... | collective-permute-start | bytes 368648 | tf_op jit(solution)/shard_map/ppermute | solution.py:570
  19.0 8.2 %collective-permute-start.1 = (f32[15,8,256]{2,1,0:T(8,128)}, f32[15,8,256]{2,1,0:T(8,128)S(1)}, u32[]{:S(2)}, u32[]{:S(2)}) collective-permute-start(f32[15,8,256]{2,1,0:T(8,128)} %get-tuple-element.12), channel_id=1, source_target_pairs={{1,0},{2,1},{3,2},{0,3},{5,4},{6,5},{7,6},{4,7},{9,8},{10,9},{11,1... | collective-permute-start | bytes 368648 | tf_op jit(solution)/shard_map/ppermute | solution.py:571
  22.6 4.6 %copy-start = (f32[17,8,16,256]{3,2,1,0:T(8,128)S(1)}, f32[17,8,16,256]{3,2,1,0:T(8,128)}, u32[]{:S(2)}) copy-start(f32[17,8,16,256]{3,2,1,0:T(8,128)} %cells_ref.3) | copy-start | bytes 6684676
  22.6 4.6 %copy-start.1 = (f32[8]{0:T(128)S(1)}, f32[8]{0:T(128)}, u32[]{:S(2)}) copy-start(f32[8]{0:T(128)} %rate_ref.3) | copy-start | bytes 100
  31.7 1.7 %copy-start.2 = (s32[2,1024]{1,0:T(2,128)S(1)}, s32[2,1024]{1,0:T(2,128)}, u32[]{:S(2)}) copy-start(s32[2,1024]{1,0:T(2,128)} %crossing_ref.1) | copy-start | bytes 24580
  31.7 1.8 %copy-start.3 = (bf16[256,2048]{1,0:T(8,128)(2,1)S(1)}, bf16[256,2048]{1,0:T(8,128)(2,1)}, u32[]{:S(2)}) copy-start(bf16[256,2048]{1,0:T(8,128)(2,1)} %get-tuple-element.19.hot_ref) | copy-start | bytes 3145732
  31.7 1.8 %copy-start.4 = (f32[8,16384]{1,0:T(8,128)S(1)}, f32[8,16384]{1,0:T(8,128)}, u32[]{:S(2)}) copy-start(f32[8,16384]{1,0:T(8,128)} %get-tuple-element.18.advanced_ref) | copy-start | bytes 1572868

commit v10 on v9

--- a/solution.py
+++ b/solution.py
@@ -195,6 +195,10 @@
 
     lax.fori_loop(0, slot_total // (4 * LANES), advance_pair, 0, unroll=4)
     copies[10].start()
+    for copy in (*copies[1:4], copies[5]):
+        copy.wait()
+    copies[6].start()
+    copies[7].start()
 
     halves_y, halves_z = size_y // 8, size_z // LANES
     part_rows = parts_ref.shape[0]
@@ -221,22 +225,14 @@
                     total = jnp.where(upper == (rows + i) // 8, picked[i : i + 8], total)
                 for number, spot in enumerate(spots):
                     leave_ref[spot] = total[:, number * LANES : (number + 1) * LANES]
-    copies[11].start()
-    copies[12].start()
-
-    copies[5].wait()
-    copies[6].start()
-    copies[7].start()
+    bucket_into(owner_total, capacity, size_x * size_y * size_z, mass_ref, owner_ref, cell_ref, filled_ref, left_ref, spot_ref)
+    copies[8].start()
     for c in range(COUNT + 1):
         source = c if c < COUNT else COUNT + 1
         yup_ref[c] = cells_ref[source, :, size_y - 1, :]
         ydown_ref[c] = cells_ref[source, :, 0, :]
-    copies[13].start()
-    copies[14].start()
-    for copy in copies[1:4]:
-        copy.wait()
-    bucket_into(owner_total, capacity, size_x * size_y * size_z, mass_ref, owner_ref, cell_ref, filled_ref, left_ref, spot_ref)
-    copies[8].start()
+    for copy in copies[11:]:
+        copy.start()
     for copy in copies[6:]:
         copy.wait()
 

time: 36.4 us -> 36.4 us (level)
  no operation moved by 1% of the time
where the time goes in v10:
time: 36.4 us; the launch traced here: 36.2 us
  Pallas kernels  17.8 us (49%)
  starting transfers between devices  13.8 us (38%)
  waiting for transfers between devices  3.64 us (10%)
  between operations  0.9 us (2%)
    pallas_call x5, Pallas kernels, call(): pl.pallas_call(kernel, out_shape=out_shape, in_specs=in_specs or [ANY] *...  17.8 us
    all_to_all x1, starting transfers between devices, on_device(): lax.all_to_all(filled, ('gx', 'gy'), split_axis=0, concat_axis=0, tiled=T...  7.3 us
    ppermute x1, starting transfers between devices, on_device(): after = lax.ppermute(send_down, 'gx', down_x)  2.95 us
    all_to_all x1, waiting for transfers between devices, on_device(): lax.all_to_all(filled, ('gx', 'gy'), split_axis=0, concat_axis=0, tiled=T...  1.91 us
    ppermute x1, starting transfers between devices, on_device(): before = lax.ppermute(send_up, 'gx', up_x)  1.82 us
    ppermute x1, starting transfers between devices, on_device(): high = lax.ppermute(side_down, 'gy', down_y)  1.74 us
    ppermute x1, waiting for transfers between devices, on_device(): after = lax.ppermute(send_down, 'gx', down_x)  1.72 us
  transfers between devices with their start and end apart: 5, of which 2 were waited for; matrix products, arithmetic and copies ran while one was open for 0% of the time, Pallas kernels for 20%

profile of v10, /device:TPU:0, one launch (start us, length us, event | category | flops | bytes accessed | tf_op | source)
XLA Modules:
  0.0 36.2 jit_solution(11034329230959442414)
XLA Ops:
  0.6 6.3 %shard_map.86 = (f32[17,16,256]{2,1,0:T(8,128)}, f32[17,16,256]{2,1,0:T(8,128)}, f32[15,8,256]{2,1,0:T(8,128)}, f32[15,8,256]{2,1,0:T(8,128)}, f32[8,16384]{1,0:...) custom-call(f32[17,8,16,256]{3,2,1,0:T(8,128)} %cells_ref.3, f32[8,16384]{1,0:T(8,128)} %parcels_hbm.1, ...), custom_call_target="tpu_custom_call" | custom-call | flops 2147483648 | bytes 6291456 | tf_op jit(solution)/shard_map/pallas_call | solution.py:27
  6.9 7.3 %all-to-all-start = ((f32[32,1,1152]{2,1,0:T(1,128)}), f32[32,1,1152]{2,1,0:T(1,128)S(1)}, u32[]{:S(2)}, u32[]{:S(2)}) async-start(f32[32,1,1152]{2,1,0:T(1,128)} %bitcast.5), calls=%async_computation | async-start | bytes 294912 | tf_op jit(solution)/shard_map/all_to_all | solution.py:571
  14.2 1.8 %collective-permute-start.2 = (f32[17,16,256]{2,1,0:T(8,128)}, f32[17,16,256]{2,1,0:T(8,128)S(1)}, u32[]{:S(2)}, u32[]{:S(2)}) collective-permute-start(f32[17,16,256]{2,1,0:T(8,128)} %get-tuple-element.15), channel_id=1, source_target_pairs={{0,4},{4,8},{8,12},{12,16},{16,20},{20,24},{24,28},{28,0},{1,5},{5... | collective-permute-start | bytes 835592 | tf_op jit(solution)/shard_map/ppermute | solution.py:564
  16.1 3.0 %collective-permute-start.3 = (f32[17,16,256]{2,1,0:T(8,128)}, f32[17,16,256]{2,1,0:T(8,128)S(1)}, u32[]{:S(2)}, u32[]{:S(2)}) collective-permute-start(f32[17,16,256]{2,1,0:T(8,128)} %get-tuple-element.16), channel_id=1, source_target_pairs={{4,0},{8,4},{12,8},{16,12},{20,16},{24,20},{28,24},{0,28},{5,1},{9... | collective-permute-start | bytes 835592 | tf_op jit(solution)/shard_map/ppermute | solution.py:565
  19.0 0.0 collective-permute-start
  19.0 1.7 %collective-permute-start.1 = (f32[15,8,256]{2,1,0:T(8,128)}, f32[15,8,256]{2,1,0:T(8,128)S(1)}, u32[]{:S(2)}, u32[]{:S(2)}) collective-permute-start(f32[15,8,256]{2,1,0:T(8,128)} %get-tuple-element.12), channel_id=1, source_target_pairs={{1,0},{2,1},{3,2},{0,3},{5,4},{6,5},{7,6},{4,7},{9,8},{10,9},{11,1... | collective-permute-start | bytes 368648 | tf_op jit(solution)/shard_map/ppermute | solution.py:567
  20.8 1.9 %all-to-all-done = f32[32,1,1152]{2,1,0:T(1,128)S(1)} async-done(((f32[32,1,1152]{2,1,0:T(1,128)}), f32[32,1,1152]{2,1,0:T(1,128)S(1)}, u32[]{:S(2)}, u32[]{:S(2)}) %all-to-all-start) | async-done | bytes 147488 | tf_op jit(solution)/shard_map/all_to_all | solution.py:571
  22.7 0.0 copy-start
  22.7 0.0 copy-start.1
  22.7 4.5 %shard_map.87.deposit_ref = f32[8,8,16,256]{3,2,1,0:T(8,128)S(1)} custom-call(f32[288,128]{1,0:T(8,128)S(1)} %bitcast.4), custom_call_target="tpu_custom_call" | custom-call | flops 1073741824 | bytes 2097152 | tf_op jit(solution)/shard_map/pallas_call | solution.py:27
  27.2 0.0 collective-permute-done.low_ref
  27.2 0.0 collective-permute-done.1.high_ref
  27.2 0.0 copy-done
  27.2 0.0 copy-done.1
  27.2 2.8 %shard_map.88 = (f32[14,8,16,256]{3,2,1,0:T(8,128)}, f32[8,128]{1,0:T(8,128)S(1)}) custom-call(f32[17,8,16,256]{3,2,1,0:T(8,128)S(1)} %copy-done, f32[15,8,256]{2,1,0:T(8,128)S(1)} %collective-permute-done.low_ref, f32[15,8,256]{2,1,0:T(8,128)S(1)} %collective-permute-done.1.high_ref, f32[8,8,16,256]{3,2,1,0:T(8,128)S(1)} %shard_map.87.deposit_ref, ...), custom_call_target="tpu_custom_call" | custom-call | flops 31457280 | bytes 4194304 | tf_op jit(solution)/shard_map/pallas_call | solution.py:27
  30.0 0.0 collective-permute-done.2.before_ref
  30.0 1.7 %collective-permute-done.3.after_ref = f32[17,16,256]{2,1,0:T(8,128)S(1)} collective-permute-done((f32[17,16,256]{2,1,0:T(8,128)}, f32[17,16,256]{2,1,0:T(8,128)S(1)}, u32[]{:S(2)}, u32[]{:S(2)}) %collective-permute-start.3) | collective-permute-done | bytes 278560 | tf_op jit(solution)/shard_map/ppermute | solution.py:565
  31.8 0.0 copy-start.2
  31.8 0.0 copy-start.3
  31.8 1.7 %shard_map.89 = f32[14,8,16,256]{3,2,1,0:T(8,128)} custom-call(f32[17,8,16,256]{3,2,1,0:T(8,128)S(1)} %copy-done, f32[14,8,16,256]{3,2,1,0:T(8,128)} %get-tuple-element.14.inner_hbm, f32[17,16,256]{2,1,0:T(8,128)S(1)} %collective-permute-done.2.before_ref, f32[17,16,256]{2,1,0:T(8,128)S(1)} %collective-permute-done.3.after_ref, ...), custom_call_target="tpu_custom_call", output_to_operand_aliasing={{}: (1, {})} | custom-call | flops 10485760 | bytes 2097152 | tf_op jit(solution)/shard_map/pallas_call | solution.py:27
  33.5 0.0 copy-done.2
  33.5 0.0 copy-done.3
  33.5 0.0 copy-done.4
  33.5 2.5 %shard_map.90 = f32[8,16384]{1,0:T(8,128)} custom-call(f32[8,128]{1,0:T(8,128)S(1)} %get-tuple-element.17.unused, f32[8,16384]{1,0:T(8,128)S(1)} %copy-done.4, bf16[256,2048]{1,0:T(8,128)(2,1)S(1)} %copy-done.3, s32[2,1024]{1,0:T(2,128)S(1)} %copy-done.2, f32[17,16,256]{2,1,0:T(8,128)S(1)} %collective-permute-done.2.before_ref, ...), custom_call_target="tpu_custom_call" | custom-call | flops 1073741824 | bytes 3145728 | tf_op jit(solution)/shard_map/pallas_call | solution.py:27
  (1 shorter events, 0.0 us)
Async XLA Ops:
  6.9 15.7 %all-to-all-start = ((f32[32,1,1152]{2,1,0:T(1,128)}), f32[32,1,1152]{2,1,0:T(1,128)S(1)}, u32[]{:S(2)}, u32[]{:S(2)}) async-start(f32[32,1,1152]{2,1,0:T(1,128)} %bitcast.5), calls=%async_computation | async-start | bytes 294912 | tf_op jit(solution)/shard_map/all_to_all | solution.py:571
  14.2 15.8 %collective-permute-start.2 = (f32[17,16,256]{2,1,0:T(8,128)}, f32[17,16,256]{2,1,0:T(8,128)S(1)}, u32[]{:S(2)}, u32[]{:S(2)}) collective-permute-start(f32[17,16,256]{2,1,0:T(8,128)} %get-tuple-element.15), channel_id=1, source_target_pairs={{0,4},{4,8},{8,12},{12,16},{16,20},{20,24},{24,28},{28,0},{1,5},{5... | collective-permute-start | bytes 835592 | tf_op jit(solution)/shard_map/ppermute | solution.py:564
  16.1 15.7 %collective-permute-start.3 = (f32[17,16,256]{2,1,0:T(8,128)}, f32[17,16,256]{2,1,0:T(8,128)S(1)}, u32[]{:S(2)}, u32[]{:S(2)}) collective-permute-start(f32[17,16,256]{2,1,0:T(8,128)} %get-tuple-element.16), channel_id=1, source_target_pairs={{4,0},{8,4},{12,8},{16,12},{20,16},{24,20},{28,24},{0,28},{5,1},{9... | collective-permute-start | bytes 835592 | tf_op jit(solution)/shard_map/ppermute | solution.py:565
  19.0 8.2 %collective-permute-start = (f32[15,8,256]{2,1,0:T(8,128)}, f32[15,8,256]{2,1,0:T(8,128)S(1)}, u32[]{:S(2)}, u32[]{:S(2)}) collective-permute-start(f32[15,8,256]{2,1,0:T(8,128)} %get-tuple-element.11), channel_id=1, source_target_pairs={{0,1},{1,2},{2,3},{3,0},{4,5},{5,6},{6,7},{7,4},{8,9},{9,10},{10,1... | collective-permute-start | bytes 368648 | tf_op jit(solution)/shard_map/ppermute | solution.py:566
  19.0 8.2 %collective-permute-start.1 = (f32[15,8,256]{2,1,0:T(8,128)}, f32[15,8,256]{2,1,0:T(8,128)S(1)}, u32[]{:S(2)}, u32[]{:S(2)}) collective-permute-start(f32[15,8,256]{2,1,0:T(8,128)} %get-tuple-element.12), channel_id=1, source_target_pairs={{1,0},{2,1},{3,2},{0,3},{5,4},{6,5},{7,6},{4,7},{9,8},{10,9},{11,1... | collective-permute-start | bytes 368648 | tf_op jit(solution)/shard_map/ppermute | solution.py:567
  22.7 4.6 %copy-start = (f32[17,8,16,256]{3,2,1,0:T(8,128)S(1)}, f32[17,8,16,256]{3,2,1,0:T(8,128)}, u32[]{:S(2)}) copy-start(f32[17,8,16,256]{3,2,1,0:T(8,128)} %cells_ref.3) | copy-start | bytes 6684676
  22.7 4.6 %copy-start.1 = (f32[8]{0:T(128)S(1)}, f32[8]{0:T(128)}, u32[]{:S(2)}) copy-start(f32[8]{0:T(128)} %rate_ref.3) | copy-start | bytes 100
  31.8 1.7 %copy-start.2 = (s32[2,1024]{1,0:T(2,128)S(1)}, s32[2,1024]{1,0:T(2,128)}, u32[]{:S(2)}) copy-start(s32[2,1024]{1,0:T(2,128)} %crossing_ref.1) | copy-start | bytes 24580
  31.8 1.8 %copy-start.3 = (bf16[256,2048]{1,0:T(8,128)(2,1)S(1)}, bf16[256,2048]{1,0:T(8,128)(2,1)}, u32[]{:S(2)}) copy-start(bf16[256,2048]{1,0:T(8,128)(2,1)} %get-tuple-element.19.hot_ref) | copy-start | bytes 3145732
  31.8 1.8 %copy-start.4 = (f32[8,16384]{1,0:T(8,128)S(1)}, f32[8,16384]{1,0:T(8,128)}, u32[]{:S(2)}) copy-start(f32[8,16384]{1,0:T(8,128)} %get-tuple-element.18.advanced_ref) | copy-start | bytes 1572868

commit v11 on v10

--- a/solution.py
+++ b/solution.py
@@ -12,7 +12,7 @@
 COUNT = SECTIONS + SPECIES
 LANES = 128
 WIDE = 256
-GROUPS = 4
+GROUPS = 2
 F32 = jnp.float32
 BF16 = jnp.bfloat16
 ANY = pl.BlockSpec(memory_space=pl.ANY)
@@ -264,7 +264,7 @@
     )
 
 
-def arrive_kernel(unused, advanced_ref, hot_ref, crossing_ref, before_ref, after_ref, out_hbm, out_ref, left_ref, sems):
+def arrive_into(advanced_ref, hot_ref, crossing_ref, before_ref, after_ref, out_hbm, out_ref, left_ref, sems):
     cross = crossing_ref.shape[1]
     uppers = advanced_ref.shape[1] // WIDE
     size_y, size_z = before_ref.shape[1:]
@@ -295,21 +295,7 @@
         out = pltpu.make_async_copy(out_ref.at[:, at], out_hbm.at[:, at], sems.at[len(outs)])
         out.start()
         outs.append(out)
-    for out in outs:
-        out.wait()
-
-
-def arrive(earlier, advanced, hot, crossing, before, after):
-    uppers = advanced.shape[1] // WIDE
-    return call(
-        arrive_kernel, jax.ShapeDtypeStruct(advanced.shape, F32), (earlier, advanced, hot, crossing, before, after),
-        [
-            pltpu.VMEM(advanced.shape, F32),
-            pltpu.VMEM((17 * uppers, crossing.size), BF16),
-            pltpu.SemaphoreType.DMA((-(-uppers // 32),)),
-        ],
-        in_specs=[ANY] + [VMEM] * 5, flops=1 << 30, moved_bytes=3 << 20,
-    )
+    return outs
 
 
 def shift_up(value, axis):
@@ -376,12 +362,9 @@
 
 
 def inner_kernel(
-    cells_ref, low_ref, high_ref, deposit_ref, rate_ref, out_hbm, token_hbm, out_ref, token_ref, sems
+    cells_ref, low_ref, high_ref, deposit_ref, rate_ref, out_hbm, out_ref, sems
 ):
     last = cells_ref.shape[1] - 1
-    token_ref[...] = jnp.zeros(token_ref.shape, F32)
-    token = pltpu.make_async_copy(token_ref, token_hbm, sems.at[0])
-    token.start()
 
     def store(x):
         return pltpu.make_async_copy(out_ref.at[:, x], out_hbm.at[:, x], sems.at[x])
@@ -405,21 +388,20 @@
     lax.fori_loop(1, last, middle, 0)
     for x in range(1, last):
         store(x).wait()
-    token.wait()
 
 
 def inner(cells, low, high, deposited, rate):
     out = jax.ShapeDtypeStruct((COUNT,) + cells.shape[1:], F32)
-    token = jax.ShapeDtypeStruct((8, LANES), F32)
     return call(
-        inner_kernel, [out, token], (cells, low, high, deposited, rate),
-        [pltpu.VMEM(out.shape, F32), pltpu.VMEM(token.shape, F32), pltpu.SemaphoreType.DMA((cells.shape[1],))],
+        inner_kernel, out, (cells, low, high, deposited, rate),
+        [pltpu.VMEM(out.shape, F32), pltpu.SemaphoreType.DMA((cells.shape[1],))],
         in_specs=[VMEM] * 4 + [SMEM], flops=30 << 20, moved_bytes=4 << 20,
     )
 
 
-def edge_kernel(
-    cells_ref, inner_hbm, before_ref, after_ref, low_ref, high_ref, deposit_ref, rate_ref, out_hbm, out_ref, sems
+def last_kernel(
+    cells_ref, inner_hbm, before_ref, after_ref, low_ref, high_ref, deposit_ref, rate_ref,
+    advanced_ref, hot_ref, crossing_ref, out_hbm, parcels_hbm, out_ref, parcels_ref, left_ref, sems, parcel_sems,
 ):
     last = cells_ref.shape[1] - 1
     copies = [
@@ -444,20 +426,28 @@
 
     layer(lambda c: before_ref[c], 0, 0, lambda c: cells_ref[c, 1])
     layer(lambda c: cells_ref[c, last - 1], 1, last, lambda c: after_ref[c])
-    copies[0].wait()
-    copies[1].wait()
-
-
-def edges(cells, inner_cells, before, after, low, high, deposited, rate):
+    copies += arrive_into(
+        advanced_ref, hot_ref, crossing_ref, before_ref, after_ref, parcels_hbm, parcels_ref, left_ref, parcel_sems
+    )
+    for copy in copies:
+        copy.wait()
+
+
+def finish(cells, inner_cells, before, after, low, high, deposited, rate, advanced, hot, crossing):
     size_y, size_z = cells.shape[2:]
+    uppers = advanced.shape[1] // WIDE
     return call(
-        edge_kernel, jax.ShapeDtypeStruct(inner_cells.shape, F32),
-        (cells, inner_cells, before, after, low, high, deposited, rate),
+        last_kernel, [jax.ShapeDtypeStruct(inner_cells.shape, F32), jax.ShapeDtypeStruct(advanced.shape, F32)],
+        (cells, inner_cells, before, after, low, high, deposited, rate, advanced, hot, crossing),
         [
             pltpu.VMEM((COUNT, 2, size_y, size_z), F32),
+            pltpu.VMEM(advanced.shape, F32),
+            pltpu.VMEM((17 * uppers, crossing.size), BF16),
             pltpu.SemaphoreType.DMA((2,)),
+            pltpu.SemaphoreType.DMA((-(-uppers // 32),)),
         ],
-        in_specs=[VMEM, ANY] + [VMEM] * 5 + [SMEM], aliases={1: 0}, flops=10 << 20, moved_bytes=2 << 20,
+        in_specs=[VMEM, ANY] + [VMEM] * 5 + [SMEM] + [VMEM] * 3, aliases={1: 0},
+        flops=1 << 30, moved_bytes=5 << 20,
     )
 
 
@@ -575,11 +565,13 @@
     parts = routed.shape[0] // 9 // 8
     windows = [layers] * parts
     if fold == 1:
-        windows = [layers * (min(q + 2, parts) - max(q - 1, 0)) // parts for q in range(parts)]
+        spans = [(max(q * GROUPS - 1, 0) // parts, ((q + 1) * GROUPS) // parts + 1) for q in range(parts)]
+        windows = [layers * (min(high, GROUPS) - low) // GROUPS for low, high in spans]
     deposited = deposit(routed, cell_state.shape[1:], windows)
-    inner_cells, token = inner(cell_state, low, high, deposited, evap_rate)
-    new_parcels = arrive(token, advanced, hot, crossing, before, after)
-    new_cells = edges(cell_state, inner_cells, before, after, low, high, deposited, evap_rate)
+    inner_cells = inner(cell_state, low, high, deposited, evap_rate)
+    new_cells, new_parcels = finish(
+        cell_state, inner_cells, before, after, low, high, deposited, evap_rate, advanced, hot, crossing
+    )
     return (new_cells, new_parcels)
 
 

time: 36.4 us -> 35.2 us (0.967)
  waiting for transfers between devices: 3.64 us -> 3.12 us
  Pallas kernels: 17.8 us -> 17.3 us
    pallas_call x5 -> x4, Pallas kernels: 17.8 us -> 17.3 us  [call(): pl.pallas_call(kernel, out_shape=out_shape, in_specs=in_specs or [ANY] *...]
    ppermute x1, waiting for transfers between devices: 1.72 us -> 1.2 us  [on_device(): after = lax.ppermute(send_down, 'gx', down_x)]
  transfers between devices with their start and end apart: 5 -> 5, of which waited for: 2 -> 2; matrix products, arithmetic and copies ran while one was open for 0% -> 0% of each run, Pallas kernels for 20% -> 22%
where the time goes in v11:
time: 35.2 us; the launch traced here: 35 us
  Pallas kernels  17.3 us (49%)
  starting transfers between devices  13.8 us (39%)
  waiting for transfers between devices  3.12 us (9%)
  between operations  0.73 us (2%)
    pallas_call x4, Pallas kernels, call(): pl.pallas_call(kernel, out_shape=out_shape, in_specs=in_specs or [ANY] *...  17.3 us
    all_to_all x1, starting transfers between devices, on_device(): lax.all_to_all(filled, ('gx', 'gy'), split_axis=0, concat_axis=0, tiled=T...  7.31 us
    ppermute x1, starting transfers between devices, on_device(): after = lax.ppermute(send_down, 'gx', down_x)  2.95 us
    all_to_all x1, waiting for transfers between devices, on_device(): lax.all_to_all(filled, ('gx', 'gy'), split_axis=0, concat_axis=0, tiled=T...  1.91 us
    ppermute x1, starting transfers between devices, on_device(): before = lax.ppermute(send_up, 'gx', up_x)  1.82 us
    ppermute x1, starting transfers between devices, on_device(): high = lax.ppermute(side_down, 'gy', down_y)  1.74 us
    ppermute x1, waiting for transfers between devices, on_device(): after = lax.ppermute(send_down, 'gx', down_x)  1.2 us
  transfers between devices with their start and end apart: 5, of which 2 were waited for; matrix products, arithmetic and copies ran while one was open for 0% of the time, Pallas kernels for 22%

profile of v11, /device:TPU:0, one launch (start us, length us, event | category | flops | bytes accessed | tf_op | source)
XLA Modules:
  0.0 35.0 jit_solution(12569535724337409938)
XLA Ops:
  0.6 5.9 %shard_map.86 = (f32[17,16,256]{2,1,0:T(8,128)}, f32[17,16,256]{2,1,0:T(8,128)}, f32[15,8,256]{2,1,0:T(8,128)}, f32[15,8,256]{2,1,0:T(8,128)}, f32[8,16384]{1,0:...) custom-call(f32[17,8,16,256]{3,2,1,0:T(8,128)} %cells_ref.3, f32[8,16384]{1,0:T(8,128)} %parcels_hbm.1, ...), custom_call_target="tpu_custom_call" | custom-call | flops 2147483648 | bytes 6291456 | tf_op jit(solution)/shard_map/pallas_call | solution.py:27
  6.6 7.3 %all-to-all-start = ((f32[32,1,1152]{2,1,0:T(1,128)}), f32[32,1,1152]{2,1,0:T(1,128)S(1)}, u32[]{:S(2)}, u32[]{:S(2)}) async-start(f32[32,1,1152]{2,1,0:T(1,128)} %bitcast.5), calls=%async_computation | async-start | bytes 294912 | tf_op jit(solution)/shard_map/all_to_all | solution.py:561
  13.9 1.8 %collective-permute-start.2 = (f32[17,16,256]{2,1,0:T(8,128)}, f32[17,16,256]{2,1,0:T(8,128)S(1)}, u32[]{:S(2)}, u32[]{:S(2)}) collective-permute-start(f32[17,16,256]{2,1,0:T(8,128)} %get-tuple-element.12), channel_id=1, source_target_pairs={{0,4},{4,8},{8,12},{12,16},{16,20},{20,24},{24,28},{28,0},{1,5},{5... | collective-permute-start | bytes 835592 | tf_op jit(solution)/shard_map/ppermute | solution.py:554
  15.7 3.0 %collective-permute-start.3 = (f32[17,16,256]{2,1,0:T(8,128)}, f32[17,16,256]{2,1,0:T(8,128)S(1)}, u32[]{:S(2)}, u32[]{:S(2)}) collective-permute-start(f32[17,16,256]{2,1,0:T(8,128)} %get-tuple-element.13), channel_id=1, source_target_pairs={{4,0},{8,4},{12,8},{16,12},{20,16},{24,20},{28,24},{0,28},{5,1},{9... | collective-permute-start | bytes 835592 | tf_op jit(solution)/shard_map/ppermute | solution.py:555
  18.6 0.0 collective-permute-start
  18.7 1.7 %collective-permute-start.1 = (f32[15,8,256]{2,1,0:T(8,128)}, f32[15,8,256]{2,1,0:T(8,128)S(1)}, u32[]{:S(2)}, u32[]{:S(2)}) collective-permute-start(f32[15,8,256]{2,1,0:T(8,128)} %get-tuple-element.10), channel_id=1, source_target_pairs={{1,0},{2,1},{3,2},{0,3},{5,4},{6,5},{7,6},{4,7},{9,8},{10,9},{11,1... | collective-permute-start | bytes 368648 | tf_op jit(solution)/shard_map/ppermute | solution.py:557
  20.4 1.9 %all-to-all-done = f32[32,1,1152]{2,1,0:T(1,128)S(1)} async-done(((f32[32,1,1152]{2,1,0:T(1,128)}), f32[32,1,1152]{2,1,0:T(1,128)S(1)}, u32[]{:S(2)}, u32[]{:S(2)}) %all-to-all-start) | async-done | bytes 147488 | tf_op jit(solution)/shard_map/all_to_all | solution.py:561
  22.3 0.0 copy-start
  22.3 0.0 copy-start.4
  22.3 4.9 %shard_map.87.deposit_ref = f32[8,8,16,256]{3,2,1,0:T(8,128)S(1)} custom-call(f32[288,128]{1,0:T(8,128)S(1)} %bitcast.4), custom_call_target="tpu_custom_call" | custom-call | flops 1073741824 | bytes 2097152 | tf_op jit(solution)/shard_map/pallas_call | solution.py:27
  27.2 0.0 copy-start.1
  27.2 0.0 copy-start.2
  27.2 0.0 copy-start.3
  27.3 0.0 collective-permute-done.low_ref
  27.3 0.0 collective-permute-done.1.high_ref
  27.3 0.0 copy-done
  27.3 0.0 copy-done.4
  27.3 2.9 %shard_map.88.inner_hbm = f32[14,8,16,256]{3,2,1,0:T(8,128)} custom-call(f32[17,8,16,256]{3,2,1,0:T(8,128)S(1)} %copy-done, f32[15,8,256]{2,1,0:T(8,128)S(1)} %collective-permute-done.low_ref, f32[15,8,256]{2,1,0:T(8,128)S(1)} %collective-permute-done.1.high_ref, f32[8,8,16,256]{3,2,1,0:T(8,128)S(1)} %shard_map.87.deposit_ref, f32[8]{0:T(128)S(1)} %copy-done.4), custom_call_target="tpu_custom_call" | custom-call | flops 31457280 | bytes 4194304 | tf_op jit(solution)/shard_map/pallas_call | solution.py:27
  30.2 0.0 collective-permute-done.2.before_ref
  30.2 1.2 %collective-permute-done.3.after_ref = f32[17,16,256]{2,1,0:T(8,128)S(1)} collective-permute-done((f32[17,16,256]{2,1,0:T(8,128)}, f32[17,16,256]{2,1,0:T(8,128)S(1)}, u32[]{:S(2)}, u32[]{:S(2)}) %collective-permute-start.3) | collective-permute-done | bytes 278560 | tf_op jit(solution)/shard_map/ppermute | solution.py:555
  31.4 0.0 copy-done.1
  31.4 0.0 copy-done.2
  31.4 0.0 copy-done.3
  31.4 3.5 %shard_map.89 = (f32[14,8,16,256]{3,2,1,0:T(8,128)}, f32[8,16384]{1,0:T(8,128)}) custom-call(f32[17,8,16,256]{3,2,1,0:T(8,128)S(1)} %copy-done, f32[14,8,16,256]{3,2,1,0:T(8,128)} %shard_map.88.inner_hbm, f32[17,16,256]{2,1,0:T(8,128)S(1)} %collective-permute-done.2.before_ref, ...), custom_call_target="tpu_custom_call", output_to_operand_aliasing={{0}: (1, {})} | custom-call | flops 1073741824 | bytes 5242880 | tf_op jit(solution)/shard_map/pallas_call | solution.py:27
Async XLA Ops:
  6.6 15.7 %all-to-all-start = ((f32[32,1,1152]{2,1,0:T(1,128)}), f32[32,1,1152]{2,1,0:T(1,128)S(1)}, u32[]{:S(2)}, u32[]{:S(2)}) async-start(f32[32,1,1152]{2,1,0:T(1,128)} %bitcast.5), calls=%async_computation | async-start | bytes 294912 | tf_op jit(solution)/shard_map/all_to_all | solution.py:561
  13.9 16.3 %collective-permute-start.2 = (f32[17,16,256]{2,1,0:T(8,128)}, f32[17,16,256]{2,1,0:T(8,128)S(1)}, u32[]{:S(2)}, u32[]{:S(2)}) collective-permute-start(f32[17,16,256]{2,1,0:T(8,128)} %get-tuple-element.12), channel_id=1, source_target_pairs={{0,4},{4,8},{8,12},{12,16},{16,20},{20,24},{24,28},{28,0},{1,5},{5... | collective-permute-start | bytes 835592 | tf_op jit(solution)/shard_map/ppermute | solution.py:554
  15.7 15.7 %collective-permute-start.3 = (f32[17,16,256]{2,1,0:T(8,128)}, f32[17,16,256]{2,1,0:T(8,128)S(1)}, u32[]{:S(2)}, u32[]{:S(2)}) collective-permute-start(f32[17,16,256]{2,1,0:T(8,128)} %get-tuple-element.13), channel_id=1, source_target_pairs={{4,0},{8,4},{12,8},{16,12},{20,16},{24,20},{28,24},{0,28},{5,1},{9... | collective-permute-start | bytes 835592 | tf_op jit(solution)/shard_map/ppermute | solution.py:555
  18.6 8.6 %collective-permute-start = (f32[15,8,256]{2,1,0:T(8,128)}, f32[15,8,256]{2,1,0:T(8,128)S(1)}, u32[]{:S(2)}, u32[]{:S(2)}) collective-permute-start(f32[15,8,256]{2,1,0:T(8,128)} %get-tuple-element.9), channel_id=1, source_target_pairs={{0,1},{1,2},{2,3},{3,0},{4,5},{5,6},{6,7},{7,4},{8,9},{9,10},{10,1... | collective-permute-start | bytes 368648 | tf_op jit(solution)/shard_map/ppermute | solution.py:556
  18.7 8.6 %collective-permute-start.1 = (f32[15,8,256]{2,1,0:T(8,128)}, f32[15,8,256]{2,1,0:T(8,128)S(1)}, u32[]{:S(2)}, u32[]{:S(2)}) collective-permute-start(f32[15,8,256]{2,1,0:T(8,128)} %get-tuple-element.10), channel_id=1, source_target_pairs={{1,0},{2,1},{3,2},{0,3},{5,4},{6,5},{7,6},{4,7},{9,8},{10,9},{11,1... | collective-permute-start | bytes 368648 | tf_op jit(solution)/shard_map/ppermute | solution.py:557
  22.3 5.0 %copy-start = (f32[17,8,16,256]{3,2,1,0:T(8,128)S(1)}, f32[17,8,16,256]{3,2,1,0:T(8,128)}, u32[]{:S(2)}) copy-start(f32[17,8,16,256]{3,2,1,0:T(8,128)} %cells_ref.3) | copy-start | bytes 6684676
  22.3 5.0 %copy-start.4 = (f32[8]{0:T(128)S(1)}, f32[8]{0:T(128)}, u32[]{:S(2)}) copy-start(f32[8]{0:T(128)} %rate_ref.3) | copy-start | bytes 100
  27.2 4.2 %copy-start.1 = (bf16[256,2048]{1,0:T(8,128)(2,1)S(1)}, bf16[256,2048]{1,0:T(8,128)(2,1)}, u32[]{:S(2)}) copy-start(bf16[256,2048]{1,0:T(8,128)(2,1)} %get-tuple-element.15.hot_ref) | copy-start | bytes 3145732
  27.2 4.2 %copy-start.2 = (f32[8,16384]{1,0:T(8,128)S(1)}, f32[8,16384]{1,0:T(8,128)}, u32[]{:S(2)}) copy-start(f32[8,16384]{1,0:T(8,128)} %get-tuple-element.14.advanced_ref) | copy-start | bytes 1572868
  27.2 4.2 %copy-start.3 = (s32[2,1024]{1,0:T(2,128)S(1)}, s32[2,1024]{1,0:T(2,128)}, u32[]{:S(2)}) copy-start(s32[2,1024]{1,0:T(2,128)} %crossing_ref.1) | copy-start | bytes 24580

commit v12 on v11

--- a/solution.py
+++ b/solution.py
@@ -264,35 +264,41 @@
     )
 
 
-def arrive_into(advanced_ref, hot_ref, crossing_ref, before_ref, after_ref, out_hbm, out_ref, left_ref, sems):
+def arrive_into(advanced_ref, hot_ref, crossing_ref, before_ref, after_ref, out_hbm, out_ref, left_refs, sems):
     cross = crossing_ref.shape[1]
     uppers = advanced_ref.shape[1] // WIDE
     size_y, size_z = before_ref.shape[1:]
     halves_y, halves_z = size_y // 8, size_z // LANES
-    for side, come_ref in ((0, before_ref), (1, after_ref)):
+    step = min(32, uppers)
+    totals = [0.0] * (uppers // step)
+    hit = 0.0
+    for side, (come_ref, left_ref) in enumerate(zip((before_ref, after_ref), left_refs)):
         for first in range(0, cross, LANES):
             layer, rest = divmod(first // LANES, halves_y * halves_z)
             half_y, half_z = divmod(rest, halves_z)
             block = come_ref[COUNT + 1 + layer, 8 * half_y : 8 * half_y + 8, LANES * half_z : LANES * (half_z + 1)]
             coarse, fine = split(block)
             upper = crossing_ref[side : side + 1, first : first + LANES] >> 8
-            at = slice(side * cross + first, side * cross + first + LANES)
+            at = slice(first, first + LANES)
             scatter_left(left_ref, at, upper, uppers, coarse, fine)
-            hit = rows_of(upper.astype(F32), uppers) == packed(iota((uppers, LANES), 0))
-            left_ref[16 * uppers :, at] = jnp.where(hit, 1.0, 0.0).astype(BF16)
-    hit = contract_lanes(left_ref[16 * uppers :], hot_ref[...])
-    step = min(32, uppers)
+            taken = rows_of(upper.astype(F32), uppers) == packed(iota((uppers, LANES), 0))
+            left_ref[16 * uppers :, at] = jnp.where(taken, 1.0, 0.0).astype(BF16)
+        hot = hot_ref[:, side * cross : (side + 1) * cross]
+        hit = hit + contract_lanes(left_ref[16 * uppers :], hot)
+        for number, u in enumerate(range(0, uppers, step)):
+            totals[number] = (
+                totals[number]
+                + contract_lanes(left_ref[8 * u : 8 * (u + step)], hot)
+                + contract_lanes(left_ref[8 * (uppers + u) : 8 * (uppers + u + step)], hot)
+            )
     outs = []
-    for u in range(0, uppers, step):
-        total = contract_lanes(left_ref[8 * u : 8 * (u + step)], hot_ref[...]) + contract_lanes(
-            left_ref[8 * (uppers + u) : 8 * (uppers + u + step)], hot_ref[...]
-        )
+    for number, u in enumerate(range(0, uppers, step)):
         for i in range(step):
             at = slice((u + i) * WIDE, (u + i + 1) * WIDE)
             taken = jnp.broadcast_to(hit[u + i : u + i + 1], (8, WIDE)) > 0.5
-            out_ref[:, at] = jnp.where(taken, total[8 * i : 8 * i + 8], advanced_ref[:, at])
+            out_ref[:, at] = jnp.where(taken, totals[number][8 * i : 8 * i + 8], advanced_ref[:, at])
         at = slice(u * WIDE, (u + step) * WIDE)
-        out = pltpu.make_async_copy(out_ref.at[:, at], out_hbm.at[:, at], sems.at[len(outs)])
+        out = pltpu.make_async_copy(out_ref.at[:, at], out_hbm.at[:, at], sems.at[number])
         out.start()
         outs.append(out)
     return outs
@@ -401,7 +407,7 @@
 
 def last_kernel(
     cells_ref, inner_hbm, before_ref, after_ref, low_ref, high_ref, deposit_ref, rate_ref,
-    advanced_ref, hot_ref, crossing_ref, out_hbm, parcels_hbm, out_ref, parcels_ref, left_ref, sems, parcel_sems,
+    advanced_ref, hot_ref, crossing_ref, out_hbm, parcels_hbm, out_ref, parcels_ref, left_before_ref, left_after_ref, sems, parcel_sems,
 ):
     last = cells_ref.shape[1] - 1
     copies = [
@@ -427,7 +433,8 @@
     layer(lambda c: before_ref[c], 0, 0, lambda c: cells_ref[c, 1])
     layer(lambda c: cells_ref[c, last - 1], 1, last, lambda c: after_ref[c])
     copies += arrive_into(
-        advanced_ref, hot_ref, crossing_ref, before_ref, after_ref, parcels_hbm, parcels_ref, left_ref, parcel_sems
+        advanced_ref, hot_ref, crossing_ref, before_ref, after_ref, parcels_hbm, parcels_ref,
+        (left_before_ref, left_after_ref), parcel_sems,
     )
     for copy in copies:
         copy.wait()
@@ -442,7 +449,8 @@
         [
             pltpu.VMEM((COUNT, 2, size_y, size_z), F32),
             pltpu.VMEM(advanced.shape, F32),
-            pltpu.VMEM((17 * uppers, crossing.size), BF16),
+            pltpu.VMEM((17 * uppers, crossing.shape[1]), BF16),
+            pltpu.VMEM((17 * uppers, crossing.shape[1]), BF16),
             pltpu.SemaphoreType.DMA((2,)),
             pltpu.SemaphoreType.DMA((-(-uppers // 32),)),
         ],

time: 35.2 us -> 35.2 us (level)
  no operation moved by 1% of the time
where the time goes in v12:
time: 35.2 us; the launch traced here: 34.9 us
  Pallas kernels  17.2 us (49%)
  starting transfers between devices  13.8 us (39%)
  waiting for transfers between devices  3.12 us (9%)
  between operations  0.73 us (2%)
    pallas_call x4, Pallas kernels, call(): pl.pallas_call(kernel, out_shape=out_shape, in_specs=in_specs or [ANY] *...  17.2 us
    all_to_all x1, starting transfers between devices, on_device(): lax.all_to_all(filled, ('gx', 'gy'), split_axis=0, concat_axis=0, tiled=T...  7.31 us
    ppermute x1, starting transfers between devices, on_device(): after = lax.ppermute(send_down, 'gx', down_x)  2.95 us
    all_to_all x1, waiting for transfers between devices, on_device(): lax.all_to_all(filled, ('gx', 'gy'), split_axis=0, concat_axis=0, tiled=T...  1.91 us
    ppermute x1, starting transfers between devices, on_device(): before = lax.ppermute(send_up, 'gx', up_x)  1.82 us
    ppermute x1, starting transfers between devices, on_device(): high = lax.ppermute(side_down, 'gy', down_y)  1.74 us
    ppermute x1, waiting for transfers between devices, on_device(): after = lax.ppermute(send_down, 'gx', down_x)  1.2 us
  transfers between devices with their start and end apart: 5, of which 2 were waited for; matrix products, arithmetic and copies ran while one was open for 0% of the time, Pallas kernels for 22%

profile of v12, /device:TPU:0, one launch (start us, length us, event | category | flops | bytes accessed | tf_op | source)
XLA Modules:
  0.0 34.9 jit_solution(6019070727406656039)
XLA Ops:
  0.6 5.9 %shard_map.86 = (f32[17,16,256]{2,1,0:T(8,128)}, f32[17,16,256]{2,1,0:T(8,128)}, f32[15,8,256]{2,1,0:T(8,128)}, f32[15,8,256]{2,1,0:T(8,128)}, f32[8,16384]{1,0:...) custom-call(f32[17,8,16,256]{3,2,1,0:T(8,128)} %cells_ref.3, f32[8,16384]{1,0:T(8,128)} %parcels_hbm.1, ...), custom_call_target="tpu_custom_call" | custom-call | flops 2147483648 | bytes 6291456 | tf_op jit(solution)/shard_map/pallas_call | solution.py:27
  6.6 7.3 %all-to-all-start = ((f32[32,1,1152]{2,1,0:T(1,128)}), f32[32,1,1152]{2,1,0:T(1,128)S(1)}, u32[]{:S(2)}, u32[]{:S(2)}) async-start(f32[32,1,1152]{2,1,0:T(1,128)} %bitcast.5), calls=%async_computation | async-start | bytes 294912 | tf_op jit(solution)/shard_map/all_to_all | solution.py:569
  13.9 1.8 %collective-permute-start.2 = (f32[17,16,256]{2,1,0:T(8,128)}, f32[17,16,256]{2,1,0:T(8,128)S(1)}, u32[]{:S(2)}, u32[]{:S(2)}) collective-permute-start(f32[17,16,256]{2,1,0:T(8,128)} %get-tuple-element.12), channel_id=1, source_target_pairs={{0,4},{4,8},{8,12},{12,16},{16,20},{20,24},{24,28},{28,0},{1,5},{5... | collective-permute-start | bytes 835592 | tf_op jit(solution)/shard_map/ppermute | solution.py:562
  15.7 3.0 %collective-permute-start.3 = (f32[17,16,256]{2,1,0:T(8,128)}, f32[17,16,256]{2,1,0:T(8,128)S(1)}, u32[]{:S(2)}, u32[]{:S(2)}) collective-permute-start(f32[17,16,256]{2,1,0:T(8,128)} %get-tuple-element.13), channel_id=1, source_target_pairs={{4,0},{8,4},{12,8},{16,12},{20,16},{24,20},{28,24},{0,28},{5,1},{9... | collective-permute-start | bytes 835592 | tf_op jit(solution)/shard_map/ppermute | solution.py:563
  18.6 0.0 collective-permute-start
  18.7 1.7 %collective-permute-start.1 = (f32[15,8,256]{2,1,0:T(8,128)}, f32[15,8,256]{2,1,0:T(8,128)S(1)}, u32[]{:S(2)}, u32[]{:S(2)}) collective-permute-start(f32[15,8,256]{2,1,0:T(8,128)} %get-tuple-element.10), channel_id=1, source_target_pairs={{1,0},{2,1},{3,2},{0,3},{5,4},{6,5},{7,6},{4,7},{9,8},{10,9},{11,1... | collective-permute-start | bytes 368648 | tf_op jit(solution)/shard_map/ppermute | solution.py:565
  20.4 1.9 %all-to-all-done = f32[32,1,1152]{2,1,0:T(1,128)S(1)} async-done(((f32[32,1,1152]{2,1,0:T(1,128)}), f32[32,1,1152]{2,1,0:T(1,128)S(1)}, u32[]{:S(2)}, u32[]{:S(2)}) %all-to-all-start) | async-done | bytes 147488 | tf_op jit(solution)/shard_map/all_to_all | solution.py:569
  22.3 0.0 copy-start
  22.3 0.0 copy-start.4
  22.3 4.9 %shard_map.87.deposit_ref = f32[8,8,16,256]{3,2,1,0:T(8,128)S(1)} custom-call(f32[288,128]{1,0:T(8,128)S(1)} %bitcast.4), custom_call_target="tpu_custom_call" | custom-call | flops 1073741824 | bytes 2097152 | tf_op jit(solution)/shard_map/pallas_call | solution.py:27
  27.2 0.0 copy-start.1
  27.2 0.0 copy-start.2
  27.2 0.0 copy-start.3
  27.3 0.0 collective-permute-done.low_ref
  27.3 0.0 collective-permute-done.1.high_ref
  27.3 0.0 copy-done
  27.3 0.0 copy-done.4
  27.3 2.9 %shard_map.88.inner_hbm = f32[14,8,16,256]{3,2,1,0:T(8,128)} custom-call(f32[17,8,16,256]{3,2,1,0:T(8,128)S(1)} %copy-done, f32[15,8,256]{2,1,0:T(8,128)S(1)} %collective-permute-done.low_ref, f32[15,8,256]{2,1,0:T(8,128)S(1)} %collective-permute-done.1.high_ref, f32[8,8,16,256]{3,2,1,0:T(8,128)S(1)} %shard_map.87.deposit_ref, f32[8]{0:T(128)S(1)} %copy-done.4), custom_call_target="tpu_custom_call" | custom-call | flops 31457280 | bytes 4194304 | tf_op jit(solution)/shard_map/pallas_call | solution.py:27
  30.2 0.0 collective-permute-done.2.before_ref
  30.2 1.2 %collective-permute-done.3.after_ref = f32[17,16,256]{2,1,0:T(8,128)S(1)} collective-permute-done((f32[17,16,256]{2,1,0:T(8,128)}, f32[17,16,256]{2,1,0:T(8,128)S(1)}, u32[]{:S(2)}, u32[]{:S(2)}) %collective-permute-start.3) | collective-permute-done | bytes 278560 | tf_op jit(solution)/shard_map/ppermute | solution.py:563
  31.4 0.0 copy-done.1
  31.4 0.0 copy-done.2
  31.4 0.0 copy-done.3
  31.4 3.5 %shard_map.89 = (f32[14,8,16,256]{3,2,1,0:T(8,128)}, f32[8,16384]{1,0:T(8,128)}) custom-call(f32[17,8,16,256]{3,2,1,0:T(8,128)S(1)} %copy-done, f32[14,8,16,256]{3,2,1,0:T(8,128)} %shard_map.88.inner_hbm, f32[17,16,256]{2,1,0:T(8,128)S(1)} %collective-permute-done.2.before_ref, ...), custom_call_target="tpu_custom_call", output_to_operand_aliasing={{0}: (1, {})} | custom-call | flops 1073741824 | bytes 5242880 | tf_op jit(solution)/shard_map/pallas_call | solution.py:27
Async XLA Ops:
  6.6 15.7 %all-to-all-start = ((f32[32,1,1152]{2,1,0:T(1,128)}), f32[32,1,1152]{2,1,0:T(1,128)S(1)}, u32[]{:S(2)}, u32[]{:S(2)}) async-start(f32[32,1,1152]{2,1,0:T(1,128)} %bitcast.5), calls=%async_computation | async-start | bytes 294912 | tf_op jit(solution)/shard_map/all_to_all | solution.py:569
  13.9 16.3 %collective-permute-start.2 = (f32[17,16,256]{2,1,0:T(8,128)}, f32[17,16,256]{2,1,0:T(8,128)S(1)}, u32[]{:S(2)}, u32[]{:S(2)}) collective-permute-start(f32[17,16,256]{2,1,0:T(8,128)} %get-tuple-element.12), channel_id=1, source_target_pairs={{0,4},{4,8},{8,12},{12,16},{16,20},{20,24},{24,28},{28,0},{1,5},{5... | collective-permute-start | bytes 835592 | tf_op jit(solution)/shard_map/ppermute | solution.py:562
  15.7 15.7 %collective-permute-start.3 = (f32[17,16,256]{2,1,0:T(8,128)}, f32[17,16,256]{2,1,0:T(8,128)S(1)}, u32[]{:S(2)}, u32[]{:S(2)}) collective-permute-start(f32[17,16,256]{2,1,0:T(8,128)} %get-tuple-element.13), channel_id=1, source_target_pairs={{4,0},{8,4},{12,8},{16,12},{20,16},{24,20},{28,24},{0,28},{5,1},{9... | collective-permute-start | bytes 835592 | tf_op jit(solution)/shard_map/ppermute | solution.py:563
  18.6 8.6 %collective-permute-start = (f32[15,8,256]{2,1,0:T(8,128)}, f32[15,8,256]{2,1,0:T(8,128)S(1)}, u32[]{:S(2)}, u32[]{:S(2)}) collective-permute-start(f32[15,8,256]{2,1,0:T(8,128)} %get-tuple-element.9), channel_id=1, source_target_pairs={{0,1},{1,2},{2,3},{3,0},{4,5},{5,6},{6,7},{7,4},{8,9},{9,10},{10,1... | collective-permute-start | bytes 368648 | tf_op jit(solution)/shard_map/ppermute | solution.py:564
  18.7 8.6 %collective-permute-start.1 = (f32[15,8,256]{2,1,0:T(8,128)}, f32[15,8,256]{2,1,0:T(8,128)S(1)}, u32[]{:S(2)}, u32[]{:S(2)}) collective-permute-start(f32[15,8,256]{2,1,0:T(8,128)} %get-tuple-element.10), channel_id=1, source_target_pairs={{1,0},{2,1},{3,2},{0,3},{5,4},{6,5},{7,6},{4,7},{9,8},{10,9},{11,1... | collective-permute-start | bytes 368648 | tf_op jit(solution)/shard_map/ppermute | solution.py:565
  22.3 5.0 %copy-start = (f32[17,8,16,256]{3,2,1,0:T(8,128)S(1)}, f32[17,8,16,256]{3,2,1,0:T(8,128)}, u32[]{:S(2)}) copy-start(f32[17,8,16,256]{3,2,1,0:T(8,128)} %cells_ref.3) | copy-start | bytes 6684676
  22.3 5.0 %copy-start.4 = (f32[8]{0:T(128)S(1)}, f32[8]{0:T(128)}, u32[]{:S(2)}) copy-start(f32[8]{0:T(128)} %rate_ref.3) | copy-start | bytes 100
  27.2 4.2 %copy-start.1 = (bf16[256,2048]{1,0:T(8,128)(2,1)S(1)}, bf16[256,2048]{1,0:T(8,128)(2,1)}, u32[]{:S(2)}) copy-start(bf16[256,2048]{1,0:T(8,128)(2,1)} %get-tuple-element.15.hot_ref) | copy-start | bytes 3145732
  27.2 4.2 %copy-start.2 = (f32[8,16384]{1,0:T(8,128)S(1)}, f32[8,16384]{1,0:T(8,128)}, u32[]{:S(2)}) copy-start(f32[8,16384]{1,0:T(8,128)} %get-tuple-element.14.advanced_ref) | copy-start | bytes 1572868
  27.2 4.2 %copy-start.3 = (s32[2,1024]{1,0:T(2,128)S(1)}, s32[2,1024]{1,0:T(2,128)}, u32[]{:S(2)}) copy-start(s32[2,1024]{1,0:T(2,128)} %crossing_ref.1) | copy-start | bytes 24580
